TPU v7x, 256 devices: a whole 4x4x8 slice. The times are simulated.
256 devices in a mesh: dp: 16 (over y, x), ctx: 8 (over z), rank: 2 (over core).
Axes of the slice: x: 4, y: 4, z: 8, core: 2. Of those that a mesh axis runs over, the one named last changes fastest.
Arguments:
- query_rows: bfloat16 [32, 4096, 1024], P(('dp', 'rank'), 'ctx'), may hold values from -6 to 6
- key_rows: bfloat16 [32, 4096, 1024], P(('dp', 'rank'), 'ctx'), may hold values from -6 to 6
- value_rows: bfloat16 [32, 4096, 1024], P(('dp', 'rank'), 'ctx'), may hold values from -6 to 6
- gate_rows: bfloat16 [32, 4096, 1024], P(('dp', 'rank'), 'ctx'), may hold values from -6 to 6
- out_grad: bfloat16 [32, 4096, 1024], P(('dp', 'rank'), 'ctx'), may hold values from -6 to 6
- out_weight: bfloat16 [1024, 1024], P('dp'), may hold values from -0.1875 to 0.1875
- time_bias: bfloat16 [8, 128], replicated, may hold values from -3 to 3
- time_bucket: int32 [32, 4096], P(('dp', 'rank'), 'ctx'), may hold values from 0 to 127
- lengths: int32 [32, 3], P(('dp', 'rank')), may hold values from 1 to 2048, 4096 in all within a row
- band_width: int32 [32, 3], P(('dp', 'rank')), may hold values from 128 to 512, as said below
- user_grad: bfloat16 [96, 1024], P(('dp', 'rank')), may hold values from -6 to 6
- user_owner: int32 [96], replicated, may hold values from 0 to 95, each once
Outputs:
- query_grad: bfloat16 [32, 4096, 1024], P(('dp', 'rank'), 'ctx')
- key_grad: bfloat16 [32, 4096, 1024], P(('dp', 'rank'), 'ctx')
- value_grad: bfloat16 [32, 4096, 1024], P(('dp', 'rank'), 'ctx')
- gate_grad: bfloat16 [32, 4096, 1024], P(('dp', 'rank'), 'ctx')
- weight_grad: float32 [1024, 1024], P('dp')
- bias_grad: float32 [8, 128], P('ctx')
Inputs may be any that keep to these rules, and one draw needn't show every extreme that they name: In every section the longest history has exactly 2048 events and the 3 lengths sum to 4096. `band_width`: in every section some user has a band of exactly 512. A permutation: ranking row r carries the gradient of encoder user user_owner[r], and encoder user g * 3 + s is user s of section g.
All inputs are finite; a program needn't handle non-finite values.
Results may differ from a plain program's by a relative error of at most 0.0059.
Values may be sent and summed in bfloat16 or wider, within the bound.
No kernel may reach another device: no remote copies, remote signals or barrier semaphores. Data moves between devices by JAX's collectives and lax.ppermute only.
A program may use at most 128 MiB of HBM per device.

v0:
```python
import math

import jax
import jax.numpy as jnp
from jax import lax
from jax.sharding import PartitionSpec as P


def owner_of(positions, user_ends):
    counted = jnp.sum((positions[:, None] >= user_ends[None, :]).astype(jnp.int32), axis=1)
    return jnp.where(positions >= 0, counted, -1)


def band_of(owners, user_bands):
    slot_ids = jnp.arange(user_bands.shape[0], dtype=jnp.int32)
    picked = jnp.where(owners[:, None] == slot_ids[None, :], user_bands[None, :], 0)
    return jnp.sum(picked, axis=1)


def window_mask(query_pos, key_pos, user_ends, user_bands):
    query_owner = owner_of(query_pos, user_ends)
    key_owner = owner_of(key_pos, user_ends)
    query_band = band_of(query_owner, user_bands)
    gap_rows = query_pos[:, None] - key_pos[None, :]
    return (
        (query_owner[:, None] == key_owner[None, :])
        & (gap_rows >= 0)
        & (gap_rows < query_band[:, None])
    )


def silu_slope(score_blk):
    sigmoid_val = jax.nn.sigmoid(score_blk)
    return sigmoid_val * (1.0 + score_blk * (1.0 - sigmoid_val))


def bucket_picker(bucket_count):
    slot_ids = jnp.arange(bucket_count, dtype=jnp.int32)
    bucket_gaps = jnp.abs(slot_ids[:, None] - slot_ids[None, :])
    picked = (bucket_gaps[:, :, None] == slot_ids[None, None, :]).astype(jnp.bfloat16)
    return picked.reshape(bucket_count * bucket_count, bucket_count)


def block_context(
    block_start, block_rows, lead_rows, bucket_side, bucket_buf, user_ends, user_bands, bucket_count
):
    window = lead_rows + block_rows
    query_pos = block_start + jnp.arange(block_rows, dtype=jnp.int32)
    key_pos = block_start - lead_rows + jnp.arange(window, dtype=jnp.int32)
    valid_mask = window_mask(query_pos, key_pos, user_ends, user_bands)
    slot_ids = jnp.arange(bucket_count, dtype=jnp.int32)
    query_bucket = lax.dynamic_slice_in_dim(bucket_side, block_start, block_rows)
    key_bucket = lax.dynamic_slice_in_dim(bucket_buf, block_start, window)
    query_hot = (query_bucket[:, None] == slot_ids[None, :]).astype(jnp.bfloat16)
    key_hot = (key_bucket[:, None] == slot_ids[None, :]).astype(jnp.bfloat16)
    return (valid_mask, query_hot, key_hot)


def attend_forward(
    query_side,
    key_buf,
    value_buf,
    bucket_side,
    bucket_buf,
    lead_rows,
    user_ends,
    user_bands,
    table_rows,
    picker,
    head_count,
):
    query_count = query_side.shape[0]
    head_dim = query_side.shape[1] // head_count
    bucket_count = table_rows.shape[1]
    block_rows = min(512, lead_rows)
    window = lead_rows + block_rows
    starts = jnp.arange(query_count // block_rows, dtype=jnp.int32) * block_rows
    score_scale = 1.0 / math.sqrt(head_dim)
    bias_mat = (
        jnp.dot(picker, table_rows[0], preferred_element_type=jnp.float32)
        .reshape(bucket_count, bucket_count)
        .astype(jnp.bfloat16)
    )

    def forward_block(block_start):
        valid_mask, query_hot, key_hot = block_context(
            block_start,
            block_rows,
            lead_rows,
            bucket_side,
            bucket_buf,
            user_ends,
            user_bands,
            bucket_count,
        )
        query_blk = lax.dynamic_slice_in_dim(query_side, block_start, block_rows)
        key_win = lax.dynamic_slice_in_dim(key_buf, block_start, window)
        value_win = lax.dynamic_slice_in_dim(value_buf, block_start, window)
        bias_rows = jnp.dot(query_hot, bias_mat, preferred_element_type=jnp.float32).astype(
            jnp.bfloat16
        )
        bias_blk = jnp.dot(bias_rows, key_hot.T, preferred_element_type=jnp.float32)
        score_blk = (
            jnp.dot(query_blk, key_win.T, preferred_element_type=jnp.float32) * score_scale
            + bias_blk
        )
        attn_blk = jnp.where(valid_mask, jax.nn.silu(score_blk), 0.0).astype(jnp.bfloat16)
        return (jnp.dot(attn_blk, value_win, preferred_element_type=jnp.float32), score_blk)

    out_blk, score_all = lax.map(forward_block, starts)
    outputs = out_blk.reshape(query_count, head_dim).astype(jnp.bfloat16)
    saved = [score_all]
    return (outputs, saved)


def attend_backward(
    query_side,
    key_buf,
    value_buf,
    grad_side,
    bucket_side,
    bucket_buf,
    lead_rows,
    user_ends,
    user_bands,
    saved,
    picker,
    head_count,
    bucket_count,
):
    query_count = query_side.shape[0]
    buf_rows = key_buf.shape[0]
    head_dim = query_side.shape[1] // head_count
    block_rows = min(512, lead_rows)
    window = lead_rows + block_rows
    starts = jnp.arange(query_count // block_rows, dtype=jnp.int32) * block_rows
    picker_f = picker.astype(jnp.float32)
    query_parts, key_parts, value_parts, bias_parts = ([], [], [], [])

    def backward_block(carried, inputs):
        key_acc, value_acc, bias_acc = carried
        block_start, score_blk = inputs
        valid_mask, query_hot, key_hot = block_context(
            block_start,
            block_rows,
            lead_rows,
            bucket_side,
            bucket_buf,
            user_ends,
            user_bands,
            bucket_count,
        )
        query_blk = lax.dynamic_slice_in_dim(query_side, block_start, block_rows)
        key_win = lax.dynamic_slice_in_dim(key_buf, block_start, window)
        value_win = lax.dynamic_slice_in_dim(value_buf, block_start, window)
        grad_blk = lax.dynamic_slice_in_dim(grad_side, block_start, block_rows)
        attn_blk = jnp.where(valid_mask, jax.nn.silu(score_blk), 0.0).astype(jnp.bfloat16)
        value_part = jnp.dot(attn_blk.T, grad_blk, preferred_element_type=jnp.float32)
        attn_grad = jnp.dot(grad_blk, value_win.T, preferred_element_type=jnp.float32)
        score_grad = jnp.where(valid_mask, attn_grad * silu_slope(score_blk), 0.0).astype(
            jnp.bfloat16
        )
        query_part = jnp.dot(score_grad, key_win, preferred_element_type=jnp.float32)
        key_part = jnp.dot(score_grad.T, query_blk, preferred_element_type=jnp.float32)
        bucket_mid = jnp.dot(score_grad, key_hot, preferred_element_type=jnp.float32)
        bias_acc = bias_acc + jnp.dot(
            query_hot.astype(jnp.float32).T, bucket_mid, precision=lax.Precision.HIGHEST
        )
        key_acc = lax.dynamic_update_slice_in_dim(
            key_acc,
            lax.dynamic_slice_in_dim(key_acc, block_start, window) + key_part,
            block_start,
            0,
        )
        value_acc = lax.dynamic_update_slice_in_dim(
            value_acc,
            lax.dynamic_slice_in_dim(value_acc, block_start, window) + value_part,
            block_start,
            0,
        )
        return ((key_acc, value_acc, bias_acc), query_part)

    start_state = (
        jnp.zeros((buf_rows, head_dim), jnp.float32),
        jnp.zeros((buf_rows, head_dim), jnp.float32),
        jnp.zeros((bucket_count, bucket_count), jnp.float32),
    )
    (key_acc, value_acc, bias_acc), query_blocks = lax.scan(
        backward_block, start_state, (starts, saved[0])
    )
    query_parts.append(query_blocks.reshape(query_count, head_dim))
    key_parts.append(key_acc)
    value_parts.append(value_acc)
    bias_parts.append(
        jnp.dot(
            bias_acc.reshape(1, bucket_count * bucket_count),
            picker_f,
            precision=lax.Precision.HIGHEST,
        )[0]
    )
    return (query_parts[0], key_parts[0], value_parts[0], jnp.stack(bias_parts, axis=0))


def on_device(
    query_rows,
    key_rows,
    value_rows,
    gate_rows,
    out_grad,
    out_weight,
    time_bias,
    time_bucket,
    lengths,
    band_width,
    user_grad,
    user_owner,
):
    queries = query_rows[0]
    keys_own = key_rows[0]
    values_own = value_rows[0]
    gate_vals = gate_rows[0]
    cotangent = out_grad[0]
    buckets = time_bucket[0]
    hist_lengths = lengths[0]
    user_bands = band_width[0]
    tok_dev = queries.shape[0]
    model_width = queries.shape[1]
    n_ctx = lax.axis_size("ctx")
    ctx_index = lax.axis_index("ctx")
    section = lax.axis_index("dp") * lax.axis_size("rank") + lax.axis_index("rank")
    user_count = hist_lengths.shape[0]
    heads_all = time_bias.shape[0]
    bucket_count = time_bias.shape[1]
    head_dim = model_width // heads_all
    score_scale = 1.0 / math.sqrt(head_dim)
    user_ends = jnp.cumsum(hist_lengths)
    own_pos = ctx_index * tok_dev + jnp.arange(tok_dev, dtype=jnp.int32)
    picker = bucket_picker(bucket_count)
    gathered = lax.all_gather(user_grad, ("dp", "rank"), axis=0, tiled=True)
    wanted = section * user_count + jnp.arange(user_count, dtype=jnp.int32)
    selector = (user_owner[None, :] == wanted[:, None]).astype(jnp.bfloat16)
    user_rows = jnp.dot(selector, gathered, preferred_element_type=jnp.float32).astype(jnp.bfloat16)
    last_hits = (own_pos[:, None] == user_ends[None, :] - 1).astype(jnp.bfloat16)
    total_grad = (
        cotangent.astype(jnp.float32)
        + jnp.dot(last_hits, user_rows, preferred_element_type=jnp.float32)
    ).astype(jnp.bfloat16)
    head_count = heads_all // n_ctx
    query_side, head_keys, head_values = (
        lax.all_to_all(queries, "ctx", split_axis=1, concat_axis=0, tiled=True),
        lax.all_to_all(keys_own, "ctx", split_axis=1, concat_axis=0, tiled=True),
        lax.all_to_all(values_own, "ctx", split_axis=1, concat_axis=0, tiled=True),
    )
    bucket_side = lax.all_gather(buckets, "ctx", axis=0, tiled=True)
    pad_rows = jnp.zeros((tok_dev, head_keys.shape[1]), jnp.bfloat16)
    key_buf = jnp.concatenate([pad_rows, head_keys], axis=0)
    value_buf = jnp.concatenate([pad_rows, head_values], axis=0)
    bucket_buf = jnp.concatenate([jnp.zeros((tok_dev,), jnp.int32), bucket_side])
    table_rows = lax.dynamic_slice_in_dim(time_bias, ctx_index * head_count, head_count, 0)
    head_mixed, saved = attend_forward(
        query_side,
        key_buf,
        value_buf,
        bucket_side,
        bucket_buf,
        tok_dev,
        user_ends,
        user_bands,
        table_rows,
        picker,
        head_count,
    )
    mixed_rows = lax.all_to_all(head_mixed, "ctx", split_axis=0, concat_axis=1, tiled=True)
    lifted = jnp.dot(
        total_grad,
        lax.all_gather(out_weight, "dp", axis=0, tiled=True).T,
        preferred_element_type=jnp.float32,
    )
    mixed_f = mixed_rows.astype(jnp.float32)
    center = jnp.mean(mixed_f, axis=1, keepdims=True)
    deviation = mixed_f - center
    variance = jnp.mean(deviation * deviation, axis=1, keepdims=True)
    inv_std = lax.rsqrt(variance + 1e-05)
    normed = deviation * inv_std
    gate_f = gate_vals.astype(jnp.float32)
    gate_grad = (lifted * normed).astype(jnp.bfloat16)
    gated_rows = (normed * gate_f).astype(jnp.bfloat16)
    normed_grad = lifted * gate_f
    mixed_grad = (
        inv_std
        * (
            normed_grad
            - jnp.mean(normed_grad, axis=1, keepdims=True)
            - normed * jnp.mean(normed_grad * normed, axis=1, keepdims=True)
        )
    ).astype(jnp.bfloat16)
    weight_part = lax.psum_scatter(
        jnp.dot(gated_rows.T, total_grad, preferred_element_type=jnp.float32),
        "dp",
        scatter_dimension=0,
        tiled=True,
    )
    weight_grad = lax.psum(weight_part, ("ctx", "rank"))
    grad_side = lax.all_to_all(mixed_grad, "ctx", split_axis=1, concat_axis=0, tiled=True)
    query_raw, key_acc, value_acc, bias_part = attend_backward(
        query_side,
        key_buf,
        value_buf,
        grad_side,
        bucket_side,
        bucket_buf,
        tok_dev,
        user_ends,
        user_bands,
        saved,
        picker,
        head_count,
        bucket_count,
    )
    query_heads = (query_raw * score_scale).astype(jnp.bfloat16)
    key_heads = (key_acc[tok_dev:] * score_scale).astype(jnp.bfloat16)
    value_heads = value_acc[tok_dev:].astype(jnp.bfloat16)
    query_grad, key_grad, value_grad = (
        lax.all_to_all(query_heads, "ctx", split_axis=0, concat_axis=1, tiled=True),
        lax.all_to_all(key_heads, "ctx", split_axis=0, concat_axis=1, tiled=True),
        lax.all_to_all(value_heads, "ctx", split_axis=0, concat_axis=1, tiled=True),
    )
    bias_grad = lax.psum(bias_part, ("dp", "rank"))
    return (
        query_grad[None],
        key_grad[None],
        value_grad[None],
        gate_grad[None],
        weight_grad,
        bias_grad,
    )


def solution(mesh):
    return jax.shard_map(
        on_device,
        mesh=mesh,
        in_specs=(
            P(("dp", "rank"), "ctx", None),
            P(("dp", "rank"), "ctx", None),
            P(("dp", "rank"), "ctx", None),
            P(("dp", "rank"), "ctx", None),
            P(("dp", "rank"), "ctx", None),
            P("dp", None),
            P(),
            P(("dp", "rank"), "ctx"),
            P(("dp", "rank"), None),
            P(("dp", "rank"), None),
            P(("dp", "rank"), None),
            P(),
        ),
        out_specs=(
            P(("dp", "rank"), "ctx", None),
            P(("dp", "rank"), "ctx", None),
            P(("dp", "rank"), "ctx", None),
            P(("dp", "rank"), "ctx", None),
            P("dp", None),
            P("ctx", None),
        ),
        check_vma=False,
    )
```

profile of v0, /device:TPU:1, one launch (start us, length us, event | category | flops | bytes accessed | tf_op | source)
XLA Modules:
  0.0 724.3 jit_solution(559486347023391537)
XLA Ops:
  9.8 9.0 %all-to-all-start.2 = ((bf16[512,8,128]{2,0,1:T(8,128)(2,1)}), bf16[512,8,128]{2,0,1:T(8,128)(2,1)S(1)}, u32[]{:S(2)}, u32[]{:S(2)}) async-start(bf16[512,8,128]{2,0,1:T(8,128)(2,1)} %copy.52), calls=%async_computation.2 | async-start | bytes 2097152 | tf_op jit(solution)/shard_map/all_to_all | solution.py:252
  20.3 27.8 %all-to-all-done.2 = bf16[512,8,128]{2,0,1:T(8,128)(2,1)S(1)} async-done(((bf16[512,8,128]{2,0,1:T(8,128)(2,1)}), bf16[512,8,128]{2,0,1:T(8,128)(2,1)S(1)}, u32[]{:S(2)}, u32[]{:S(2)}) %all-to-all-start.2) | async-done | bytes 1048608 | tf_op jit(solution)/shard_map/all_to_all | solution.py:252
  48.0 3.6 all-to-all-start.1
  53.0 27.7 %all-to-all-done.1 = bf16[512,8,128]{2,0,1:T(8,128)(2,1)S(1)} async-done(((bf16[512,8,128]{2,0,1:T(8,128)(2,1)}), bf16[512,8,128]{2,0,1:T(8,128)(2,1)S(1)}, u32[]{:S(2)}, u32[]{:S(2)}) %all-to-all-start.1) | async-done | bytes 1048608 | tf_op jit(solution)/shard_map/all_to_all | solution.py:251
  80.8 4.2 all-to-all-start
  85.8 3.7 fusion.51
  89.5 34.2 %all-gather = s32[1,4096]{1,0:T(1,128)} all-gather(s32[1,512]{1,0:T(1,128)S(1)} %copy-done.12), channel_id=2, replica_groups=mesh['dp'=16,'ctx'=8,'rank'=2] {'ctx'}, dimensions={1}, use_global_device_ids=true | all-gather | bytes 18432 | tf_op jit(solution)/shard_map/all_gather | solution.py:254
  128.2 124.2 %while.35 = (s32[]{:T(128)}, bf16[8,512,128]{2,1,0:T(8,128)(2,1)}, f32[8,512,1024]{2,1,0:T(8,128)}, s32[8]{0:T(128)}, s32[3]{0:T(128)S(1)}, /*index=5*/s32[1,3]{...) while((s32[]{:T(128)}, bf16[8,512,128]{2,1,0:T(8,128)(2,1)}, ...), condition=%wide.region_5.6_spmd.clone, body=%wide.region_1.5_spmd.sunk.clone | while | flops 427055104 | bytes 11504912 | solution.py:110
  140.4 3.3 fusion.134
  156.0 3.3 fusion.134
  171.5 3.3 fusion.134
  187.0 3.3 fusion.134
  197.7 2.7 bitcast_dynamic-update-slice_fusion.3
  202.7 3.3 fusion.134
  218.1 3.3 fusion.134
  233.6 3.3 fusion.134
  249.1 3.3 fusion.134
  252.4 3.8 all-to-all-start.3
  256.2 31.6 %all-gather.1 = bf16[32,3,1024]{2,1,0:T(4,128)(2,1)S(1)} all-gather(bf16[1,3,1024]{2,1,0:T(4,128)(2,1)S(1)} %bitcast.207), channel_id=1, replica_groups=mesh['dp'=16,'ctx'=8,'rank'=2] {'dp','rank'}, dimensions={0}, use_global_device_ids=true | all-gather | bytes 202752 | tf_op jit(solution)/shard_map/all_gather | solution.py:239
  292.4 3.5 fusion.66
  298.9 6.9 all-to-all-start.4
  306.0 4.9 fusion.63
  311.0 24.2 %all-to-all-done.4 = bf16[512,8,128]{2,0,1:T(8,128)(2,1)} async-done(((bf16[512,8,128]{2,0,1:T(8,128)(2,1)}), bf16[512,8,128]{2,0,1:T(8,128)(2,1)}, u32[]{:S(2)}, u32[]{:S(2)}) %all-to-all-start.4) | async-done | bytes 1048608 | tf_op jit(solution)/shard_map/all_to_all | solution.py:304
  338.4 190.6 %while.36 = (s32[]{:T(128)}, f32[4608,128]{1,0:T(8,128)}, f32[4608,128]{1,0:T(8,128)}, f32[128,128]{1,0:T(8,128)S(1)}, f32[8,512,128]{2,1,0:T(8,128)}, /*index=5...) while((s32[]{:T(128)}, f32[4608,128]{1,0:T(8,128)}, ...), condition=%wide.region_14.15_spmd.clone.clone, body=%wide.region_10.14_spmd.clone.sunk.clone | while | flops 786946048 | bytes 14501706 | solution.py:188
  345.1 3.1 fusion.145
  349.8 3.0 dynamic_update_slice.51
  354.0 2.9 convolution_add_fusion.10
  356.8 3.0 dynamic_update_slice.52
  369.3 3.0 fusion.145
  373.9 3.0 dynamic_update_slice.51
  378.1 3.0 convolution_add_fusion.10
  381.1 3.0 dynamic_update_slice.52
  393.5 3.1 fusion.145
  398.1 3.0 dynamic_update_slice.51
  402.3 2.9 convolution_add_fusion.10
  405.1 3.0 dynamic_update_slice.52
  417.5 3.0 fusion.145
  422.2 3.0 dynamic_update_slice.51
  426.3 2.9 convolution_add_fusion.10
  429.2 3.0 dynamic_update_slice.52
  441.6 3.1 fusion.145
  446.2 3.0 dynamic_update_slice.51
  450.4 2.9 convolution_add_fusion.10
  453.3 3.0 dynamic_update_slice.52
  465.7 3.0 fusion.145
  470.4 3.0 dynamic_update_slice.51
  474.5 2.9 convolution_add_fusion.10
  477.4 3.0 dynamic_update_slice.52
  489.8 3.1 fusion.145
  494.5 3.0 dynamic_update_slice.51
  498.6 2.9 convolution_add_fusion.10
  501.5 3.0 dynamic_update_slice.52
  513.8 3.0 fusion.145
  521.5 2.9 convolution_add_fusion.10
  529.6 2.9 multiply_convert_fusion.2
  532.5 3.6 all-to-all-start.5
  537.2 28.1 %all-to-all-done.5 = bf16[8,512,128]{2,1,0:T(8,128)(2,1)S(1)} async-done(((bf16[8,512,128]{2,1,0:T(8,128)(2,1)}), bf16[8,512,128]{2,1,0:T(8,128)(2,1)S(1)}, u32[]{:S(2)}, u32[]{:S(2)}) %all-to-all-start.5) | async-done | bytes 1048608 | tf_op jit(solution)/shard_map/all_to_all | solution.py:324
  565.3 3.6 all-to-all-start.6
  568.9 2.7 slice.12
  571.6 26.4 %all-to-all-done.6 = bf16[8,512,128]{2,1,0:T(8,128)(2,1)S(1)} async-done(((bf16[8,512,128]{2,1,0:T(8,128)(2,1)}), bf16[8,512,128]{2,1,0:T(8,128)(2,1)S(1)}, u32[]{:S(2)}, u32[]{:S(2)}) %all-to-all-start.6) | async-done | bytes 1048608 | tf_op jit(solution)/shard_map/all_to_all | solution.py:325
  598.0 3.6 all-to-all-start.7
  602.3 3.4 fusion.53
  605.7 63.3 %psum.15 = f32[1,128]{1,0:T(1,128)} all-reduce(f32[1,128]{1,0:T(1,128)S(1)} %fusion.53), channel_id=1, replica_groups=mesh['dp'=16,'ctx'=8,'rank'=2] {'dp','rank'}, use_global_device_ids=true, to_apply=%region_17.18 | all-reduce | flops 128 | bytes 1024 | tf_op jit(solution)/shard_map/psum | solution.py:328
  676.7 39.4 %all-reduce.5.cloned.1.call-done = f32[64,1024]{1,0:T(8,128)} async-done(((f32[64,1024]{1,0:T(8,128)}), f32[64,1024]{1,0:T(8,128)}) %all-reduce.5.cloned.1.call-update) | async-done | bytes 262160 | tf_op jit(solution)/shard_map/psum | solution.py:303
  (288 shorter events, 166.8 us)
Async XLA Ops:
  7.2 78.6 %copy-start = (bf16[8,128]{1,0:T(8,128)(2,1)S(1)}, bf16[8,128]{1,0:T(8,128)(2,1)}, u32[]{:S(2)}) copy-start(bf16[8,128]{1,0:T(8,128)(2,1)} %param.22) | copy-start | bytes 6148
  8.7 10.2 %copy-start.5 = (bf16[1,512,1024]{2,1,0:T(8,128)(2,1)S(1)}, bf16[1,512,1024]{2,1,0:T(8,128)(2,1)}, u32[]{:S(2)}) copy-start(bf16[1,512,1024]{2,1,0:T(8,128)(2,1)} %param.17) | copy-start | bytes 3145732
  9.8 38.2 %all-to-all-start.2 = ((bf16[512,8,128]{2,0,1:T(8,128)(2,1)}), bf16[512,8,128]{2,0,1:T(8,128)(2,1)S(1)}, u32[]{:S(2)}, u32[]{:S(2)}) async-start(bf16[512,8,128]{2,0,1:T(8,128)(2,1)} %copy.52), calls=%async_computation.2 | async-start | bytes 2097152 | tf_op jit(solution)/shard_map/all_to_all | solution.py:252
  19.1 32.5 %copy-start.6 = (bf16[1,512,1024]{2,1,0:T(8,128)(2,1)S(1)}, bf16[1,512,1024]{2,1,0:T(8,128)(2,1)}, u32[]{:S(2)}) copy-start(bf16[1,512,1024]{2,1,0:T(8,128)(2,1)} %param.16) | copy-start | bytes 3145732
  48.0 32.7 %all-to-all-start.1 = ((bf16[512,8,128]{2,0,1:T(8,128)(2,1)}), bf16[512,8,128]{2,0,1:T(8,128)(2,1)S(1)}, u32[]{:S(2)}, u32[]{:S(2)}) async-start(bf16[512,8,128]{2,0,1:T(8,128)(2,1)} %copy.51), calls=%async_computation.1 | async-start | bytes 2097152 | tf_op jit(solution)/shard_map/all_to_all | solution.py:251
  53.0 36.5 %copy-start.12 = (s32[1,512]{1,0:T(1,128)S(1)}, s32[1,512]{1,0:T(1,128)}, u32[]{:S(2)}) copy-start(s32[1,512]{1,0:T(1,128)} %param.23) | copy-start | bytes 6148
  53.0 72.0 %copy-start.13 = (s32[1,3]{1,0:T(1,128)S(1)}, s32[1,3]{1,0:T(1,128)}, u32[]{:S(2)}) copy-start(s32[1,3]{1,0:T(1,128)} %param.24) | copy-start | bytes 40
  80.8 47.4 %all-to-all-start = ((bf16[512,8,128]{2,0,1:T(8,128)(2,1)}), bf16[512,8,128]{2,0,1:T(8,128)(2,1)}, u32[]{:S(2)}, u32[]{:S(2)}) async-start(bf16[512,8,128]{2,0,1:T(8,128)(2,1)} %copy.50), calls=%async_computation | async-start | bytes 2097152 | tf_op jit(solution)/shard_map/all_to_all | solution.py:250
  85.0 206.8 %all-gather.4.cloned.1.call-start = ((), (), s32[]{:S(2)}) async-start(), calls=%async_computation.9 | async-start | bytes 2228224 | tf_op jit(solution)/shard_map/all_gather | solution.py:276
  126.9 1.2 copy-start.10
  252.4 3.8 copy-start.11
  252.4 36.2 %copy-start.7 = (bf16[1,512,1024]{2,1,0:T(8,128)(2,1)S(1)}, bf16[1,512,1024]{2,1,0:T(8,128)(2,1)}, u32[]{:S(2)}) copy-start(bf16[1,512,1024]{2,1,0:T(8,128)(2,1)} %param.20) | copy-start | bytes 3145732
  252.4 38.8 %all-to-all-start.3 = ((bf16[8,512,128]{2,1,0:T(8,128)(2,1)}), bf16[8,512,128]{2,1,0:T(8,128)(2,1)S(1)}, u32[]{:S(2)}, u32[]{:S(2)}) async-start(bf16[8,512,128]{2,1,0:T(8,128)(2,1)} %get-tuple-element.344), calls=%async_computation.3 | async-start | bytes 2097152 | tf_op jit(solution)/shard_map/all_to_all | solution.py:273
  291.1 1.2 copy-start.8
  292.4 3.6 copy-start.9
  298.9 36.2 %all-to-all-start.4 = ((bf16[512,8,128]{2,0,1:T(8,128)(2,1)}), bf16[512,8,128]{2,0,1:T(8,128)(2,1)}, u32[]{:S(2)}, u32[]{:S(2)}) async-start(bf16[512,8,128]{2,0,1:T(8,128)(2,1)} %bitcast.146), calls=%async_computation.4 | async-start | bytes 2097152 | tf_op jit(solution)/shard_map/all_to_all | solution.py:304
  305.8 295.9 %reduce-scatter.2.cloned.1.call-start = ((), (), s32[]{:S(2)}) async-start(), calls=%async_computation.10 | async-start | bytes 4456448 | tf_op jit(solution)/shard_map/reduce_scatter | solution.py:297
  528.9 0.6 copy-start.3
  529.6 6.5 copy-start.2
  532.5 32.8 %all-to-all-start.5 = ((bf16[8,512,128]{2,1,0:T(8,128)(2,1)}), bf16[8,512,128]{2,1,0:T(8,128)(2,1)S(1)}, u32[]{:S(2)}, u32[]{:S(2)}) async-start(bf16[8,512,128]{2,1,0:T(8,128)(2,1)} %multiply_convert_fusion.2), calls=%async_computation.5 | async-start | bytes 2097152 | tf_op jit(solution)/shard_map/all_to_all | solution.py:324
  565.3 32.7 %all-to-all-start.6 = ((bf16[8,512,128]{2,1,0:T(8,128)(2,1)}), bf16[8,512,128]{2,1,0:T(8,128)(2,1)S(1)}, u32[]{:S(2)}, u32[]{:S(2)}) async-start(bf16[8,512,128]{2,1,0:T(8,128)(2,1)} %bitcast.25), calls=%async_computation.6 | async-start | bytes 2097152 | tf_op jit(solution)/shard_map/all_to_all | solution.py:325
  568.8 33.5 %copy-start.4 = (f32[128,128]{1,0:T(8,128)S(1)}, f32[128,128]{1,0:T(8,128)}, u32[]{:S(2)}) copy-start(f32[128,128]{1,0:T(8,128)} %copy-done.3) | copy-start | bytes 196612
  598.0 76.8 %all-to-all-start.7 = ((bf16[8,512,128]{2,1,0:T(8,128)(2,1)}), bf16[8,512,128]{2,1,0:T(8,128)(2,1)S(1)}, u32[]{:S(2)}, u32[]{:S(2)}) async-start(bf16[8,512,128]{2,1,0:T(8,128)(2,1)} %bitcast.28), calls=%async_computation.7 | async-start | bytes 2097152 | tf_op jit(solution)/shard_map/all_to_all | solution.py:326
  601.6 114.5 %all-reduce.5.cloned.1.call-start = ((), (), s32[]{:S(2)}) async-start(), calls=%async_computation.11 | async-start | bytes 524288 | tf_op jit(solution)/shard_map/psum | solution.py:303
  673.5 44.3 %copy-start.1 = (bf16[8,128]{1,0:T(8,128)(2,1)S(1)}, bf16[8,128]{1,0:T(8,128)(2,1)}, u32[]{:S(2)}) copy-start(bf16[8,128]{1,0:T(8,128)(2,1)} %param.22) | copy-start | bytes 6148
Sparse Core Ops, SparseCore 0:
  88.3 50.5 all-gather.3
  311.1 80.0 reduce-scatter.1
  604.8 111.2 all-reduce.4
where the time goes:
time: 730 us; the launch traced here: 724 us
  waiting for transfers between devices  175 us (24%)
  matrix products  154 us (21%)
  blocking collectives  129 us (18%)
  local copies, waits for them, and re-layouts  117 us (16%)
  loops' own time  63.2 us (9%)
  starting transfers between devices  38.5 us (5%)
  other arithmetic  33.5 us (5%)
  between operations  14.1 us (2%)
    psum x1, blocking collectives, on_device(): bias_grad = lax.psum(bias_part, ('dp', 'rank'))  63.3 us
    psum x1, waiting for transfers between devices, on_device(): weight_grad = lax.psum(weight_part, ('ctx', 'rank'))  39.4 us
    all_gather x1, blocking collectives, on_device(): bucket_side = lax.all_gather(buckets, 'ctx', axis=0, tiled=True)  34.2 us
    another operation x1, loops' own time, attend_backward(): lax.scan(backward_block, start_state, (starts, saved[0]))  31.8 us
    all_gather x1, blocking collectives, on_device(): gathered = lax.all_gather(user_grad, ('dp', 'rank'), axis=0, tiled=True)  31.6 us
    another operation x1, loops' own time, attend_forward(): out_blk, score_all = lax.map(forward_block, starts)  31.5 us
    all_to_all x1, waiting for transfers between devices, on_device(): lax.all_to_all(query_heads, 'ctx', split_axis=0, concat_axis=1, tiled=True)  28.1 us
    all_to_all x1, waiting for transfers between devices, on_device(): lax.all_to_all(values_own, 'ctx', split_axis=1, concat_axis=0, tiled=True)  27.8 us
  transfers between devices with their start and end apart: 11, of which 6 were waited for; matrix products, arithmetic and copies ran while one was open for 40% of the time, Pallas kernels for 0%

commit v1 on v0

v1 whole, which is shorter than its diff:
```python
import functools
import math

import jax
import jax.numpy as jnp
from jax import lax
from jax.experimental import pallas as pl
from jax.experimental.pallas import tpu as pltpu
from jax.sharding import PartitionSpec as P

F32 = jnp.float32
BF16 = jnp.bfloat16
HEADS = 8
DIM = 128
TOK = 512
HALF = 256
WIDTH = 1024
PAD = 16
MASKED = -1e9
SCALE = 1.0 / math.sqrt(DIM)
VMEM_LIMIT = 48 * 1024 * 1024


def dot_nt(a, b):
    return lax.dot_general(a, b, (((1,), (1,)), ((), ())), preferred_element_type=F32)


def dot_nn(a, b):
    return lax.dot_general(a, b, (((1,), (0,)), ((), ())), preferred_element_type=F32)


def dot_tn(a, b):
    return lax.dot_general(a, b, (((0,), (0,)), ((), ())), preferred_element_type=F32)


def lowest_key(meta, first, rows):
    pos = first + lax.broadcasted_iota(jnp.int32, (rows, 1), 0)
    e0, e1, e2 = meta[0], meta[1], meta[2]
    start = jnp.where(pos >= e0, e0, 0)
    band = jnp.where(pos >= e0, meta[4], meta[3])
    start = jnp.where(pos >= e1, e1, start)
    band = jnp.where(pos >= e1, meta[5], band)
    start = jnp.where(pos >= e2, e2, start)
    band = jnp.where(pos >= e2, 0, band)
    return pos, jnp.maximum(start, pos - band + 1)


def mask_tile(meta, q_first, rows, k_first, cols, causal):
    pos, low = lowest_key(meta, q_first, rows)
    key = k_first + lax.broadcasted_iota(jnp.int32, (rows, cols), 1)
    ok = key >= low
    if causal:
        ok = ok & (key <= pos)
    return jnp.where(ok, 0.0, MASKED)


def bucket_cols(row):
    count = row.shape[1]
    return jnp.transpose(jnp.broadcast_to(row.astype(F32), (DIM, count))).astype(jnp.int32)


def lanes(rows):
    return lax.broadcasted_iota(jnp.int32, (rows, DIM), 1)


def one_hot(row):
    cols = bucket_cols(row)
    return jnp.where(cols == lanes(cols.shape[0]), 1.0, 0.0).astype(BF16)


def bias_rows(table_row, cols):
    gap = jnp.abs(cols - lanes(cols.shape[0]))
    spread = jnp.broadcast_to(table_row, gap.shape)
    return jnp.take_along_axis(spread, gap, axis=1).astype(BF16)


def bias_sum(mid, cols):
    lane = lanes(cols.shape[0])
    up, down = cols + lane, cols - lane
    above = jnp.take_along_axis(mid, up & (DIM - 1), axis=1)
    below = jnp.take_along_axis(mid, down & (DIM - 1), axis=1)
    both = jnp.where(up < DIM, above, 0.0) + jnp.where((down >= 0) & (lane > 0), below, 0.0)
    return jnp.sum(both, axis=0, keepdims=True) * 0.5


def attn_of(q_aug, k_aug, mask):
    half_score = dot_nt(q_aug, k_aug) * (0.5 * SCALE) + mask
    t = jnp.tanh(half_score)
    u = 1.0 + t
    return half_score * u, t, u


def back_of(q_aug, k_aug, mask, grad, value):
    attn, t, u = attn_of(q_aug, k_aug, mask)
    slope2 = u + attn * (1.0 - t)
    score_grad2 = (dot_nt(grad, value) * slope2).astype(BF16)
    return attn.astype(BF16), score_grad2


def cat(*parts):
    return jnp.concatenate(parts, axis=1)


def own_forward_body(meta, q, k, v, bkt, tab, out, mask, hot, cols):
    h = pl.program_id(0)

    @pl.when(h == 0)
    def _():
        mask[...] = mask_tile(meta, meta[6], TOK, meta[6], TOK, True)
        hot[...] = one_hot(bkt[...])
        cols[...] = bucket_cols(bkt[...])

    q_aug = cat(q[...], bias_rows(tab[pl.ds(h, 1), :], cols[...]))
    k_aug = cat(k[...], hot[...])
    for i in range(2):
        lo, hi = i * HALF, (i + 1) * HALF
        attn, _, _ = attn_of(q_aug[lo:hi], k_aug[:hi], mask[lo:hi, :hi])
        out[lo:hi, :] = dot_nn(attn.astype(BF16), v[:hi, :])


def sent_forward_body(meta, q, q_bkt, k, v, bkt, tab, out, mask, hot, cols):
    h = pl.program_id(0)

    @pl.when(h == 0)
    def _():
        mask[...] = mask_tile(meta, meta[6] + TOK, HALF, meta[6], TOK, False)
        hot[...] = one_hot(bkt[...])
        cols[...] = bucket_cols(q_bkt[0:1, :HALF])

    q_aug = cat(q[...], bias_rows(tab[pl.ds(h, 1), :], cols[...]))
    k_aug = cat(k[...], hot[...])
    attn, _, _ = attn_of(q_aug, k_aug, mask[...])
    out[...] = dot_nn(attn.astype(BF16), v[...]).astype(BF16)


def norm_rows(mixed, lifted, gate):
    mixed = mixed.astype(BF16).astype(F32)
    center = jnp.mean(mixed, axis=1, keepdims=True)
    deviation = mixed - center
    variance = jnp.mean(deviation * deviation, axis=1, keepdims=True)
    inv_std = lax.rsqrt(variance + 1e-05)
    normed = deviation * inv_std
    gate = gate.astype(F32)
    normed_grad = lifted * gate
    mean_one = jnp.mean(normed_grad, axis=1, keepdims=True)
    mean_two = jnp.mean(normed_grad * normed, axis=1, keepdims=True)
    mixed_grad = inv_std * (normed_grad - mean_one - normed * mean_two)
    return (lifted * normed).astype(BF16), (normed * gate).astype(BF16), mixed_grad.astype(BF16)


def late_rows_body(
    meta, q, k, v, k_bkt, bkt, tab, partial, lifted, gate,
    gate_grad, gated, mixed_grad, mixed, mask, hot, cols,
):
    h = pl.program_id(0)

    @pl.when(h == 0)
    def _():
        mask[...] = mask_tile(meta, meta[6] + HALF, HALF, meta[6] - HALF, HALF, False)
        hot[...] = one_hot(k_bkt[0:1, HALF:])
        cols[...] = bucket_cols(bkt[:, HALF:])

    q_aug = cat(q[...], bias_rows(tab[pl.ds(h, 1), :], cols[...]))
    k_aug = cat(k[...], hot[...])
    attn, _, _ = attn_of(q_aug, k_aug, mask[...])
    mixed[:, pl.ds(pl.multiple_of(h * DIM, DIM), DIM)] = partial[...] + dot_nn(attn.astype(BF16), v[...])

    @pl.when(h == HEADS - 1)
    def _():
        @pl.loop(0, HALF // 32)
        def _(c):
            rows = pl.ds(pl.multiple_of(c * 32, 32), 32)
            a, b, d = norm_rows(mixed[rows, :], lifted[rows, :], gate[rows, :])
            gate_grad[rows, :] = a
            gated[rows, :] = b
            mixed_grad[rows, :] = d


def early_rows_body(partial, came, lifted, gate, _, gate_grad, gated, mixed_grad):
    for c in range(2):
        rows = slice(c * 32, c * 32 + 32)
        a, b, d = norm_rows(
            partial[rows, :] + came[rows, :].astype(F32), lifted[rows, :], gate[rows, :]
        )
        gate_grad[rows, :] = a
        gated[rows, :] = b
        mixed_grad[rows, :] = d


def lifted_body(meta, cot, users, owner, weight, lifted, total):
    @pl.when(pl.program_id(0) == 0)
    def _():
        count = users.shape[0]
        slot = lax.broadcasted_iota(jnp.int32, (DIM, count), 0)
        pick = (owner[...] == meta[7] * 3 + slot) & (slot < 3)
        rows = dot_nn(jnp.where(pick, 1.0, 0.0).astype(BF16), users[...]).astype(BF16)
        pos = meta[6] + lax.broadcasted_iota(jnp.int32, (TOK, 1), 0)
        lane = lanes(TOK)
        last = jnp.where(lane == 0, meta[0], jnp.where(lane == 1, meta[1], meta[2])) - 1
        hits = jnp.where((pos == last) & (lane < 3), 1.0, 0.0).astype(BF16)
        total[...] = (cot[...].astype(F32) + dot_nn(hits, rows)).astype(BF16)

    lifted[...] = dot_nt(total[...], weight[...])


def weight_body(meta, late, early, total, keep, send):
    part = dot_tn(early[...], total[:HALF, :]) + dot_tn(late[...], total[HALF:, :])
    part = part.reshape(4, 2, 32, WIDTH)

    @pl.when(meta[8] == 0)
    def _():
        keep[...] = part[:, 0]
        send[...] = part[:, 1].astype(BF16)

    @pl.when(meta[8] == 1)
    def _():
        keep[...] = part[:, 1]
        send[...] = part[:, 0].astype(BF16)


def own_backward_body(
    meta, q, k, v, kh, vh, kh_bkt, bkt, tab, grad_early, grad_late,
    dq, dq_early, dk, dv, bias, mask, mask_h, hot, hot_h, cols,
):
    h = pl.program_id(0)

    @pl.when(h == 0)
    def _():
        mask[...] = mask_tile(meta, meta[6], TOK, meta[6], TOK, True)
        mask_h[...] = mask_tile(meta, meta[6] + HALF, HALF, meta[6] - HALF, HALF, False)
        hot[...] = one_hot(bkt[...])
        hot_h[...] = one_hot(kh_bkt[0:1, HALF:])
        cols[...] = bucket_cols(bkt[...])

    q_aug = cat(q[...], bias_rows(tab[pl.ds(h, 1), :], cols[...]))
    k_aug = cat(k[...], hot[...])
    kh_aug = cat(kh[...], hot_h[...])
    ge, gl = grad_early[...], grad_late[...]
    attn, sg = back_of(q_aug[:HALF], k_aug[:HALF], mask[:HALF, :HALF], ge, v[:HALF, :])
    early = dot_nn(sg, k_aug[:HALF])
    dk[:HALF, :] = dot_tn(sg, q[:HALF, :])
    dv[:HALF, :] = dot_tn(attn, ge)
    attn, sg = back_of(q_aug[HALF:], k_aug, mask[HALF:, :], gl, v[...])
    late = dot_nn(sg, k_aug)
    more_k = dot_tn(sg, q[HALF:, :])
    more_v = dot_tn(attn, gl)
    dk[:HALF, :] += more_k[:HALF]
    dv[:HALF, :] += more_v[:HALF]
    dk[HALF:, :] = more_k[HALF:]
    dv[HALF:, :] = more_v[HALF:]
    _, sg = back_of(q_aug[HALF:], kh_aug, mask_h[...], gl, vh[...])
    late = late + dot_nn(sg, kh_aug)
    dq_early[...] = early[:, :DIM]
    dq[:HALF, :] = (early[:, :DIM] * (0.5 * SCALE)).astype(BF16)
    dq[HALF:, :] = (late[:, :DIM] * (0.5 * SCALE)).astype(BF16)
    bias[pl.ds(h, 1), :] = bias_sum(early[:, DIM:], cols[:HALF, :]) + bias_sum(late[:, DIM:], cols[HALF:, :])


def sent_backward_body(
    meta, qe, q_bkt, ql, grad_early, grad_late, k, v, bkt, tab, dk_own, dv_own, bias_own,
    dk, dv, dq, bias, mask, mask_l, hot, cols,
):
    h = pl.program_id(0)

    @pl.when(h == 0)
    def _():
        mask[...] = mask_tile(meta, meta[6] + TOK, HALF, meta[6], TOK, False)
        mask_l[...] = mask_tile(meta, meta[6] + TOK + HALF, HALF, meta[6] + HALF, HALF, False)
        hot[...] = one_hot(bkt[...])
        cols[...] = bucket_cols(q_bkt[0:1, :TOK])

    row = tab[pl.ds(h, 1), :]
    added = bias_rows(row, cols[...])
    k_aug = cat(k[...], hot[...])
    ge, gl = grad_early[...], grad_late[...]
    attn, sg = back_of(cat(qe[...], added[:HALF]), k_aug, mask[...], ge, v[...])
    early = dot_nn(sg, k_aug)
    dq[...] = (early[:, :DIM] * 0.5).astype(BF16)
    bias[pl.ds(h, 1), :] = bias_own[pl.ds(h, 1), :] + bias_sum(early[:, DIM:], cols[:HALF, :])
    sum_k = dk_own[...] + dot_tn(sg, qe[...])
    sum_v = dv_own[...] + dot_tn(attn, ge)
    attn, sg = back_of(cat(ql[...], added[HALF:]), k_aug[HALF:], mask_l[...], gl, v[HALF:, :])
    dk[:HALF, :] = (sum_k[:HALF] * (0.5 * SCALE)).astype(BF16)
    dv[:HALF, :] = sum_v[:HALF].astype(BF16)
    dk[HALF:, :] = ((sum_k[HALF:] + dot_tn(sg, ql[...])) * (0.5 * SCALE)).astype(BF16)
    dv[HALF:, :] = (sum_v[HALF:] + dot_tn(attn, gl)).astype(BF16)


def finish_body(own, came, _, out):
    out[...] = ((own[...] * 0.5 + came[...].astype(F32)) * SCALE).astype(BF16)


SMEM = pl.BlockSpec(memory_space=pltpu.SMEM)


def heads_of(rows, at=0):
    return pl.BlockSpec((rows, DIM), lambda h: (at, h))


def whole(*shape):
    return pl.BlockSpec(shape, lambda h: (0,) * len(shape))


def tail_rows(at, cols):
    return pl.BlockSpec((PAD, cols), lambda h: (at, 0))


def shape_of(rows, kind, cols=WIDTH):
    return jax.ShapeDtypeStruct((rows, cols), kind)


def call(body, name, grid, in_specs, out_specs, out_shape, scratch=(), aliases=None, flops=0, moved=0):
    return pl.pallas_call(
        body,
        name=name,
        grid=grid,
        in_specs=in_specs,
        out_specs=out_specs,
        out_shape=out_shape,
        scratch_shapes=list(scratch),
        input_output_aliases=aliases or {},
        cost_estimate=pl.CostEstimate(flops=flops, bytes_accessed=moved, transcendentals=0),
        compiler_params=pltpu.CompilerParams(vmem_limit_bytes=VMEM_LIMIT),
    )


def on_device(
    query_rows, key_rows, value_rows, gate_rows, out_grad, out_weight,
    time_bias, time_bucket, lengths, band_width, user_grad, user_owner,
):
    q, k, v = query_rows[0], key_rows[0], value_rows[0]
    gate, cot = gate_rows[0], out_grad[0]
    bkt = time_bucket
    ctx = lax.axis_index("ctx")
    rank = lax.axis_index("rank")
    n_ctx = lax.axis_size("ctx")
    n_dp = lax.axis_size("dp")
    section = lax.axis_index("dp") * lax.axis_size("rank") + rank
    ends = jnp.cumsum(lengths[0])
    first = ctx * TOK
    meta = jnp.concatenate(
        [ends, band_width[0], jnp.stack([first, section, rank])]
    ).astype(jnp.int32)
    tab = time_bias.astype(F32) * math.sqrt(DIM)
    up = [(i, i + 1) for i in range(n_ctx - 1)]
    down = [(i + 1, i) for i in range(n_ctx - 1)]

    bkt_rows = jnp.pad(
        jnp.broadcast_to(bkt.astype(BF16), (PAD, TOK)), ((0, 0), (0, WIDTH - TOK))
    )
    q_early = lax.ppermute(jnp.concatenate([q[:HALF], bkt_rows]), "ctx", down)
    kv_came = lax.ppermute(jnp.concatenate([k[HALF:], v[HALF:], bkt_rows]), "ctx", up)
    q_late = lax.ppermute(q[HALF:], "ctx", down)
    users = lax.all_to_all(
        jnp.broadcast_to(user_grad[None], (2 * n_dp,) + user_grad.shape), ("dp", "rank"), 0, 0, tiled=True
    ).reshape(-1, WIDTH)
    weight = lax.all_to_all(
        jnp.broadcast_to(out_weight[None], (n_dp,) + out_weight.shape), "dp", 0, 0, tiled=True
    ).reshape(WIDTH, WIDTH)

    col = pltpu.VMEM((TOK, DIM), jnp.int32)
    half_col = pltpu.VMEM((HALF, DIM), jnp.int32)
    hot = pltpu.VMEM((TOK, DIM), BF16)
    half_hot = pltpu.VMEM((HALF, DIM), BF16)

    own_out = call(
        own_forward_body, "own_forward", (HEADS,),
        [SMEM, heads_of(TOK), heads_of(TOK), heads_of(TOK), whole(1, TOK), whole(HEADS, DIM)],
        heads_of(TOK), shape_of(TOK, F32),
        [pltpu.VMEM((TOK, TOK), F32), hot, col],
        flops=4_000_000_000, moved=5 << 20,
    )(meta, q, k, v, bkt, tab)

    lifted, total = call(
        lifted_body, "lifted", (4,),
        [SMEM, whole(TOK, WIDTH), whole(users.shape[0], WIDTH), whole(1, users.shape[0]),
         pl.BlockSpec((HALF, WIDTH), lambda h: (h, 0))],
        (pl.BlockSpec((TOK, HALF), lambda h: (0, h)), whole(TOK, WIDTH)),
        (shape_of(TOK, F32), shape_of(TOK, BF16)),
        flops=1_200_000_000, moved=6 << 20,
    )(meta, cot, users, user_owner[None, :], weight)

    sent_out = call(
        sent_forward_body, "sent_forward", (HEADS,),
        [SMEM, heads_of(HALF), tail_rows(HALF // PAD, TOK), heads_of(TOK), heads_of(TOK),
         whole(1, TOK), whole(HEADS, DIM)],
        heads_of(HALF), shape_of(HALF, BF16),
        [pltpu.VMEM((HALF, TOK), F32), hot, half_col],
        flops=2_000_000_000, moved=3 << 20,
    )(meta, q_early, q_early, k, v, bkt, tab)
    out_came = lax.ppermute(sent_out, "ctx", up)

    late_half = pl.BlockSpec((HALF, WIDTH), lambda h: (1, 0))
    gate_grad, gated_late, grad_late = call(
        late_rows_body, "late_rows", (HEADS,),
        [SMEM, heads_of(HALF, 1), heads_of(HALF, 0), heads_of(HALF, 1), tail_rows(TOK // PAD, TOK),
         whole(1, TOK), whole(HEADS, DIM), heads_of(HALF, 1), late_half, late_half],
        (late_half, whole(HALF, WIDTH), whole(HALF, WIDTH)),
        (shape_of(TOK, BF16), shape_of(HALF, BF16), shape_of(HALF, BF16)),
        [pltpu.VMEM((HALF, WIDTH), F32), pltpu.VMEM((HALF, HALF), F32), half_hot, half_col],
        flops=1_000_000_000, moved=7 << 20,
    )(meta, q, kv_came, kv_came, kv_came, bkt, tab, own_out, lifted, gate)
    grad_late_came = lax.ppermute(grad_late, "ctx", down)

    part = pl.BlockSpec((64, WIDTH), lambda h: (h, 0))
    gate_grad, gated_early, grad_early = call(
        early_rows_body, "early_rows", (HALF // 64,),
        [part, part, part, part, pl.BlockSpec(memory_space=pl.ANY)],
        (part, part, part),
        (shape_of(TOK, BF16), shape_of(HALF, BF16), shape_of(HALF, BF16)),
        aliases={4: 0}, flops=10_000_000, moved=5 << 20,
    )(own_out, out_came, lifted, gate, gate_grad)
    grad_early_came = lax.ppermute(grad_early, "ctx", down)

    cut = pl.BlockSpec((HALF, HALF), lambda h: (0, h))
    piece = pl.BlockSpec((4, 32, WIDTH), lambda h: (h, 0, 0))
    keep, send = call(
        weight_body, "weight_part", (4,),
        [SMEM, cut, cut, whole(TOK, WIDTH)],
        (piece, piece),
        (jax.ShapeDtypeStruct((16, 32, WIDTH), F32), jax.ShapeDtypeStruct((16, 32, WIDTH), BF16)),
        flops=1_100_000_000, moved=6 << 20,
    )(meta, gated_late, gated_early, total)
    other = lax.ppermute(send, "rank", [(0, 1), (1, 0)])
    pair = (keep + other.astype(F32)).astype(BF16)
    rows = jnp.sum(lax.all_to_all(pair, "dp", 0, 0, tiled=True).astype(F32), axis=0).astype(BF16)
    rows = lax.all_to_all(
        jnp.broadcast_to(rows[None], (2 * n_ctx,) + rows.shape), ("ctx", "rank"), 0, 0, tiled=True
    )
    weight_grad = jnp.sum(
        rows.reshape(n_ctx, 64, WIDTH).astype(F32), axis=0
    )

    dq, dq_early, dk_own, dv_own, bias_own = call(
        own_backward_body, "own_backward", (HEADS,),
        [SMEM, heads_of(TOK), heads_of(TOK), heads_of(TOK), heads_of(HALF, 0), heads_of(HALF, 1),
         tail_rows(TOK // PAD, TOK), whole(1, TOK), whole(HEADS, DIM), heads_of(HALF), heads_of(HALF)],
        (heads_of(TOK), heads_of(HALF), heads_of(TOK), heads_of(TOK), whole(HEADS, DIM)),
        (shape_of(TOK, BF16), shape_of(HALF, F32), shape_of(TOK, F32), shape_of(TOK, F32),
         shape_of(HEADS, F32, DIM)),
        [pltpu.VMEM((TOK, TOK), F32), pltpu.VMEM((HALF, HALF), F32), hot, half_hot, col],
        flops=8_000_000_000, moved=12 << 20,
    )(meta, q, k, v, kv_came, kv_came, kv_came, bkt, tab, grad_early, grad_late)

    dk, dv, dq_sent, bias = call(
        sent_backward_body, "sent_backward", (HEADS,),
        [SMEM, heads_of(HALF), tail_rows(HALF // PAD, WIDTH), heads_of(HALF), heads_of(HALF),
         heads_of(HALF), heads_of(TOK), heads_of(TOK), whole(1, TOK), whole(HEADS, DIM),
         heads_of(TOK), heads_of(TOK), whole(HEADS, DIM)],
        (heads_of(TOK), heads_of(TOK), heads_of(HALF), whole(HEADS, DIM)),
        (shape_of(TOK, BF16), shape_of(TOK, BF16), shape_of(HALF, BF16), shape_of(HEADS, F32, DIM)),
        [pltpu.VMEM((HALF, TOK), F32), pltpu.VMEM((HALF, HALF), F32), hot, col],
        flops=5_000_000_000, moved=10 << 20,
    )(meta, q_early, q_early, q_late, grad_early_came, grad_late_came, k, v, bkt, tab,
      dk_own, dv_own, bias_own)
    dq_came = lax.ppermute(dq_sent, "ctx", up)

    dq = call(
        finish_body, "finish", (HALF // 64,),
        [part, part, pl.BlockSpec(memory_space=pl.ANY)],
        part, shape_of(TOK, BF16), aliases={2: 0}, flops=1_000_000, moved=2 << 20,
    )(dq_early, dq_came, dq)

    spread = jnp.broadcast_to(bias[None, :, None], (n_dp, n_ctx, 2, DIM)).reshape(-1, DIM)
    bias_grad = jnp.sum(
        lax.all_to_all(spread, ("dp", "ctx", "rank"), 0, 0, tiled=True), axis=0, keepdims=True
    )
    return (dq[None], dk[None], dv[None], gate_grad[None], weight_grad, bias_grad)


def solution(mesh):
    rows = P(("dp", "rank"), "ctx", None)
    users = P(("dp", "rank"), None)
    return jax.shard_map(
        on_device,
        mesh=mesh,
        in_specs=(
            rows, rows, rows, rows, rows, P("dp", None), P(), P(("dp", "rank"), "ctx"),
            users, users, users, P(),
        ),
        out_specs=(rows, rows, rows, rows, P("dp", None), P("ctx", None)),
        check_vma=False,
    )
```

time: 730 us -> 212 us (0.29)
  matrix products: 154 us -> 0 us
  waiting for transfers between devices: 175 us -> 59.8 us
  blocking collectives: 129 us -> 17.3 us
  local copies, waits for them, and re-layouts: 117 us -> 12.7 us
  Pallas kernels: 0 us -> 65.8 us
  loops' own time: 63.2 us -> 0 us
  other arithmetic: 33.5 us -> 6.48 us
  between operations: 14.1 us -> 0.95 us
  starting transfers between devices: 38.5 us -> 47.2 us
    dot_general x77 -> x0, matrix products: 154 us -> none  [the longest x8 26.1 us: forward_block(): jnp.dot(attn_blk, value_win, preferred_element_type=jnp.float32)]
    all_to_all x8 -> x4, waiting for transfers between devices: 134 us -> 11.4 us  [the longest x1 11.4 us: on_device(): lax.all_to_all(spread, ('dp', 'ctx', 'rank'), 0, 0, tiled=True)]
    all_gather x2 -> x0, blocking collectives: 65.8 us -> none  [the longest x1 34.2 us: on_device(): bucket_side = lax.all_gather(buckets, 'ctx', axis=0, tiled=True)]
    pallas_call x0 -> x9, Pallas kernels: none -> 65.8 us  [the longest x1 16.5 us: on_device(): call(own_backward_body, 'own_backward', (HEADS,), [SMEM, heads_of(TOK), h...]
    psum x1 -> x0, blocking collectives: 63.3 us -> none  [on_device(): bias_grad = lax.psum(bias_part, ('dp', 'rank'))]
    another operation x2 -> x0, loops' own time: 63.2 us -> none  [the longest x1 31.8 us: attend_backward(): lax.scan(backward_block, start_state, (starts, saved[0]))]
    ppermute x0 -> x8, waiting for transfers between devices: none -> 48.4 us  [the longest x1 30.1 us: on_device(): dq_came = lax.ppermute(dq_sent, 'ctx', up)]
    dynamic_update_slice x16 -> x0, local copies, waits for them, and re-layouts: 45.6 us -> none  [the longest x8 22.8 us: backward_block(): lax.dynamic_update_slice_in_dim(value_acc, lax.dynamic_slice_in_dim(value...]
  transfers between devices with their start and end apart: 11 -> 12, of which waited for: 6 -> 4; matrix products, arithmetic and copies ran while one was open for 40% -> 3% of each run, Pallas kernels for 0% -> 28%
where the time goes in v1:
time: 212 us; the launch traced here: 210 us
  Pallas kernels  65.8 us (31%)
  waiting for transfers between devices  59.8 us (28%)
  starting transfers between devices  47.2 us (22%)
  blocking collectives  17.3 us (8%)
  local copies, waits for them, and re-layouts  12.7 us (6%)
  other arithmetic  6.48 us (3%)
    ppermute x1, waiting for transfers between devices, on_device(): dq_came = lax.ppermute(dq_sent, 'ctx', up)  30.1 us
    all_to_all x1, blocking collectives, on_device(): lax.all_to_all(jnp.broadcast_to(user_grad[None], (2 * n_dp,) + user_grad....  17.3 us
    pallas_call x1, Pallas kernels, on_device(): call(own_backward_body, 'own_backward', (HEADS,), [SMEM, heads_of(TOK), h...  16.5 us
    all_to_all x1, starting transfers between devices, on_device(): lax.all_to_all(spread, ('dp', 'ctx', 'rank'), 0, 0, tiled=True)  14.1 us
    pallas_call x1, Pallas kernels, on_device(): call(sent_backward_body, 'sent_backward', (HEADS,), [SMEM, heads_of(HALF)...  12.1 us
    all_to_all x1, waiting for transfers between devices, on_device(): lax.all_to_all(spread, ('dp', 'ctx', 'rank'), 0, 0, tiled=True)  11.4 us
    pallas_call x1, Pallas kernels, on_device(): call(late_rows_body, 'late_rows', (HEADS,), [SMEM, heads_of(HALF, 1), hea...  10.6 us
    ppermute x1, waiting for transfers between devices, on_device(): q_early = lax.ppermute(jnp.concatenate([q[:HALF], bkt_rows]), 'ctx', down)  9.63 us
  transfers between devices with their start and end apart: 12, of which 4 were waited for; matrix products, arithmetic and copies ran while one was open for 3% of the time, Pallas kernels for 28%

profile of v1, /device:TPU:1, one launch (start us, length us, event | category | flops | bytes accessed | tf_op | source)
XLA Modules:
  0.0 210.3 jit_solution(15744902826262741072)
XLA Ops:
  0.6 0.8 broadcast_in_dim.23
  1.4 17.3 %all_to_all.29 = bf16[32,3,1024]{2,1,0:T(4,128)(2,1)S(1)} all-to-all(bf16[32,3,1024]{2,1,0:T(4,128)(2,1)S(1)} %broadcast_in_dim.23), channel_id=1, replica_groups=mesh['dp'=16,'ctx'=8,'rank'=2] {'dp','rank'}, dimensions={0} | all-to-all | bytes 393216 | tf_op jit(solution)/shard_map/all_to_all | solution.py:354
  18.7 2.5 %broadcast_in_dim.50 = bf16[16,64,1024]{2,1,0:T(8,128)(2,1)} broadcast(bf16[64,1024]{1,0:T(8,128)(2,1)} %param.17), dimensions={1,2} | broadcast | bytes 2228224 | tf_op jit(solution)/shard_map/broadcast_in_dim | solution.py:358
  21.2 4.6 %all-to-all-start.1 = ((bf16[16,64,1024]{2,1,0:T(8,128)(2,1)}), bf16[16,64,1024]{2,1,0:T(8,128)(2,1)}, u32[]{:S(2)}, u32[]{:S(2)}) async-start(bf16[16,64,1024]{2,1,0:T(8,128)(2,1)} %broadcast_in_dim.50), calls=%async_computation.1 | async-start | bytes 4194304 | tf_op jit(solution)/shard_map/all_to_all | solution.py:357
  25.8 0.0 copy-start.6
  25.8 0.0 copy-start.9
  25.9 0.9 slice_bitcast_fusion
  26.7 0.8 pad_maximum_fusion.1
  27.6 1.4 collective-permute-start.1
  29.0 0.0 copy-done.6
  29.0 0.0 copy-done.9
  29.0 0.1 slice_bitcast_fusion.2
  29.1 1.0 pad_maximum_fusion
  30.1 4.2 %collective-permute-start = (bf16[528,1024]{1,0:T(8,128)(2,1)}, bf16[528,1024]{1,0:T(8,128)(2,1)S(1)}, u32[]{:S(2)}, u32[]{:S(2)}) collective-permute-start(bf16[528,1024]{1,0:T(8,128)(2,1)} %pad_maximum_fusion), channel_id=1, source_target_pairs={{0,2},{2,4},{4,6},{6,8},{8,10},{10,12},{12,14},{1,3},{3,5},{5,7},{... | collective-permute-start | bytes 3244040 | tf_op jit(solution)/shard_map/ppermute | solution.py:352
  34.4 0.2 reduce-window.9
  34.6 0.0 copy-done.17
  34.6 0.1 concatenate.9.meta
  34.7 9.6 %collective-permute-done.1.q.q_bkt.qe = bf16[272,1024]{1,0:T(8,128)(2,1)} collective-permute-done((bf16[272,1024]{1,0:T(8,128)(2,1)}, bf16[272,1024]{1,0:T(8,128)(2,1)}, u32[]{:S(2)}, u32[]{:S(2)}) %collective-permute-start.1) | collective-permute-done | bytes 557088 | tf_op jit(solution)/shard_map/ppermute | solution.py:351
  44.3 1.2 copy-done.10
  45.5 6.9 %sent_forward.1 = bf16[256,1024]{1,0:T(8,128)(2,1)} custom-call(s32[9]{0:T(128)S(1)} %concatenate.9.meta, bf16[272,1024]{1,0:T(8,128)(2,1)} %collective-permute-done.1.q.q_bkt.qe, bf16[272,1024]{1,0:T(8,128)(2,1)} %collective-permute-done.1.q.q_bkt.qe, bf16[512,1024]{1,0:T(8,128)(2,1)S(1)} %bitcast.36, bf16[512,1024]{1,0:T(8,128)(2,1)S(1)} %bitcast.40, ...), custom_call_target="tpu_custom_call" | custom-call | flops 2000000000 | bytes 3145728 | tf_op jit(solution)/shard_map/sent_forward/pallas_call | solution.py:383
  52.4 3.6 %collective-permute-start.2 = (bf16[256,1024]{1,0:T(8,128)(2,1)}, bf16[256,1024]{1,0:T(8,128)(2,1)S(1)}, u32[]{:S(2)}, u32[]{:S(2)}) collective-permute-start(bf16[256,1024]{1,0:T(8,128)(2,1)} %sent_forward.1), channel_id=1, source_target_pairs={{0,2},{2,4},{4,6},{6,8},{8,10},{10,12},{12,14},{1,3},{3,5},{5,7},{... | collective-permute-start | bytes 1572872 | tf_op jit(solution)/shard_map/ppermute | solution.py:391
  56.0 0.0 copy-start.15
  56.0 7.1 %own_forward.1.partial = f32[512,1024]{1,0:T(8,128)S(1)} custom-call(s32[9]{0:T(128)S(1)} %concatenate.9.meta, bf16[512,1024]{1,0:T(8,128)(2,1)S(1)} %bitcast.31, bf16[512,1024]{1,0:T(8,128)(2,1)S(1)} %bitcast.37, bf16[512,1024]{1,0:T(8,128)(2,1)S(1)} %bitcast.41, s32[1,512]{1,0:T(1,128)S(1)} %copy-done.13, f32[8,128]{1,0:T(8,128)S(1)} %convert_multiply_fusion.tab), custom_call_target="tpu_custom_call" | custom-call | flops 4000000000 | bytes 5242880 | tf_op jit(solution)/shard_map/own_forward/pallas_call | solution.py:366
  63.1 1.3 copy-done.1
  64.4 0.2 reshape.62.users
  64.6 0.0 all-to-all-done.1
  64.6 0.0 copy-done.15
  64.6 0.0 copy-start.14
  64.6 1.2 copy-done.14
  65.8 4.3 %lifted.1 = (f32[512,1024]{1,0:T(8,128)S(1)}, bf16[512,1024]{1,0:T(8,128)(2,1)S(1)}) custom-call(s32[9]{0:T(128)S(1)} %concatenate.9.meta, bf16[512,1024]{1,0:T(8,128)(2,1)S(1)} %bitcast.44, bf16[96,1024]{1,0:T(8,128)(2,1)S(1)} %reshape.62.users, s32[1,96]{1,0:T(1,128)S(1)} %bitcast.45, bf16[1024,1024]{1,0:T(8,128)(2,1)} %bitcast.14.weight), custom_call_target="tpu_custom_call" | custom-call | flops 1200000000 | bytes 6291456 | tf_op jit(solution)/shard_map/lifted/pallas_call | solution.py:374
  70.2 1.3 copy-done.3
  71.5 0.0 collective-permute-done.k.v.k_bkt.kh.vh.kh_bkt
  71.5 0.0 copy-done.5
  71.5 10.6 %late_rows.1 = (bf16[512,1024]{1,0:T(8,128)(2,1)}, bf16[256,1024]{1,0:T(8,128)(2,1)S(1)}, bf16[256,1024]{1,0:T(8,128)(2,1)}) custom-call(s32[9]{0:T(128)S(1)} %concatenate.9.meta, bf16[512,1024]{1,0:T(8,128)(2,1)S(1)} %bitcast.32, bf16[528,1024]{1,0:T(8,128)(2,1)S(1)} %collective-permute-done.k.v.k_bkt.kh.vh.kh_bkt, ...), custom_call_target="tpu_custom_call" | custom-call | flops 1000000000 | bytes 7340032 | tf_op jit(solution)/shard_map/late_rows/pallas_call | solution.py:394
  82.2 0.0 collective-permute-done.2.came
  82.2 4.0 %early_rows.1 = (bf16[512,1024]{1,0:T(8,128)(2,1)}, bf16[256,1024]{1,0:T(8,128)(2,1)S(1)}, bf16[256,1024]{1,0:T(8,128)(2,1)}) custom-call(f32[512,1024]{1,0:T(8,128)S(1)} %copy-done.2, bf16[256,1024]{1,0:T(8,128)(2,1)S(1)} %collective-permute-done.2.came, f32[512,1024]{1,0:T(8,128)} %copy-done.3, ...), custom_call_target="tpu_custom_call", output_to_operand_aliasing={{0}: (4, {})} | custom-call | flops 10000000 | bytes 5242880 | tf_op jit(solution)/shard_map/early_rows/pallas_call | solution.py:406
  86.1 2.8 %weight_part.1 = (f32[16,32,1024]{2,1,0:T(8,128)S(1)}, bf16[16,32,1024]{2,1,0:T(8,128)(2,1)S(1)}) custom-call(s32[9]{0:T(128)S(1)} %concatenate.9.meta, bf16[256,1024]{1,0:T(8,128)(2,1)S(1)} %get-tuple-element.38.late, bf16[256,1024]{1,0:T(8,128)(2,1)S(1)} %get-tuple-element.39.early, bf16[512,1024]{1,0:T(8,128)(2,1)S(1)} %get-tuple-element.40.total), custom_call_target="tpu_custom_call" | custom-call | flops 1100000000 | bytes 6291456 | tf_op jit(solution)/shard_map/weight_part/pallas_call | solution.py:417
  88.9 1.1 collective-permute-start.7
  90.1 1.3 collective-permute-start.3
  91.3 1.3 collective-permute-start.4
  92.6 1.3 collective-permute-start.5
  93.9 0.0 collective-permute-done.7
  94.0 1.3 add_convert_fusion
  95.3 6.7 %all-to-all-start.2 = ((bf16[16,32,1024]{2,1,0:T(8,128)(2,1)}), bf16[16,32,1024]{2,1,0:T(8,128)(2,1)}, u32[]{:S(2)}, u32[]{:S(2)}) async-start(bf16[16,32,1024]{2,1,0:T(8,128)(2,1)} %add_convert_fusion), calls=%async_computation.2 | async-start | bytes 2097152 | tf_op jit(solution)/shard_map/all_to_all | solution.py:426
  102.0 0.0 copy-start.11
  102.0 1.2 copy-done.11
  103.2 16.5 %own_backward.1 = (bf16[512,1024]{1,0:T(8,128)(2,1)}, f32[256,1024]{1,0:T(8,128)S(1)}, f32[512,1024]{1,0:T(8,128)}, f32[512,1024]{1,0:T(8,128)}, f32[8,128]{1,0:T(8,128)S(1)}) custom-call(s32[9]{0:T(128)S(1)} %concatenate.9.meta, bf16[512,1024]{1,0:T(8,128)(2,1)S(1)} %bitcast.33, bf16[512,1024]{1,0:T(8,128)(2,1)S(1)} %bitcast.38, ...), custom_call_target="tpu_custom_call" | custom-call | flops 8000000000 | bytes 12582912 | tf_op jit(solution)/shard_map/own_backward/pallas_call | solution.py:434
  119.8 0.0 collective-permute-done.3.ql
  119.8 0.0 collective-permute-done.4.grad_early
  119.8 8.7 %collective-permute-done.5.grad_late = bf16[256,1024]{1,0:T(8,128)(2,1)} collective-permute-done((bf16[256,1024]{1,0:T(8,128)(2,1)}, bf16[256,1024]{1,0:T(8,128)(2,1)}, u32[]{:S(2)}, u32[]{:S(2)}) %collective-permute-start.5) | collective-permute-done | bytes 524320 | tf_op jit(solution)/shard_map/ppermute | solution.py:403
  128.5 12.1 %sent_backward.1 = (bf16[512,1024]{1,0:T(8,128)(2,1)}, bf16[512,1024]{1,0:T(8,128)(2,1)}, bf16[256,1024]{1,0:T(8,128)(2,1)S(1)}, f32[8,128]{1,0:T(8,128)S(1)}) custom-call(s32[9]{0:T(128)S(1)} %concatenate.9.meta, bf16[272,1024]{1,0:T(8,128)(2,1)} %collective-permute-done.1.q.q_bkt.qe, bf16[272,1024]{1,0:T(8,128)(2,1)} %collective-permute-done.1.q.q_bkt.qe, ...), custom_call_target="tpu_custom_call" | custom-call | flops 5000000000 | bytes 10485760 | tf_op jit(solution)/shard_map/sent_backward/pallas_call | solution.py:445
  140.6 0.0 all-to-all-done.2
  140.6 0.7 broadcast_in_dim.56
  141.3 14.1 %all-to-all-start.4 = ((f32[256,1,128]{2,1,0:T(1,128)}), f32[256,1,128]{2,1,0:T(1,128)S(1)}, u32[]{:S(2)}, u32[]{:S(2)}) async-start(f32[256,1,128]{2,1,0:T(1,128)} %bitcast.22), calls=%async_computation.4 | async-start | bytes 262144 | tf_op jit(solution)/shard_map/all_to_all | solution.py:466
  155.4 1.4 reduce_sum.30
  156.9 11.4 %all-to-all-done.4 = f32[256,1,128]{2,1,0:T(1,128)S(1)} async-done(((f32[256,1,128]{2,1,0:T(1,128)}), f32[256,1,128]{2,1,0:T(1,128)S(1)}, u32[]{:S(2)}, u32[]{:S(2)}) %all-to-all-start.4) | async-done | bytes 131104 | tf_op jit(solution)/shard_map/all_to_all | solution.py:466
  168.2 1.1 broadcast_in_dim.55
  169.4 4.3 %all-to-all-start.3 = ((bf16[16,32,1024]{2,1,0:T(8,128)(2,1)}), bf16[16,32,1024]{2,1,0:T(8,128)(2,1)S(1)}, u32[]{:S(2)}, u32[]{:S(2)}) async-start(bf16[16,32,1024]{2,1,0:T(8,128)(2,1)} %broadcast_in_dim.55), calls=%async_computation.3 | async-start | bytes 2097152 | tf_op jit(solution)/shard_map/all_to_all | solution.py:427
  173.7 3.3 %collective-permute-start.6 = (bf16[256,1024]{1,0:T(8,128)(2,1)S(1)}, bf16[256,1024]{1,0:T(8,128)(2,1)S(1)}, u32[]{:S(2)}, u32[]{:S(2)}) collective-permute-start(bf16[256,1024]{1,0:T(8,128)(2,1)S(1)} %get-tuple-element.33), channel_id=1, source_target_pairs={{0,2},{2,4},{4,6},{6,8},{8,10},{10,12},{12,14},{1,3},{3,5},{5,7},{... | collective-permute-start | bytes 1572872 | tf_op jit(solution)/shard_map/ppermute | solution.py:456
  177.0 0.8 reduce_sum.32
  177.8 30.1 %collective-permute-done.6.came = bf16[256,1024]{1,0:T(8,128)(2,1)S(1)} collective-permute-done((bf16[256,1024]{1,0:T(8,128)(2,1)S(1)}, bf16[256,1024]{1,0:T(8,128)(2,1)S(1)}, u32[]{:S(2)}, u32[]{:S(2)}) %collective-permute-start.6) | collective-permute-done | bytes 524320 | tf_op jit(solution)/shard_map/ppermute | solution.py:456
  207.9 1.5 finish.1
  209.4 0.0 all-to-all-done.3
  209.4 0.9 convert_reduce_fusion
  (27 shorter events, 0.1 us)
Async XLA Ops:
  21.2 4.6 %copy-start.13 = (s32[1,512]{1,0:T(1,128)S(1)}, s32[1,512]{1,0:T(1,128)}, u32[]{:S(2)}) copy-start(s32[1,512]{1,0:T(1,128)} %bkt.9) | copy-start | bytes 6148
  21.2 4.6 %copy-start.4 = (bf16[1,512,1024]{2,1,0:T(8,128)(2,1)S(1)}, bf16[1,512,1024]{2,1,0:T(8,128)(2,1)}, u32[]{:S(2)}) copy-start(bf16[1,512,1024]{2,1,0:T(8,128)(2,1)} %param.12) | copy-start | bytes 3145732
  21.2 43.4 %all-to-all-start.1 = ((bf16[16,64,1024]{2,1,0:T(8,128)(2,1)}), bf16[16,64,1024]{2,1,0:T(8,128)(2,1)}, u32[]{:S(2)}, u32[]{:S(2)}) async-start(bf16[16,64,1024]{2,1,0:T(8,128)(2,1)} %broadcast_in_dim.50), calls=%async_computation.1 | async-start | bytes 4194304 | tf_op jit(solution)/shard_map/all_to_all | solution.py:357
  25.8 3.2 %copy-start.6 = (bf16[1,512,1024]{2,1,0:T(8,128)(2,1)S(1)}, bf16[1,512,1024]{2,1,0:T(8,128)(2,1)}, u32[]{:S(2)}) copy-start(bf16[1,512,1024]{2,1,0:T(8,128)(2,1)} %param.13) | copy-start | bytes 3145732
  25.8 3.2 %copy-start.9 = (bf16[1,512,1024]{2,1,0:T(8,128)(2,1)S(1)}, bf16[1,512,1024]{2,1,0:T(8,128)(2,1)}, u32[]{:S(2)}) copy-start(bf16[1,512,1024]{2,1,0:T(8,128)(2,1)} %param.14) | copy-start | bytes 3145732
  27.6 6.8 %copy-start.18 = (s32[1,3]{1,0:T(1,128)S(1)}, s32[1,3]{1,0:T(1,128)}, u32[]{:S(2)}) copy-start(s32[1,3]{1,0:T(1,128)} %param.20) | copy-start | bytes 40
  27.6 7.0 %copy-start.17 = (s32[1,3]{1,0:T(1,128)S(1)}, s32[1,3]{1,0:T(1,128)}, u32[]{:S(2)}) copy-start(s32[1,3]{1,0:T(1,128)} %param.21) | copy-start | bytes 40
  27.6 7.1 %copy-start.16 = (bf16[8,128]{1,0:T(8,128)(2,1)S(1)}, bf16[8,128]{1,0:T(8,128)(2,1)}, u32[]{:S(2)}) copy-start(bf16[8,128]{1,0:T(8,128)(2,1)} %param.18) | copy-start | bytes 6148
  27.6 16.7 %collective-permute-start.1 = (bf16[272,1024]{1,0:T(8,128)(2,1)}, bf16[272,1024]{1,0:T(8,128)(2,1)}, u32[]{:S(2)}, u32[]{:S(2)}) collective-permute-start(bf16[272,1024]{1,0:T(8,128)(2,1)} %pad_maximum_fusion.1), channel_id=1, source_target_pairs={{2,0},{4,2},{6,4},{8,6},{10,8},{12,10},{14,12},{3,1},{5,3},{7,5},{... | collective-permute-start | bytes 1671176 | tf_op jit(solution)/shard_map/ppermute | solution.py:351
  30.1 41.4 %collective-permute-start = (bf16[528,1024]{1,0:T(8,128)(2,1)}, bf16[528,1024]{1,0:T(8,128)(2,1)S(1)}, u32[]{:S(2)}, u32[]{:S(2)}) collective-permute-start(bf16[528,1024]{1,0:T(8,128)(2,1)} %pad_maximum_fusion), channel_id=1, source_target_pairs={{0,2},{2,4},{4,6},{6,8},{8,10},{10,12},{12,14},{1,3},{3,5},{5,7},{... | collective-permute-start | bytes 3244040 | tf_op jit(solution)/shard_map/ppermute | solution.py:352
  44.3 1.2 copy-start.10
  45.5 10.4 %copy-start.7 = (bf16[1,512,1024]{2,1,0:T(8,128)(2,1)S(1)}, bf16[1,512,1024]{2,1,0:T(8,128)(2,1)}, u32[]{:S(2)}) copy-start(bf16[1,512,1024]{2,1,0:T(8,128)(2,1)} %param.13) | copy-start | bytes 3145732
  52.4 29.8 %collective-permute-start.2 = (bf16[256,1024]{1,0:T(8,128)(2,1)}, bf16[256,1024]{1,0:T(8,128)(2,1)S(1)}, u32[]{:S(2)}, u32[]{:S(2)}) collective-permute-start(bf16[256,1024]{1,0:T(8,128)(2,1)} %sent_forward.1), channel_id=1, source_target_pairs={{0,2},{2,4},{4,6},{6,8},{8,10},{10,12},{12,14},{1,3},{3,5},{5,7},{... | collective-permute-start | bytes 1572872 | tf_op jit(solution)/shard_map/ppermute | solution.py:391
  56.0 8.6 %copy-start.15 = (s32[96]{0:T(128)S(1)}, s32[96]{0:T(128)}, u32[]{:S(2)}) copy-start(s32[96]{0:T(128)} %param.23) | copy-start | bytes 1156
  63.1 1.3 copy-start.1
  64.6 1.2 copy-start.14
  65.8 5.7 %copy-start.5 = (bf16[1,512,1024]{2,1,0:T(8,128)(2,1)S(1)}, bf16[1,512,1024]{2,1,0:T(8,128)(2,1)}, u32[]{:S(2)}) copy-start(bf16[1,512,1024]{2,1,0:T(8,128)(2,1)} %param.15) | copy-start | bytes 3145732
  70.2 1.3 copy-start.3
  71.5 10.7 %copy-start = (bf16[528,1024]{1,0:T(8,128)(2,1)}, bf16[528,1024]{1,0:T(8,128)(2,1)S(1)}, u32[]{:S(2)}) copy-start(bf16[528,1024]{1,0:T(8,128)(2,1)S(1)} %collective-permute-done.k.v.k_bkt.kh.vh.kh_bkt) | copy-start | bytes 3244036
  71.5 10.7 %copy-start.2 = (f32[512,1024]{1,0:T(8,128)S(1)}, f32[512,1024]{1,0:T(8,128)}, u32[]{:S(2)}) copy-start(f32[512,1024]{1,0:T(8,128)} %copy-done.1) | copy-start | bytes 6291460
  88.9 5.0 %collective-permute-start.7 = (bf16[16,32,1024]{2,1,0:T(8,128)(2,1)S(1)}, bf16[16,32,1024]{2,1,0:T(8,128)(2,1)S(1)}, u32[]{:S(2)}, u32[]{:S(2)}) collective-permute-start(bf16[16,32,1024]{2,1,0:T(8,128)(2,1)S(1)} %get-tuple-element.42), channel_id=1, source_target_pairs={{0,1},{1,0},{2,3},{3,2},{4,5},{5,4},{6,7},{7,6},{8,9},{9,8},{10,11... | collective-permute-start | bytes 3145736 | tf_op jit(solution)/shard_map/ppermute | solution.py:424
  90.1 29.7 %collective-permute-start.3 = (bf16[256,1024]{1,0:T(8,128)(2,1)}, bf16[256,1024]{1,0:T(8,128)(2,1)}, u32[]{:S(2)}, u32[]{:S(2)}) collective-permute-start(bf16[256,1024]{1,0:T(8,128)(2,1)} %get-tuple-element.44), channel_id=1, source_target_pairs={{2,0},{4,2},{6,4},{8,6},{10,8},{12,10},{14,12},{3,1},{5,3},{7,5},{... | collective-permute-start | bytes 1572872 | tf_op jit(solution)/shard_map/ppermute | solution.py:353
  91.3 28.4 %collective-permute-start.4 = (bf16[256,1024]{1,0:T(8,128)(2,1)}, bf16[256,1024]{1,0:T(8,128)(2,1)}, u32[]{:S(2)}, u32[]{:S(2)}) collective-permute-start(bf16[256,1024]{1,0:T(8,128)(2,1)} %get-tuple-element.27.grad_early), channel_id=1, source_target_pairs={{2,0},{4,2},{6,4},{8,6},{10,8},{12,10},{14,12},{3,1},{5,3},{7,5},{... | collective-permute-start | bytes 1572872 | tf_op jit(solution)/shard_map/ppermute | solution.py:413
  92.6 35.8 %collective-permute-start.5 = (bf16[256,1024]{1,0:T(8,128)(2,1)}, bf16[256,1024]{1,0:T(8,128)(2,1)}, u32[]{:S(2)}, u32[]{:S(2)}) collective-permute-start(bf16[256,1024]{1,0:T(8,128)(2,1)} %get-tuple-element.28.grad_late), channel_id=1, source_target_pairs={{2,0},{4,2},{6,4},{8,6},{10,8},{12,10},{14,12},{3,1},{5,3},{7,5},{... | collective-permute-start | bytes 1572872 | tf_op jit(solution)/shard_map/ppermute | solution.py:403
  95.3 6.7 %copy-start.8 = (bf16[1,512,1024]{2,1,0:T(8,128)(2,1)S(1)}, bf16[1,512,1024]{2,1,0:T(8,128)(2,1)}, u32[]{:S(2)}) copy-start(bf16[1,512,1024]{2,1,0:T(8,128)(2,1)} %param.13) | copy-start | bytes 3145732
  95.3 45.3 %all-to-all-start.2 = ((bf16[16,32,1024]{2,1,0:T(8,128)(2,1)}), bf16[16,32,1024]{2,1,0:T(8,128)(2,1)}, u32[]{:S(2)}, u32[]{:S(2)}) async-start(bf16[16,32,1024]{2,1,0:T(8,128)(2,1)} %add_convert_fusion), calls=%async_computation.2 | async-start | bytes 2097152 | tf_op jit(solution)/shard_map/all_to_all | solution.py:426
  102.0 1.2 copy-start.11
  103.2 25.3 %copy-start.12 = (bf16[1,512,1024]{2,1,0:T(8,128)(2,1)S(1)}, bf16[1,512,1024]{2,1,0:T(8,128)(2,1)}, u32[]{:S(2)}) copy-start(bf16[1,512,1024]{2,1,0:T(8,128)(2,1)} %param.14) | copy-start | bytes 3145732
  141.3 26.9 %all-to-all-start.4 = ((f32[256,1,128]{2,1,0:T(1,128)}), f32[256,1,128]{2,1,0:T(1,128)S(1)}, u32[]{:S(2)}, u32[]{:S(2)}) async-start(f32[256,1,128]{2,1,0:T(1,128)} %bitcast.22), calls=%async_computation.4 | async-start | bytes 262144 | tf_op jit(solution)/shard_map/all_to_all | solution.py:466
  169.4 40.0 %all-to-all-start.3 = ((bf16[16,32,1024]{2,1,0:T(8,128)(2,1)}), bf16[16,32,1024]{2,1,0:T(8,128)(2,1)S(1)}, u32[]{:S(2)}, u32[]{:S(2)}) async-start(bf16[16,32,1024]{2,1,0:T(8,128)(2,1)} %broadcast_in_dim.55), calls=%async_computation.3 | async-start | bytes 2097152 | tf_op jit(solution)/shard_map/all_to_all | solution.py:427
  173.7 34.2 %collective-permute-start.6 = (bf16[256,1024]{1,0:T(8,128)(2,1)S(1)}, bf16[256,1024]{1,0:T(8,128)(2,1)S(1)}, u32[]{:S(2)}, u32[]{:S(2)}) collective-permute-start(bf16[256,1024]{1,0:T(8,128)(2,1)S(1)} %get-tuple-element.33), channel_id=1, source_target_pairs={{0,2},{2,4},{4,6},{6,8},{8,10},{10,12},{12,14},{1,3},{3,5},{5,7},{... | collective-permute-start | bytes 1572872 | tf_op jit(solution)/shard_map/ppermute | solution.py:456

commit v2 on v1

v2 whole, which is shorter than its diff:
```python
import functools
import math

import jax
import jax.numpy as jnp
from jax import lax
from jax.experimental import pallas as pl
from jax.experimental.pallas import tpu as pltpu
from jax.sharding import PartitionSpec as P

F32 = jnp.float32
BF16 = jnp.bfloat16
HEADS = 8
DIM = 128
TOK = 512
HALF = 256
WIDTH = 1024
MASKED = -1e9
SCALE = 1.0 / math.sqrt(DIM)
STEP = 2
COST = 1
VMEM_LIMIT = 60 * 1024 * 1024


def dot_nt(a, b):
    return lax.dot_general(a, b, (((1,), (1,)), ((), ())), preferred_element_type=F32)


def dot_nn(a, b):
    return lax.dot_general(a, b, (((1,), (0,)), ((), ())), preferred_element_type=F32)


def dot_tn(a, b):
    return lax.dot_general(a, b, (((0,), (0,)), ((), ())), preferred_element_type=F32)


def lowest_key(meta, first, rows):
    pos = first + lax.broadcasted_iota(jnp.int32, (rows, 1), 0)
    e0, e1, e2 = meta[0], meta[1], meta[2]
    start = jnp.where(pos >= e0, e0, 0)
    band = jnp.where(pos >= e0, meta[4], meta[3])
    start = jnp.where(pos >= e1, e1, start)
    band = jnp.where(pos >= e1, meta[5], band)
    start = jnp.where(pos >= e2, e2, start)
    band = jnp.where(pos >= e2, 0, band)
    return pos, jnp.maximum(start, pos - band + 1)


def mask_tile(meta, q_first, rows, k_first, cols, causal):
    pos, low = lowest_key(meta, q_first, rows)
    key = k_first + lax.broadcasted_iota(jnp.int32, (rows, cols), 1)
    ok = key >= low
    if causal:
        ok = ok & (key <= pos)
    return jnp.where(ok, 0.0, MASKED)


def bucket_cols(row):
    count = row.shape[1]
    return jnp.transpose(jnp.broadcast_to(row.astype(F32), (DIM, count))).astype(jnp.int32)


def lanes(rows):
    return lax.broadcasted_iota(jnp.int32, (rows, DIM), 1)


def one_hot(row):
    cols = bucket_cols(row)
    return jnp.where(cols == lanes(cols.shape[0]), 1.0, 0.0).astype(BF16)


def bias_rows(table_row, cols):
    gap = jnp.abs(cols - lanes(cols.shape[0]))
    spread = jnp.broadcast_to(table_row, gap.shape)
    return jnp.take_along_axis(spread, gap, axis=1).astype(BF16)


def bias_sum(mid, cols):
    lane = lanes(cols.shape[0])
    up, down = cols + lane, cols - lane
    above = jnp.take_along_axis(mid, up & (DIM - 1), axis=1)
    below = jnp.take_along_axis(mid, down & (DIM - 1), axis=1)
    both = jnp.where(up < DIM, above, 0.0) + jnp.where((down >= 0) & (lane > 0), below, 0.0)
    return jnp.sum(both, axis=0, keepdims=True) * 0.5


def attn_of(q_aug, k_aug, mask):
    half_score = dot_nt(q_aug, k_aug) * (0.5 * SCALE) + mask
    t = jnp.tanh(half_score)
    u = 1.0 + t
    return half_score * u, t, u


def back_of(q_aug, k_aug, mask, grad, value):
    attn, t, u = attn_of(q_aug, k_aug, mask)
    slope2 = u + attn * (1.0 - t)
    score_grad2 = (dot_nt(grad, value) * slope2).astype(BF16)
    return attn.astype(BF16), score_grad2


def cat(*parts):
    return jnp.concatenate(parts, axis=1)


def each_head(tab, base=0):
    for j in range(STEP):
        h = base + pl.program_id(0) * STEP + j
        yield h, slice(j * DIM, (j + 1) * DIM), tab[pl.ds(h, 1), :]


def own_forward_body(base, meta, q, k, v, bkt, tab, *rest):
    out, mask, hot, cols = rest[-4:]

    @pl.when(pl.program_id(0) == 0)
    def _():
        mask[...] = mask_tile(meta, meta[6], TOK, meta[6], TOK, True)
        hot[...] = one_hot(bkt[...])
        cols[...] = bucket_cols(bkt[...])

    for _, at, row in each_head(tab, base):
        q_aug = cat(q[:, at], bias_rows(row, cols[...]))
        k_aug = cat(k[:, at], hot[...])
        for i in range(2):
            lo, hi = i * HALF, (i + 1) * HALF
            attn, _, _ = attn_of(q_aug[lo:hi], k_aug[:hi], mask[lo:hi, :hi])
            out[lo:hi, at] = dot_nn(attn.astype(BF16), v[:hi, at])


def norm_of(mixed):
    mixed = mixed.astype(F32)
    center = jnp.mean(mixed, axis=1, keepdims=True)
    deviation = mixed - center
    variance = jnp.mean(deviation * deviation, axis=1, keepdims=True)
    inv_std = lax.rsqrt(variance + 1e-05)
    return deviation * inv_std, inv_std


def rows_body(
    meta, q, k, v, k_bkt, bkt, tab, partial, lifted, gate,
    gate_grad, gated, mixed_grad, total, mask, hot, cols,
):
    @pl.when(pl.program_id(0) == 0)
    def _():
        mask[...] = mask_tile(meta, meta[6], TOK, meta[6] - TOK, TOK, False)
        hot[...] = one_hot(k_bkt[...])
        cols[...] = bucket_cols(bkt[...])

    for h, at, row in each_head(tab):
        q_aug = cat(q[:, at], bias_rows(row, cols[...]))
        k_aug = cat(k[:, at], hot[...])
        column = pl.ds(pl.multiple_of(h * DIM, DIM), DIM)
        for i in range(2):
            lo, hi = i * HALF, (i + 1) * HALF
            attn, _, _ = attn_of(q_aug[lo:hi], k_aug[lo:], mask[lo:hi, lo:])
            total[lo:hi, column] = (
                partial[lo:hi, at] + dot_nn(attn.astype(BF16), v[lo:, at])
            ).astype(BF16)

    @pl.when(pl.program_id(0) == HEADS // STEP - 1)
    def _():
        @pl.loop(0, TOK // 64)
        def _(c):
            for i in range(2):
                rows = pl.ds(pl.multiple_of(c * 64 + i * 32, 32), 32)
                lift = lifted[rows, :]
                gate_f = gate[rows, :].astype(F32)
                normed, inv_std = norm_of(total[rows, :])
                gate_grad[rows, :] = (lift * normed).astype(BF16)
                gated[rows, :] = (normed * gate_f).astype(BF16)
                normed_grad = lift * gate_f
                mean_one = jnp.mean(normed_grad, axis=1, keepdims=True)
                mean_two = jnp.mean(normed_grad * normed, axis=1, keepdims=True)
                mixed_grad[rows, :] = (
                    inv_std * (normed_grad - mean_one - normed * mean_two)
                ).astype(BF16)


def lifted_body(meta, cot, users, owner, weight, lifted, total):
    @pl.when(pl.program_id(0) == 0)
    def _():
        count = users.shape[0]
        slot = lax.broadcasted_iota(jnp.int32, (DIM, count), 0)
        source = lax.broadcasted_iota(jnp.int32, (DIM, count), 1)
        pick = (owner[...] == meta[7] * 3 + (slot >> 3)) & ((source & 7) == (slot & 7)) & (slot < 24)
        rows = dot_nn(jnp.where(pick, 1.0, 0.0).astype(BF16), users[...]).astype(BF16)
        pos = meta[6] + lax.broadcasted_iota(jnp.int32, (TOK, 1), 0)
        lane = lanes(TOK)
        user = lane >> 3
        last = jnp.where(user == 0, meta[0], jnp.where(user == 1, meta[1], meta[2])) - 1
        hit = (pos == last) & (lane < 24)
        for c in range(WIDTH // DIM):
            at = slice(c * DIM, (c + 1) * DIM)
            hits = jnp.where(hit & ((lane & 7) == c), 1.0, 0.0).astype(BF16)
            total[:, at] = (cot[:, at].astype(F32) + dot_nn(hits, rows)).astype(BF16)

    lifted[...] = dot_nt(total[...], weight[...])


def weight_body(meta, gated, total, keep, send):
    part = dot_tn(gated[...], total[...])
    part = part.reshape(4, 2, 32, WIDTH)

    @pl.when(meta[8] == 0)
    def _():
        keep[...] = part[:, 0]
        send[...] = part[:, 1].astype(BF16)

    @pl.when(meta[8] == 1)
    def _():
        keep[...] = part[:, 1]
        send[...] = part[:, 0].astype(BF16)


def own_backward_body(
    meta, q, k, v, kh, vh, kh_bkt, bkt, tab, grad,
    dq, dk, dv, bias, mask, mask_h, hot, hot_h, cols,
):
    @pl.when(pl.program_id(0) == 0)
    def _():
        mask[...] = mask_tile(meta, meta[6], TOK, meta[6], TOK, True)
        mask_h[...] = mask_tile(meta, meta[6], TOK, meta[6] - TOK, TOK, False)
        hot[...] = one_hot(bkt[...])
        hot_h[...] = one_hot(kh_bkt[...])
        cols[...] = bucket_cols(bkt[...])

    for h, at, row in each_head(tab):
        own_backward_head(
            q[:, at], k[:, at], v[:, at], kh[:, at], vh[:, at], row, grad[:, at],
            dq, dk, dv, bias, mask, mask_h, hot, hot_h, cols, h, at,
        )


def own_backward_head(
    q, k, v, kh, vh, row, grad, dq, dk, dv, bias, mask, mask_h, hot, hot_h, cols, h, at
):
    q_aug = cat(q, bias_rows(row, cols[...]))
    k_aug = cat(k, hot[...])
    kh_aug = cat(kh, hot_h[...])
    ge, gl = grad[:HALF], grad[HALF:]
    attn, sg = back_of(q_aug[:HALF], k_aug[:HALF], mask[:HALF, :HALF], ge, v[:HALF])
    early = dot_nn(sg, k_aug[:HALF])
    dk[:HALF, at] = dot_tn(sg, q[:HALF])
    dv[:HALF, at] = dot_tn(attn, ge)
    _, sg = back_of(q_aug[:HALF], kh_aug, mask_h[:HALF, :], ge, vh)
    early = early + dot_nn(sg, kh_aug)
    attn, sg = back_of(q_aug[HALF:], k_aug, mask[HALF:, :], gl, v)
    late = dot_nn(sg, k_aug)
    more_k = dot_tn(sg, q[HALF:])
    more_v = dot_tn(attn, gl)
    dk[:HALF, at] += more_k[:HALF]
    dv[:HALF, at] += more_v[:HALF]
    dk[HALF:, at] = more_k[HALF:]
    dv[HALF:, at] = more_v[HALF:]
    _, sg = back_of(q_aug[HALF:], kh_aug[HALF:], mask_h[HALF:, HALF:], gl, vh[HALF:])
    late = late + dot_nn(sg, kh_aug[HALF:])
    dq[:HALF, at] = (early[:, :DIM] * (0.5 * SCALE)).astype(BF16)
    dq[HALF:, at] = (late[:, :DIM] * (0.5 * SCALE)).astype(BF16)
    bias[pl.ds(h, 1), :] = bias_sum(early[:, DIM:], cols[:HALF, :]) + bias_sum(late[:, DIM:], cols[HALF:, :])


def sent_backward_body(
    base, meta, qs, q_bkt, grad, k, v, bkt, tab, dk_own, dv_own, *rest
):
    dk, dv, mask, mask_l, hot, cols = rest[-6:]

    @pl.when(pl.program_id(0) == 0)
    def _():
        mask[...] = mask_tile(meta, meta[6] + TOK, HALF, meta[6], TOK, False)
        mask_l[...] = mask_tile(meta, meta[6] + TOK + HALF, HALF, meta[6] + HALF, HALF, False)
        hot[...] = one_hot(bkt[...])
        cols[...] = bucket_cols(q_bkt[...])

    for _, at, row in each_head(tab, base):
        added = bias_rows(row, cols[...])
        k_aug = cat(k[:, at], hot[...])
        ge, gl = grad[:HALF, at], grad[HALF:, at]
        qe, ql = qs[:HALF, at], qs[HALF:, at]
        attn, sg = back_of(cat(qe, added[:HALF]), k_aug, mask[...], ge, v[:, at])
        sum_k = dk_own[:, at] + dot_tn(sg, qe)
        sum_v = dv_own[:, at] + dot_tn(attn, ge)
        attn, sg = back_of(cat(ql, added[HALF:]), k_aug[HALF:], mask_l[...], gl, v[HALF:, at])
        dk[:HALF, at] = (sum_k[:HALF] * (0.5 * SCALE)).astype(BF16)
        dv[:HALF, at] = sum_v[:HALF].astype(BF16)
        dk[HALF:, at] = ((sum_k[HALF:] + dot_tn(sg, ql)) * (0.5 * SCALE)).astype(BF16)
        dv[HALF:, at] = (sum_v[HALF:] + dot_tn(attn, gl)).astype(BF16)


SMEM = pl.BlockSpec(memory_space=pltpu.SMEM)


def heads_of(rows, at=0):
    return pl.BlockSpec((rows, STEP * DIM), lambda h: (at, h))


def whole(*shape):
    return pl.BlockSpec(shape, lambda h: (0,) * len(shape))


def shape_of(rows, kind, cols=WIDTH):
    return jax.ShapeDtypeStruct((rows, cols), kind)


def call(body, name, grid, in_specs, out_specs, out_shape, scratch=(), aliases=None, flops=0, moved=0):
    return pl.pallas_call(
        body,
        name=name,
        grid=grid,
        in_specs=in_specs,
        out_specs=out_specs,
        out_shape=out_shape,
        scratch_shapes=list(scratch),
        input_output_aliases=aliases or {},
        cost_estimate=pl.CostEstimate(flops=flops // COST, bytes_accessed=moved // COST, transcendentals=0),
        compiler_params=pltpu.CompilerParams(vmem_limit_bytes=VMEM_LIMIT),
    )


def on_device(
    query_rows, key_rows, value_rows, gate_rows, out_grad, out_weight,
    time_bias, time_bucket, lengths, band_width, user_grad, user_owner,
):
    q, k, v = query_rows[0], key_rows[0], value_rows[0]
    gate, cot = gate_rows[0], out_grad[0]
    bkt = time_bucket
    ctx = lax.axis_index("ctx")
    rank = lax.axis_index("rank")
    n_ctx = lax.axis_size("ctx")
    n_dp = lax.axis_size("dp")
    section = lax.axis_index("dp") * lax.axis_size("rank") + rank
    ends = jnp.cumsum(lengths[0])
    first = ctx * TOK
    meta = jnp.concatenate(
        [ends, band_width[0], jnp.stack([first, section, rank])]
    ).astype(jnp.int32)
    tab = time_bias.astype(F32) * math.sqrt(DIM)
    up = [(i, i + 1) for i in range(n_ctx - 1)]
    down = [(i + 1, i) for i in range(n_ctx - 1)]

    k_came = lax.ppermute(k, "ctx", up)
    v_came = lax.ppermute(v, "ctx", up)
    q_came = lax.ppermute(q, "ctx", down)
    bkt_before = lax.ppermute(bkt, "ctx", up)
    bkt_after = lax.ppermute(bkt, "ctx", down)
    owner = jnp.pad(
        jnp.repeat(user_owner.reshape(-1, 3), 8, axis=1), ((0, 0), (0, 8)), constant_values=-1
    ).reshape(1, WIDTH)

    col = pltpu.VMEM((TOK, DIM), jnp.int32)
    hot = pltpu.VMEM((TOK, DIM), BF16)

    own_half = functools.partial(
        call, grid=(HEADS // STEP // 2,), out_shape=shape_of(TOK, F32),
        scratch=[pltpu.VMEM((TOK, TOK), F32), hot, col], flops=2_000_000_000, moved=3 << 20,
    )
    shift = HEADS // STEP // 2
    lower = pl.BlockSpec((TOK, STEP * DIM), lambda h: (0, h))
    upper = pl.BlockSpec((TOK, STEP * DIM), lambda h: (0, h + shift))
    own_out = own_half(
        functools.partial(own_forward_body, 0), "own_forward_low",
        in_specs=[SMEM, lower, lower, lower, whole(1, TOK), whole(HEADS, DIM)], out_specs=lower,
    )(meta, q, k, v, bkt, tab)

    pieces = jnp.pad(user_grad.reshape(24, DIM), ((0, 8), (0, 0)))
    half_weight = lax.dynamic_slice_in_dim(out_weight, rank * 32, 32)
    shared = jnp.concatenate([half_weight, pieces], axis=1)
    weight = lax.all_to_all(
        jnp.broadcast_to(shared[None], (2 * n_dp, 32, WIDTH + DIM)), ("dp", "rank"), 0, 0, tiled=True
    ).reshape(WIDTH, WIDTH + DIM)

    own_out = own_half(
        functools.partial(own_forward_body, HEADS // 2), "own_forward_high",
        in_specs=[SMEM, upper, upper, upper, whole(1, TOK), whole(HEADS, DIM),
                  pl.BlockSpec(memory_space=pl.ANY)],
        out_specs=upper, aliases={6: 0},
    )(meta, q, k, v, bkt, tab, own_out)

    lifted, total = call(
        lifted_body, "lifted", (4,),
        [SMEM, whole(TOK, WIDTH), pl.BlockSpec((WIDTH, DIM), lambda h: (0, WIDTH // DIM)),
         whole(1, WIDTH), pl.BlockSpec((HALF, WIDTH), lambda h: (h, 0))],
        (pl.BlockSpec((TOK, HALF), lambda h: (0, h)), whole(TOK, WIDTH)),
        (shape_of(TOK, F32), shape_of(TOK, BF16)),
        flops=1_200_000_000, moved=6 << 20,
    )(meta, cot, weight, owner, weight)

    meta_rows, q_came, bkt_after = lax.optimization_barrier((meta, q_came, bkt_after))
    gate_grad, gated, grad = call(
        rows_body, "rows", (HEADS // STEP,),
        [SMEM, heads_of(TOK), heads_of(TOK), heads_of(TOK), whole(1, TOK), whole(1, TOK),
         whole(HEADS, DIM), heads_of(TOK), whole(TOK, WIDTH), whole(TOK, WIDTH)],
        (whole(TOK, WIDTH),) * 3,
        (shape_of(TOK, BF16),) * 3,
        [pltpu.VMEM((TOK, WIDTH), BF16), pltpu.VMEM((TOK, TOK), F32), hot, col],
        flops=2_000_000_000, moved=10 << 20,
    )(meta_rows, q, k_came, v_came, bkt_before, bkt, tab, own_out, lifted, gate)
    grad_came = lax.ppermute(grad, "ctx", down)

    cut = pl.BlockSpec((TOK, HALF), lambda h: (0, h))
    piece = pl.BlockSpec((4, 32, WIDTH), lambda h: (h, 0, 0))
    keep, send = call(
        weight_body, "weight_part", (4,),
        [SMEM, cut, whole(TOK, WIDTH)],
        (piece, piece),
        (jax.ShapeDtypeStruct((16, 32, WIDTH), F32), jax.ShapeDtypeStruct((16, 32, WIDTH), BF16)),
        flops=1_100_000_000, moved=6 << 20,
    )(meta, gated, total)
    other = lax.ppermute(send, "rank", [(0, 1), (1, 0)])
    pair = (keep + other.astype(F32)).astype(BF16)
    rows = lax.all_to_all(pair, "dp", 0, 0, tiled=True)
    meta_own, _ = lax.optimization_barrier((meta, pair))
    passed = pl.BlockSpec(memory_space=pl.ANY)

    dq, dk_own, dv_own, bias = call(
        own_backward_body, "own_backward", (HEADS // STEP,),
        [SMEM] + [heads_of(TOK)] * 5 + [whole(1, TOK), whole(1, TOK), whole(HEADS, DIM), heads_of(TOK)],
        (heads_of(TOK), heads_of(TOK), heads_of(TOK), whole(HEADS, DIM)),
        (shape_of(TOK, BF16), shape_of(TOK, F32), shape_of(TOK, F32), shape_of(HEADS, F32, DIM)),
        [pltpu.VMEM((TOK, TOK), F32), pltpu.VMEM((TOK, TOK), F32), hot, hot, col],
        flops=10_000_000_000, moved=12 << 20,
    )(meta_own, q, k, v, k_came, v_came, bkt_before, bkt, tab, grad)

    spread = jnp.broadcast_to(bias[None, :, None], (n_dp, n_ctx, 2, DIM)).reshape(-1, DIM)
    rows, spread, grad_came = lax.optimization_barrier((rows, spread, grad_came))
    bias_all = lax.all_to_all(spread, ("dp", "ctx", "rank"), 0, 0, tiled=True)
    rows = jnp.sum(rows.astype(F32), axis=0)
    def sent_half(at, meta, *done):
        cols = functools.partial(pl.BlockSpec, index_map=lambda h: (0, h + at))
        out = cols((TOK, STEP * DIM))
        return call(
            functools.partial(sent_backward_body, at * STEP), "sent_backward", (HEADS // STEP // 2,),
            [SMEM, out, whole(1, TOK), out, out, out, whole(1, TOK), whole(HEADS, DIM), out, out]
            + [passed] * len(done),
            (out, out),
            (shape_of(TOK, BF16), shape_of(TOK, BF16)),
            [pltpu.VMEM((HALF, TOK), F32), pltpu.VMEM((HALF, HALF), F32), hot, col],
            aliases={10: 0, 11: 1} if done else None,
            flops=2_000_000_000, moved=5 << 20,
        )(meta, q_came, bkt_after, grad_came, k, v, bkt, tab, dk_own, dv_own, *done)

    def add_swap(rows, bit):
        return rows + lax.ppermute(rows, "ctx", [(i, i ^ bit) for i in range(n_ctx)])

    rows, meta_back = lax.optimization_barrier((rows, meta))
    done = sent_half(0, meta_back)
    rows = add_swap(rows, 1)
    rows, meta_back, *done = lax.optimization_barrier((rows, meta, *done))
    dk, dv = sent_half(HEADS // STEP // 2, meta_back, *done)
    rows = add_swap(rows, 2)
    rows, dk, dv = lax.optimization_barrier((rows, dk, dv))
    rows = add_swap(rows, 4)
    rows, bias_all = lax.optimization_barrier((rows, bias_all))
    other_rows = lax.ppermute(rows, "rank", [(0, 1), (1, 0)])
    weight_grad = jnp.concatenate(
        [jnp.where(rank == 0, rows, other_rows), jnp.where(rank == 0, other_rows, rows)], axis=0
    )
    bias_grad = jnp.sum(bias_all, axis=0, keepdims=True)
    return (dq[None], dk[None], dv[None], gate_grad[None], weight_grad, bias_grad)


def solution(mesh):
    rows = P(("dp", "rank"), "ctx", None)
    users = P(("dp", "rank"), None)
    return jax.shard_map(
        on_device,
        mesh=mesh,
        in_specs=(
            rows, rows, rows, rows, rows, P("dp", None), P(), P(("dp", "rank"), "ctx"),
            users, users, users, P(),
        ),
        out_specs=(rows, rows, rows, rows, P("dp", None), P("ctx", None)),
        check_vma=False,
    )
```

time: 212 us -> 160 us (0.75)
  waiting for transfers between devices: 59.8 us -> 16.3 us
  blocking collectives: 17.3 us -> 0 us
  starting transfers between devices: 47.2 us -> 62.4 us
  Pallas kernels: 65.8 us -> 61.6 us
    ppermute x7 -> x10, waiting for transfers between devices: 48.4 us -> 15.1 us  [the longest x1 11.4 us: on_device(): bkt_before = lax.ppermute(bkt, 'ctx', up)]
    all_to_all x1 -> x0, blocking collectives: 17.3 us -> none  [on_device(): lax.all_to_all(jnp.broadcast_to(user_grad[None], (2 * n_dp,) + user_grad....]
    ppermute x7 -> x10, starting transfers between devices: 16.4 us -> 29.1 us  [the longest x3 8.89 us: add_swap(): lax.ppermute(rows, 'ctx', [(i, i ^ bit) for i in range(n_ctx)])]
    all_to_all x4 -> x3, waiting for transfers between devices: 11.4 us -> 0.01 us  [the longest x1 0.01 us: on_device(): lax.all_to_all(jnp.broadcast_to(shared[None], (2 * n_dp, 32, WIDTH + DIM)...]
    pallas_call x9 -> x8, Pallas kernels: 65.8 us -> 61.6 us  [the longest x1 16.6 us: on_device(): call(own_backward_body, 'own_backward', (HEADS // STEP,), [SMEM] + [heads...]
    unnamed x38 -> x15, local copies, waits for them, and re-layouts: 6.36 us -> 2.36 us
    reshape x1 -> x5, local copies, waits for them, and re-layouts: 0.17 us -> 4.14 us  [the longest x2 1.41 us: on_device(): user_owner.reshape(-1, 3)]
    broadcast_in_dim x3 -> x1, local copies, waits for them, and re-layouts: 4.42 us -> 1.58 us  [on_device(): jnp.broadcast_to(shared[None], (2 * n_dp, 32, WIDTH + DIM))]
  transfers between devices with their start and end apart: 12 -> 14, of which waited for: 4 -> 4; matrix products, arithmetic and copies ran while one was open for 3% -> 7% of each run, Pallas kernels for 28% -> 28%
where the time goes in v2:
time: 160 us; the launch traced here: 159 us
  starting transfers between devices  62.4 us (39%)
  Pallas kernels  61.6 us (38%)
  waiting for transfers between devices  16.3 us (10%)
  local copies, waits for them, and re-layouts  11.4 us (7%)
  other arithmetic  6.45 us (4%)
    all_to_all x1, starting transfers between devices, on_device(): bias_all = lax.all_to_all(spread, ('dp', 'ctx', 'rank'), 0, 0, tiled=True)  16.8 us
    pallas_call x1, Pallas kernels, on_device(): call(own_backward_body, 'own_backward', (HEADS // STEP,), [SMEM] + [heads...  16.6 us
    pallas_call x2, Pallas kernels, sent_half(): call(functools.partial(sent_backward_body, at * STEP), 'sent_backward', (...  13.4 us
    pallas_call x1, Pallas kernels, on_device(): call(rows_body, 'rows', (HEADS // STEP,), [SMEM, heads_of(TOK), heads_of(...  11.5 us
    ppermute x1, waiting for transfers between devices, on_device(): bkt_before = lax.ppermute(bkt, 'ctx', up)  11.4 us
    ppermute x3, starting transfers between devices, add_swap(): lax.ppermute(rows, 'ctx', [(i, i ^ bit) for i in range(n_ctx)])  8.89 us
    all_to_all x1, starting transfers between devices, on_device(): lax.all_to_all(jnp.broadcast_to(shared[None], (2 * n_dp, 32, WIDTH + DIM)...  8.72 us
    all_to_all x1, starting transfers between devices, on_device(): rows = lax.all_to_all(pair, 'dp', 0, 0, tiled=True)  6.7 us
  transfers between devices with their start and end apart: 14, of which 4 were waited for; matrix products, arithmetic and copies ran while one was open for 7% of the time, Pallas kernels for 28%

profile of v2, /device:TPU:1, one launch (start us, length us, event | category | flops | bytes accessed | tf_op | source)
XLA Modules:
  0.0 159.1 jit_solution(9902655925093441048)
XLA Ops:
  0.6 0.0 copy-start
  0.7 0.7 reshape.63
  1.4 0.2 copy-done
  1.6 1.6 broadcast_in_dim.30
  3.2 0.0 copy-start.2
  3.2 0.0 copy-start.6
  3.2 8.7 %all-to-all-start = ((bf16[32,32,1152]{2,1,0:T(8,128)(2,1)}), bf16[32,32,1152]{2,1,0:T(8,128)(2,1)S(1)}, u32[]{:S(2)}, u32[]{:S(2)}) async-start(bf16[32,32,1152]{2,1,0:T(8,128)(2,1)} %broadcast_in_dim.30), calls=%async_computation | async-start | bytes 4718592 | tf_op jit(solution)/shard_map/all_to_all | solution.py:366
  11.9 1.3 collective-permute-start
  13.2 0.0 copy-done.2
  13.2 5.1 %collective-permute-start.2 = (bf16[512,1024]{1,0:T(8,128)(2,1)S(1)}, bf16[512,1024]{1,0:T(8,128)(2,1)}, u32[]{:S(2)}, u32[]{:S(2)}) collective-permute-start(bf16[512,1024]{1,0:T(8,128)(2,1)S(1)} %bitcast.29), channel_id=1, source_target_pairs={{0,2},{2,4},{4,6},{6,8},{8,10},{10,12},{12,14},{1,3},{3,5},{5,7},{... | collective-permute-start | bytes 3145736 | tf_op jit(solution)/shard_map/ppermute | solution.py:339
  18.3 3.6 %collective-permute-start.3 = (bf16[512,1024]{1,0:T(8,128)(2,1)}, bf16[512,1024]{1,0:T(8,128)(2,1)}, u32[]{:S(2)}, u32[]{:S(2)}) collective-permute-start(bf16[512,1024]{1,0:T(8,128)(2,1)} %bitcast.30), channel_id=1, source_target_pairs={{0,2},{2,4},{4,6},{6,8},{8,10},{10,12},{12,14},{1,3},{3,5},{5,7},{... | collective-permute-start | bytes 3145736 | tf_op jit(solution)/shard_map/ppermute | solution.py:340
  21.9 3.2 %collective-permute-start.4 = (s32[1,512]{1,0:T(1,128)}, s32[1,512]{1,0:T(1,128)}, u32[]{:S(2)}, u32[]{:S(2)}) collective-permute-start(s32[1,512]{1,0:T(1,128)} %bkt.11), channel_id=1, source_target_pairs={{0,2},{2,4},{4,6},{6,8},{8,10},{10,12},{12,14},{1,3},{3,5},{5,7},{... | collective-permute-start | bytes 6152 | tf_op jit(solution)/shard_map/ppermute | solution.py:342
  25.1 1.3 collective-permute-start.1
  26.4 0.0 copy-done.6
  26.4 0.7 reduce-window.9
  27.1 0.7 reshape.65
  27.8 0.7 copy.23
  28.5 1.3 concatenate.9.meta
  29.8 1.3 convert_multiply_fusion.tab
  31.0 4.5 %own_forward_low.1.rest_0_ = f32[512,1024]{1,0:T(8,128)} custom-call(s32[9]{0:T(128)} %concatenate.9.meta, bf16[512,1024]{1,0:T(8,128)(2,1)} %bitcast.38, bf16[512,1024]{1,0:T(8,128)(2,1)} %bitcast.24, bf16[512,1024]{1,0:T(8,128)(2,1)} %bitcast.31, s32[1,512]{1,0:T(1,128)} %bkt.11, f32[8,128]{1,0:T(8,128)} %convert_multiply_fusion.tab), custom_call_target="tpu_custom_call" | custom-call | flops 2000000000 | bytes 3145728 | tf_op jit(solution)/shard_map/own_forward_low/pallas_call | solution.py:358
  35.6 0.0 copy-done.4
  35.6 0.6 broadcast_bitcast_fusion
  36.2 4.5 %own_forward_high.1.partial = f32[512,1024]{1,0:T(8,128)} custom-call(s32[9]{0:T(128)} %concatenate.9.meta, bf16[512,1024]{1,0:T(8,128)(2,1)} %bitcast.39, bf16[512,1024]{1,0:T(8,128)(2,1)} %bitcast.25, bf16[512,1024]{1,0:T(8,128)(2,1)} %bitcast.32, s32[1,512]{1,0:T(1,128)} %bkt.11, ...), custom_call_target="tpu_custom_call", output_to_operand_aliasing={{}: (6, {})} | custom-call | flops 2000000000 | bytes 3145728 | tf_op jit(solution)/shard_map/own_forward_high/pallas_call | solution.py:370
  40.7 0.8 copy.25
  41.5 0.6 pad.9.clone
  42.1 1.4 reshape.67.owner
  43.5 0.0 collective-permute-done.1.q_bkt
  43.5 0.0 collective-permute-done.qs
  43.5 0.0 all-to-all-done
  43.5 0.0 copy-start.1
  43.5 1.4 copy-done.1
  44.9 5.9 %lifted.1 = (f32[512,1024]{1,0:T(8,128)}, bf16[512,1024]{1,0:T(8,128)(2,1)}) custom-call(s32[9]{0:T(128)} %concatenate.9.meta, bf16[512,1024]{1,0:T(8,128)(2,1)} %bitcast.44, bf16[1024,1152]{1,0:T(8,128)(2,1)} %bitcast.22, s32[1,1024]{1,0:T(1,128)} %reshape.67.owner, bf16[1024,1152]{1,0:T(8,128)(2,1)} %bitcast.23), custom_call_target="tpu_custom_call" | custom-call | flops 1200000000 | bytes 6291456 | tf_op jit(solution)/shard_map/lifted/pallas_call | solution.py:377
  50.8 11.4 %collective-permute-done.4.k_bkt.kh_bkt = s32[1,512]{1,0:T(1,128)} collective-permute-done((s32[1,512]{1,0:T(1,128)}, s32[1,512]{1,0:T(1,128)}, u32[]{:S(2)}, u32[]{:S(2)}) %collective-permute-start.4) | collective-permute-done | bytes 2080 | tf_op jit(solution)/shard_map/ppermute | solution.py:342
  62.2 0.0 collective-permute-done.2.k.kh
  62.2 0.0 collective-permute-done.3.v.vh
  62.2 11.5 %rows.1 = (bf16[512,1024]{1,0:T(8,128)(2,1)}, bf16[512,1024]{1,0:T(8,128)(2,1)}, bf16[512,1024]{1,0:T(8,128)(2,1)}) custom-call(s32[9]{0:T(128)} %concatenate.9.meta, bf16[512,1024]{1,0:T(8,128)(2,1)} %bitcast.40, bf16[512,1024]{1,0:T(8,128)(2,1)} %collective-permute-done.2.k.kh, bf16[512,1024]{1,0:T(8,128)(2,1)} %collective-permute-done.3.v.vh, ...), custom_call_target="tpu_custom_call" | custom-call | flops 2000000000 | bytes 10485760 | tf_op jit(solution)/shard_map/rows/pallas_call | solution.py:387
  73.6 5.2 %weight_part.1 = (f32[16,32,1024]{2,1,0:T(8,128)}, bf16[16,32,1024]{2,1,0:T(8,128)(2,1)}) custom-call(s32[9]{0:T(128)} %concatenate.9.meta, bf16[512,1024]{1,0:T(8,128)(2,1)} %get-tuple-element.41.gated, bf16[512,1024]{1,0:T(8,128)(2,1)} %get-tuple-element.42.total), custom_call_target="tpu_custom_call" | custom-call | flops 1100000000 | bytes 6291456 | tf_op jit(solution)/shard_map/weight_part/pallas_call | solution.py:400
  78.8 1.1 collective-permute-start.5
  80.0 0.0 copy-done.5
  80.0 1.3 collective-permute-start.6
  81.2 1.2 collective-permute-done.5
  82.5 3.0 %add_convert_fusion = bf16[16,32,1024]{2,1,0:T(8,128)(2,1)} fusion(f32[16,32,1024]{2,1,0:T(8,128)} %get-tuple-element.43, bf16[16,32,1024]{2,1,0:T(8,128)(2,1)S(1)} %collective-permute-done.5), kind=kLoop, calls=%fused_computation.1 | loop fusion | flops 1572864 | bytes 4194304 | tf_op jit(solution)/shard_map/convert_element_type | solution.py:408
  85.4 6.7 %all-to-all-start.1 = ((bf16[16,32,1024]{2,1,0:T(8,128)(2,1)}), bf16[16,32,1024]{2,1,0:T(8,128)(2,1)S(1)}, u32[]{:S(2)}, u32[]{:S(2)}) async-start(bf16[16,32,1024]{2,1,0:T(8,128)(2,1)} %add_convert_fusion), calls=%async_computation.1 | async-start | bytes 2097152 | tf_op jit(solution)/shard_map/all_to_all | solution.py:409
  92.1 16.6 %own_backward.1 = (bf16[512,1024]{1,0:T(8,128)(2,1)}, f32[512,1024]{1,0:T(8,128)}, f32[512,1024]{1,0:T(8,128)}, f32[8,128]{1,0:T(8,128)}) custom-call(s32[9]{0:T(128)} %concatenate.9.meta, bf16[512,1024]{1,0:T(8,128)(2,1)} %bitcast.41, bf16[512,1024]{1,0:T(8,128)(2,1)} %bitcast.26, bf16[512,1024]{1,0:T(8,128)(2,1)} %bitcast.33, ...), custom_call_target="tpu_custom_call" | custom-call | flops 10000000000 | bytes 12582912 | tf_op jit(solution)/shard_map/own_backward/pallas_call | solution.py:413
  108.7 0.0 collective-permute-done.6.grad
  108.7 0.0 copy-start.3
  108.7 0.0 all-to-all-done.1
  108.7 1.4 broadcast_in_dim.33
  110.1 0.2 convert_reduce_fusion
  110.3 16.8 %all-to-all-start.2 = ((f32[256,1,128]{2,1,0:T(1,128)}), f32[256,1,128]{2,1,0:T(1,128)S(1)}, u32[]{:S(2)}, u32[]{:S(2)}) async-start(f32[256,1,128]{2,1,0:T(1,128)} %bitcast.18), calls=%async_computation.2 | async-start | bytes 262144 | tf_op jit(solution)/shard_map/all_to_all | solution.py:424
  127.1 1.6 %collective-permute-start.7 = (f32[32,1024]{1,0:T(8,128)S(1)}, f32[32,1024]{1,0:T(8,128)S(1)}, u32[]{:S(2)}, u32[]{:S(2)}) collective-permute-start(f32[32,1024]{1,0:T(8,128)S(1)} %convert_reduce_fusion), channel_id=1, source_target_pairs={{0,2},{2,0},{4,6},{6,4},{8,10},{10,8},{12,14},{14,12},{1,3},{3,1},... | collective-permute-start | bytes 393224 | tf_op jit(solution)/shard_map/ppermute | solution.py:441
  128.7 0.0 copy-done.3
  128.7 6.8 %sent_backward.2 = (bf16[512,1024]{1,0:T(8,128)(2,1)}, bf16[512,1024]{1,0:T(8,128)(2,1)}) custom-call(s32[9]{0:T(128)} %concatenate.9.meta, bf16[512,1024]{1,0:T(8,128)(2,1)} %collective-permute-done.qs, s32[1,512]{1,0:T(1,128)} %collective-permute-done.1.q_bkt, bf16[512,1024]{1,0:T(8,128)(2,1)} %copy-done.3, bf16[512,1024]{1,0:T(8,128)(2,1)} %bitcast.27, ...), custom_call_target="tpu_custom_call" | custom-call | flops 2000000000 | bytes 5242880 | tf_op jit(solution)/shard_map/sent_backward/pallas_call | solution.py:429
  135.5 0.0 collective-permute-done.7
  135.6 2.7 %collective-permute-start.8 = (f32[32,1024]{1,0:T(8,128)S(1)}, f32[32,1024]{1,0:T(8,128)S(1)}, u32[]{:S(2)}, u32[]{:S(2)}) collective-permute-start(f32[32,1024]{1,0:T(8,128)S(1)} %add.25), channel_id=1, source_target_pairs={{0,4},{2,6},{4,0},{6,2},{8,12},{10,14},{12,8},{14,10},{1,5},{3,7},... | collective-permute-start | bytes 393224 | tf_op jit(solution)/shard_map/ppermute | solution.py:441
  138.3 6.6 %sent_backward.3 = (bf16[512,1024]{1,0:T(8,128)(2,1)}, bf16[512,1024]{1,0:T(8,128)(2,1)}) custom-call(s32[9]{0:T(128)} %concatenate.9.meta, bf16[512,1024]{1,0:T(8,128)(2,1)} %collective-permute-done.qs, s32[1,512]{1,0:T(1,128)} %collective-permute-done.1.q_bkt, bf16[512,1024]{1,0:T(8,128)(2,1)} %copy-done.3, ...), custom_call_target="tpu_custom_call", output_to_operand_aliasing={{0}: (10, {}), {1}: (11, {})} | custom-call | flops 2000000000 | bytes 5242880 | tf_op jit(solution)/shard_map/sent_backward/pallas_call | solution.py:429
  144.9 0.0 collective-permute-done.8
  144.9 4.6 %collective-permute-start.9 = (f32[32,1024]{1,0:T(8,128)S(1)}, f32[32,1024]{1,0:T(8,128)S(1)}, u32[]{:S(2)}, u32[]{:S(2)}) collective-permute-start(f32[32,1024]{1,0:T(8,128)S(1)} %add.26), channel_id=1, source_target_pairs={{0,8},{2,10},{4,12},{6,14},{8,0},{10,2},{12,4},{14,6},{1,9},{3,11}... | collective-permute-start | bytes 393224 | tf_op jit(solution)/shard_map/ppermute | solution.py:441
  149.5 3.3 %collective-permute-done.9 = f32[32,1024]{1,0:T(8,128)S(1)} collective-permute-done((f32[32,1024]{1,0:T(8,128)S(1)}, f32[32,1024]{1,0:T(8,128)S(1)}, u32[]{:S(2)}, u32[]{:S(2)}) %collective-permute-start.9) | collective-permute-done | bytes 131104 | tf_op jit(solution)/shard_map/ppermute | solution.py:441
  152.8 0.0 all-to-all-done.2
  152.9 4.5 %collective-permute-start.10 = (f32[32,1024]{1,0:T(8,128)S(1)}, f32[32,1024]{1,0:T(8,128)S(1)}, u32[]{:S(2)}, u32[]{:S(2)}) collective-permute-start(f32[32,1024]{1,0:T(8,128)S(1)} %add.27), channel_id=1, source_target_pairs={{0,1},{1,0},{2,3},{3,2},{4,5},{5,4},{6,7},{7,6},{8,9},{9,8},{10,11... | collective-permute-start | bytes 393224 | tf_op jit(solution)/shard_map/ppermute | solution.py:452
  157.3 0.6 reduce_sum.19
  157.9 0.4 collective-permute-done.10
  158.4 0.7 pad_maximum_fusion
  (8 shorter events, 0.1 us)
Async XLA Ops:
  0.6 0.9 copy-start
  3.2 10.0 %copy-start.2 = (bf16[1,512,1024]{2,1,0:T(8,128)(2,1)S(1)}, bf16[1,512,1024]{2,1,0:T(8,128)(2,1)}, u32[]{:S(2)}) copy-start(bf16[1,512,1024]{2,1,0:T(8,128)(2,1)} %param.13) | copy-start | bytes 3145732
  3.2 23.2 %copy-start.6 = (s32[1,3]{1,0:T(1,128)S(1)}, s32[1,3]{1,0:T(1,128)}, u32[]{:S(2)}) copy-start(s32[1,3]{1,0:T(1,128)} %param.20) | copy-start | bytes 40
  3.2 40.3 %all-to-all-start = ((bf16[32,32,1152]{2,1,0:T(8,128)(2,1)}), bf16[32,32,1152]{2,1,0:T(8,128)(2,1)S(1)}, u32[]{:S(2)}, u32[]{:S(2)}) async-start(bf16[32,32,1152]{2,1,0:T(8,128)(2,1)} %broadcast_in_dim.30), calls=%async_computation | async-start | bytes 4718592 | tf_op jit(solution)/shard_map/all_to_all | solution.py:366
  11.9 31.6 %collective-permute-start = (bf16[512,1024]{1,0:T(8,128)(2,1)}, bf16[512,1024]{1,0:T(8,128)(2,1)}, u32[]{:S(2)}, u32[]{:S(2)}) collective-permute-start(bf16[512,1024]{1,0:T(8,128)(2,1)} %bitcast.37), channel_id=1, source_target_pairs={{2,0},{4,2},{6,4},{8,6},{10,8},{12,10},{14,12},{3,1},{5,3},{7,5},{... | collective-permute-start | bytes 3145736 | tf_op jit(solution)/shard_map/ppermute | solution.py:341
  13.2 49.0 %collective-permute-start.2 = (bf16[512,1024]{1,0:T(8,128)(2,1)S(1)}, bf16[512,1024]{1,0:T(8,128)(2,1)}, u32[]{:S(2)}, u32[]{:S(2)}) collective-permute-start(bf16[512,1024]{1,0:T(8,128)(2,1)S(1)} %bitcast.29), channel_id=1, source_target_pairs={{0,2},{2,4},{4,6},{6,8},{8,10},{10,12},{12,14},{1,3},{3,5},{5,7},{... | collective-permute-start | bytes 3145736 | tf_op jit(solution)/shard_map/ppermute | solution.py:339
  18.3 43.8 %collective-permute-start.3 = (bf16[512,1024]{1,0:T(8,128)(2,1)}, bf16[512,1024]{1,0:T(8,128)(2,1)}, u32[]{:S(2)}, u32[]{:S(2)}) collective-permute-start(bf16[512,1024]{1,0:T(8,128)(2,1)} %bitcast.30), channel_id=1, source_target_pairs={{0,2},{2,4},{4,6},{6,8},{8,10},{10,12},{12,14},{1,3},{3,5},{5,7},{... | collective-permute-start | bytes 3145736 | tf_op jit(solution)/shard_map/ppermute | solution.py:340
  21.9 40.2 %collective-permute-start.4 = (s32[1,512]{1,0:T(1,128)}, s32[1,512]{1,0:T(1,128)}, u32[]{:S(2)}, u32[]{:S(2)}) collective-permute-start(s32[1,512]{1,0:T(1,128)} %bkt.11), channel_id=1, source_target_pairs={{0,2},{2,4},{4,6},{6,8},{8,10},{10,12},{12,14},{1,3},{3,5},{5,7},{... | collective-permute-start | bytes 6152 | tf_op jit(solution)/shard_map/ppermute | solution.py:342
  25.1 18.4 %collective-permute-start.1 = (s32[1,512]{1,0:T(1,128)}, s32[1,512]{1,0:T(1,128)}, u32[]{:S(2)}, u32[]{:S(2)}) collective-permute-start(s32[1,512]{1,0:T(1,128)} %bkt.11), channel_id=1, source_target_pairs={{2,0},{4,2},{6,4},{8,6},{10,8},{12,10},{14,12},{3,1},{5,3},{7,5},{... | collective-permute-start | bytes 6152 | tf_op jit(solution)/shard_map/ppermute | solution.py:343
  31.0 4.5 %copy-start.4 = (s32[32,3]{0,1:T(4,128)S(1)}, s32[32,3]{0,1:T(4,128)}, u32[]{:S(2)}) copy-start(s32[32,3]{0,1:T(4,128)} %copy.23) | copy-start | bytes 1156
  43.5 1.4 copy-start.1
  73.6 6.3 %copy-start.5 = (bf16[512,1024]{1,0:T(8,128)(2,1)S(1)}, bf16[512,1024]{1,0:T(8,128)(2,1)}, u32[]{:S(2)}) copy-start(bf16[512,1024]{1,0:T(8,128)(2,1)} %get-tuple-element.46.grad) | copy-start | bytes 3145732
  78.8 3.6 %collective-permute-start.5 = (bf16[16,32,1024]{2,1,0:T(8,128)(2,1)}, bf16[16,32,1024]{2,1,0:T(8,128)(2,1)S(1)}, u32[]{:S(2)}, u32[]{:S(2)}) collective-permute-start(bf16[16,32,1024]{2,1,0:T(8,128)(2,1)} %get-tuple-element.44), channel_id=1, source_target_pairs={{0,1},{1,0},{2,3},{3,2},{4,5},{5,4},{6,7},{7,6},{8,9},{9,8},{10,11... | collective-permute-start | bytes 3145736 | tf_op jit(solution)/shard_map/ppermute | solution.py:407
  80.0 28.7 %collective-permute-start.6 = (bf16[512,1024]{1,0:T(8,128)(2,1)S(1)}, bf16[512,1024]{1,0:T(8,128)(2,1)S(1)}, u32[]{:S(2)}, u32[]{:S(2)}) collective-permute-start(bf16[512,1024]{1,0:T(8,128)(2,1)S(1)} %copy-done.5), channel_id=1, source_target_pairs={{2,0},{4,2},{6,4},{8,6},{10,8},{12,10},{14,12},{3,1},{5,3},{7,5},{... | collective-permute-start | bytes 3145736 | tf_op jit(solution)/shard_map/ppermute | solution.py:396
  85.4 23.3 %all-to-all-start.1 = ((bf16[16,32,1024]{2,1,0:T(8,128)(2,1)}), bf16[16,32,1024]{2,1,0:T(8,128)(2,1)S(1)}, u32[]{:S(2)}, u32[]{:S(2)}) async-start(bf16[16,32,1024]{2,1,0:T(8,128)(2,1)} %add_convert_fusion), calls=%async_computation.1 | async-start | bytes 2097152 | tf_op jit(solution)/shard_map/all_to_all | solution.py:409
  108.7 20.0 %copy-start.3 = (bf16[512,1024]{1,0:T(8,128)(2,1)}, bf16[512,1024]{1,0:T(8,128)(2,1)S(1)}, u32[]{:S(2)}) copy-start(bf16[512,1024]{1,0:T(8,128)(2,1)S(1)} %collective-permute-done.6.grad) | copy-start | bytes 3145732
  110.3 42.5 %all-to-all-start.2 = ((f32[256,1,128]{2,1,0:T(1,128)}), f32[256,1,128]{2,1,0:T(1,128)S(1)}, u32[]{:S(2)}, u32[]{:S(2)}) async-start(f32[256,1,128]{2,1,0:T(1,128)} %bitcast.18), calls=%async_computation.2 | async-start | bytes 262144 | tf_op jit(solution)/shard_map/all_to_all | solution.py:424
  127.1 8.4 %collective-permute-start.7 = (f32[32,1024]{1,0:T(8,128)S(1)}, f32[32,1024]{1,0:T(8,128)S(1)}, u32[]{:S(2)}, u32[]{:S(2)}) collective-permute-start(f32[32,1024]{1,0:T(8,128)S(1)} %convert_reduce_fusion), channel_id=1, source_target_pairs={{0,2},{2,0},{4,6},{6,4},{8,10},{10,8},{12,14},{14,12},{1,3},{3,1},... | collective-permute-start | bytes 393224 | tf_op jit(solution)/shard_map/ppermute | solution.py:441
  135.6 9.3 %collective-permute-start.8 = (f32[32,1024]{1,0:T(8,128)S(1)}, f32[32,1024]{1,0:T(8,128)S(1)}, u32[]{:S(2)}, u32[]{:S(2)}) collective-permute-start(f32[32,1024]{1,0:T(8,128)S(1)} %add.25), channel_id=1, source_target_pairs={{0,4},{2,6},{4,0},{6,2},{8,12},{10,14},{12,8},{14,10},{1,5},{3,7},... | collective-permute-start | bytes 393224 | tf_op jit(solution)/shard_map/ppermute | solution.py:441
  144.9 7.9 %collective-permute-start.9 = (f32[32,1024]{1,0:T(8,128)S(1)}, f32[32,1024]{1,0:T(8,128)S(1)}, u32[]{:S(2)}, u32[]{:S(2)}) collective-permute-start(f32[32,1024]{1,0:T(8,128)S(1)} %add.26), channel_id=1, source_target_pairs={{0,8},{2,10},{4,12},{6,14},{8,0},{10,2},{12,4},{14,6},{1,9},{3,11}... | collective-permute-start | bytes 393224 | tf_op jit(solution)/shard_map/ppermute | solution.py:441
  152.9 5.5 %collective-permute-start.10 = (f32[32,1024]{1,0:T(8,128)S(1)}, f32[32,1024]{1,0:T(8,128)S(1)}, u32[]{:S(2)}, u32[]{:S(2)}) collective-permute-start(f32[32,1024]{1,0:T(8,128)S(1)} %add.27), channel_id=1, source_target_pairs={{0,1},{1,0},{2,3},{3,2},{4,5},{5,4},{6,7},{7,6},{8,9},{9,8},{10,11... | collective-permute-start | bytes 393224 | tf_op jit(solution)/shard_map/ppermute | solution.py:452

commit v3 on v2

--- a/solution.py
+++ b/solution.py
@@ -15,6 +15,7 @@
 TOK = 512
 HALF = 256
 WIDTH = 1024
+PAD = 16
 MASKED = -1e9
 SCALE = 1.0 / math.sqrt(DIM)
 STEP = 2
@@ -34,8 +35,9 @@
     return lax.dot_general(a, b, (((0,), (0,)), ((), ())), preferred_element_type=F32)
 
 
-def lowest_key(meta, first, rows):
-    pos = first + lax.broadcasted_iota(jnp.int32, (rows, 1), 0)
+def lowest_key(meta, first, rows, axis=0):
+    shape = (rows, 1) if axis == 0 else (1, rows)
+    pos = first + lax.broadcasted_iota(jnp.int32, shape, axis)
     e0, e1, e2 = meta[0], meta[1], meta[2]
     start = jnp.where(pos >= e0, e0, 0)
     band = jnp.where(pos >= e0, meta[4], meta[3])
@@ -46,9 +48,11 @@
     return pos, jnp.maximum(start, pos - band + 1)
 
 
-def mask_tile(meta, q_first, rows, k_first, cols, causal):
-    pos, low = lowest_key(meta, q_first, rows)
-    key = k_first + lax.broadcasted_iota(jnp.int32, (rows, cols), 1)
+def mask_tile(meta, q_first, rows, k_first, cols, causal, turned=False):
+    axis = 1 if turned else 0
+    pos, low = lowest_key(meta, q_first, rows, axis)
+    shape = (cols, rows) if turned else (rows, cols)
+    key = k_first + lax.broadcasted_iota(jnp.int32, shape, 1 - axis)
     ok = key >= low
     if causal:
         ok = ok & (key <= pos)
@@ -142,7 +146,7 @@
     @pl.when(pl.program_id(0) == 0)
     def _():
         mask[...] = mask_tile(meta, meta[6], TOK, meta[6] - TOK, TOK, False)
-        hot[...] = one_hot(k_bkt[...])
+        hot[...] = one_hot(k_bkt[0:1, :])
         cols[...] = bucket_cols(bkt[...])
 
     for h, at, row in each_head(tab):
@@ -217,10 +221,10 @@
 ):
     @pl.when(pl.program_id(0) == 0)
     def _():
-        mask[...] = mask_tile(meta, meta[6], TOK, meta[6], TOK, True)
+        mask[...] = mask_tile(meta, meta[6], TOK, meta[6], TOK, True, True)
         mask_h[...] = mask_tile(meta, meta[6], TOK, meta[6] - TOK, TOK, False)
         hot[...] = one_hot(bkt[...])
-        hot_h[...] = one_hot(kh_bkt[...])
+        hot_h[...] = one_hot(kh_bkt[0:1, :])
         cols[...] = bucket_cols(bkt[...])
 
     for h, at, row in each_head(tab):
@@ -237,20 +241,17 @@
     k_aug = cat(k, hot[...])
     kh_aug = cat(kh, hot_h[...])
     ge, gl = grad[:HALF], grad[HALF:]
-    attn, sg = back_of(q_aug[:HALF], k_aug[:HALF], mask[:HALF, :HALF], ge, v[:HALF])
-    early = dot_nn(sg, k_aug[:HALF])
-    dk[:HALF, at] = dot_tn(sg, q[:HALF])
-    dv[:HALF, at] = dot_tn(attn, ge)
+    attn, sg = back_of(k_aug[:HALF], q_aug, mask[:HALF, :], v[:HALF], grad)
+    dk[:HALF, at] = dot_nn(sg, q)
+    dv[:HALF, at] = dot_nn(attn, grad)
+    own = dot_tn(sg, k_aug[:HALF])
+    early, late = own[:HALF], own[HALF:]
+    attn, sg = back_of(k_aug[HALF:], q_aug[HALF:], mask[HALF:, HALF:], v[HALF:], gl)
+    dk[HALF:, at] = dot_nn(sg, q[HALF:])
+    dv[HALF:, at] = dot_nn(attn, gl)
+    late = late + dot_tn(sg, k_aug[HALF:])
     _, sg = back_of(q_aug[:HALF], kh_aug, mask_h[:HALF, :], ge, vh)
     early = early + dot_nn(sg, kh_aug)
-    attn, sg = back_of(q_aug[HALF:], k_aug, mask[HALF:, :], gl, v)
-    late = dot_nn(sg, k_aug)
-    more_k = dot_tn(sg, q[HALF:])
-    more_v = dot_tn(attn, gl)
-    dk[:HALF, at] += more_k[:HALF]
-    dv[:HALF, at] += more_v[:HALF]
-    dk[HALF:, at] = more_k[HALF:]
-    dv[HALF:, at] = more_v[HALF:]
     _, sg = back_of(q_aug[HALF:], kh_aug[HALF:], mask_h[HALF:, HALF:], gl, vh[HALF:])
     late = late + dot_nn(sg, kh_aug[HALF:])
     dq[:HALF, at] = (early[:, :DIM] * (0.5 * SCALE)).astype(BF16)
@@ -265,8 +266,8 @@
 
     @pl.when(pl.program_id(0) == 0)
     def _():
-        mask[...] = mask_tile(meta, meta[6] + TOK, HALF, meta[6], TOK, False)
-        mask_l[...] = mask_tile(meta, meta[6] + TOK + HALF, HALF, meta[6] + HALF, HALF, False)
+        mask[...] = mask_tile(meta, meta[6] + TOK, HALF, meta[6], TOK, False, True)
+        mask_l[...] = mask_tile(meta, meta[6] + TOK + HALF, HALF, meta[6] + HALF, HALF, False, True)
         hot[...] = one_hot(bkt[...])
         cols[...] = bucket_cols(q_bkt[...])
 
@@ -275,14 +276,14 @@
         k_aug = cat(k[:, at], hot[...])
         ge, gl = grad[:HALF, at], grad[HALF:, at]
         qe, ql = qs[:HALF, at], qs[HALF:, at]
-        attn, sg = back_of(cat(qe, added[:HALF]), k_aug, mask[...], ge, v[:, at])
-        sum_k = dk_own[:, at] + dot_tn(sg, qe)
-        sum_v = dv_own[:, at] + dot_tn(attn, ge)
-        attn, sg = back_of(cat(ql, added[HALF:]), k_aug[HALF:], mask_l[...], gl, v[HALF:, at])
+        attn, sg = back_of(k_aug, cat(qe, added[:HALF]), mask[...], v[:, at], ge)
+        sum_k = dk_own[:, at] + dot_nn(sg, qe)
+        sum_v = dv_own[:, at] + dot_nn(attn, ge)
+        attn, sg = back_of(k_aug[HALF:], cat(ql, added[HALF:]), mask_l[...], v[HALF:, at], gl)
         dk[:HALF, at] = (sum_k[:HALF] * (0.5 * SCALE)).astype(BF16)
         dv[:HALF, at] = sum_v[:HALF].astype(BF16)
-        dk[HALF:, at] = ((sum_k[HALF:] + dot_tn(sg, ql)) * (0.5 * SCALE)).astype(BF16)
-        dv[HALF:, at] = (sum_v[HALF:] + dot_tn(attn, gl)).astype(BF16)
+        dk[HALF:, at] = ((sum_k[HALF:] + dot_nn(sg, ql)) * (0.5 * SCALE)).astype(BF16)
+        dv[HALF:, at] = (sum_v[HALF:] + dot_nn(attn, gl)).astype(BF16)
 
 
 SMEM = pl.BlockSpec(memory_space=pltpu.SMEM)
@@ -336,15 +337,15 @@
     up = [(i, i + 1) for i in range(n_ctx - 1)]
     down = [(i + 1, i) for i in range(n_ctx - 1)]
 
-    k_came = lax.ppermute(k, "ctx", up)
-    v_came = lax.ppermute(v, "ctx", up)
+    bkt_rows = jnp.pad(jnp.broadcast_to(bkt.astype(BF16), (PAD, TOK)), ((0, 0), (0, WIDTH - TOK)))
+    kv_came = lax.ppermute(jnp.concatenate([k, v, bkt_rows]), "ctx", up)
     q_came = lax.ppermute(q, "ctx", down)
-    bkt_before = lax.ppermute(bkt, "ctx", up)
     bkt_after = lax.ppermute(bkt, "ctx", down)
     owner = jnp.pad(
         jnp.repeat(user_owner.reshape(-1, 3), 8, axis=1), ((0, 0), (0, 8)), constant_values=-1
     ).reshape(1, WIDTH)
 
+    came_bkt = pl.BlockSpec((PAD, TOK), lambda h: (2 * TOK // PAD, 0))
     col = pltpu.VMEM((TOK, DIM), jnp.int32)
     hot = pltpu.VMEM((TOK, DIM), BF16)
 
@@ -386,13 +387,13 @@
     meta_rows, q_came, bkt_after = lax.optimization_barrier((meta, q_came, bkt_after))
     gate_grad, gated, grad = call(
         rows_body, "rows", (HEADS // STEP,),
-        [SMEM, heads_of(TOK), heads_of(TOK), heads_of(TOK), whole(1, TOK), whole(1, TOK),
+        [SMEM, heads_of(TOK), heads_of(TOK), heads_of(TOK, 1), came_bkt, whole(1, TOK),
          whole(HEADS, DIM), heads_of(TOK), whole(TOK, WIDTH), whole(TOK, WIDTH)],
         (whole(TOK, WIDTH),) * 3,
         (shape_of(TOK, BF16),) * 3,
         [pltpu.VMEM((TOK, WIDTH), BF16), pltpu.VMEM((TOK, TOK), F32), hot, col],
         flops=2_000_000_000, moved=10 << 20,
-    )(meta_rows, q, k_came, v_came, bkt_before, bkt, tab, own_out, lifted, gate)
+    )(meta_rows, q, kv_came, kv_came, kv_came, bkt, tab, own_out, lifted, gate)
     grad_came = lax.ppermute(grad, "ctx", down)
 
     cut = pl.BlockSpec((TOK, HALF), lambda h: (0, h))
@@ -405,55 +406,53 @@
         flops=1_100_000_000, moved=6 << 20,
     )(meta, gated, total)
     other = lax.ppermute(send, "rank", [(0, 1), (1, 0)])
-    pair = (keep + other.astype(F32)).astype(BF16)
-    rows = lax.all_to_all(pair, "dp", 0, 0, tiled=True)
-    meta_own, _ = lax.optimization_barrier((meta, pair))
+    other, meta_own = lax.optimization_barrier((other, meta))
     passed = pl.BlockSpec(memory_space=pl.ANY)
 
     dq, dk_own, dv_own, bias = call(
         own_backward_body, "own_backward", (HEADS // STEP,),
-        [SMEM] + [heads_of(TOK)] * 5 + [whole(1, TOK), whole(1, TOK), whole(HEADS, DIM), heads_of(TOK)],
+        [SMEM] + [heads_of(TOK)] * 4 + [heads_of(TOK, 1), came_bkt, whole(1, TOK), whole(HEADS, DIM), heads_of(TOK)],
         (heads_of(TOK), heads_of(TOK), heads_of(TOK), whole(HEADS, DIM)),
         (shape_of(TOK, BF16), shape_of(TOK, F32), shape_of(TOK, F32), shape_of(HEADS, F32, DIM)),
         [pltpu.VMEM((TOK, TOK), F32), pltpu.VMEM((TOK, TOK), F32), hot, hot, col],
         flops=10_000_000_000, moved=12 << 20,
-    )(meta_own, q, k, v, k_came, v_came, bkt_before, bkt, tab, grad)
-
-    spread = jnp.broadcast_to(bias[None, :, None], (n_dp, n_ctx, 2, DIM)).reshape(-1, DIM)
-    rows, spread, grad_came = lax.optimization_barrier((rows, spread, grad_came))
-    bias_all = lax.all_to_all(spread, ("dp", "ctx", "rank"), 0, 0, tiled=True)
+    )(meta_own, q, k, v, kv_came, kv_came, kv_came, bkt, tab, grad)
+
+    flat = bias.reshape(1, WIDTH)
+    high = flat.astype(BF16)
+    low = (flat - high.astype(F32)).astype(BF16)
+    extra = jnp.concatenate([high, low, jnp.zeros((6, WIDTH), BF16)], axis=0)
+    pair = jnp.concatenate(
+        [(keep + other.astype(F32)).astype(BF16), jnp.broadcast_to(extra[None], (n_dp, 8, WIDTH))], axis=1
+    )
+    rows = lax.all_to_all(pair, "dp", 0, 0, tiled=True)
+
+    def sent_all(meta):
+        return call(
+            functools.partial(sent_backward_body, 0), "sent_backward", (HEADS // STEP,),
+            [SMEM, heads_of(TOK), whole(1, TOK)] + [heads_of(TOK)] * 3
+            + [whole(1, TOK), whole(HEADS, DIM), heads_of(TOK), heads_of(TOK)],
+            (heads_of(TOK), heads_of(TOK)),
+            (shape_of(TOK, BF16), shape_of(TOK, BF16)),
+            [pltpu.VMEM((TOK, HALF), F32), pltpu.VMEM((HALF, HALF), F32), hot, col],
+            flops=4_000_000_000, moved=10 << 20,
+        )(meta, q_came, bkt_after, grad_came, k, v, bkt, tab, dk_own, dv_own)
+
+    dk, dv = sent_all(meta)
+    rows, dk, dv = lax.optimization_barrier((rows, dk, dv))
     rows = jnp.sum(rows.astype(F32), axis=0)
-    def sent_half(at, meta, *done):
-        cols = functools.partial(pl.BlockSpec, index_map=lambda h: (0, h + at))
-        out = cols((TOK, STEP * DIM))
-        return call(
-            functools.partial(sent_backward_body, at * STEP), "sent_backward", (HEADS // STEP // 2,),
-            [SMEM, out, whole(1, TOK), out, out, out, whole(1, TOK), whole(HEADS, DIM), out, out]
-            + [passed] * len(done),
-            (out, out),
-            (shape_of(TOK, BF16), shape_of(TOK, BF16)),
-            [pltpu.VMEM((HALF, TOK), F32), pltpu.VMEM((HALF, HALF), F32), hot, col],
-            aliases={10: 0, 11: 1} if done else None,
-            flops=2_000_000_000, moved=5 << 20,
-        )(meta, q_came, bkt_after, grad_came, k, v, bkt, tab, dk_own, dv_own, *done)
-
-    def add_swap(rows, bit):
-        return rows + lax.ppermute(rows, "ctx", [(i, i ^ bit) for i in range(n_ctx)])
-
-    rows, meta_back = lax.optimization_barrier((rows, meta))
-    done = sent_half(0, meta_back)
-    rows = add_swap(rows, 1)
-    rows, meta_back, *done = lax.optimization_barrier((rows, meta, *done))
-    dk, dv = sent_half(HEADS // STEP // 2, meta_back, *done)
-    rows = add_swap(rows, 2)
-    rows, dk, dv = lax.optimization_barrier((rows, dk, dv))
-    rows = add_swap(rows, 4)
-    rows, bias_all = lax.optimization_barrier((rows, bias_all))
-    other_rows = lax.ppermute(rows, "rank", [(0, 1), (1, 0)])
-    weight_grad = jnp.concatenate(
-        [jnp.where(rank == 0, rows, other_rows), jnp.where(rank == 0, other_rows, rows)], axis=0
+    high = rows.astype(BF16)
+    row = rows[32:33] + rows[33:34]
+    top = row.astype(BF16)
+    rest = (row - top.astype(F32)).astype(BF16)
+    rows = jnp.concatenate([high[:32], top, rest, high[34:]], axis=0)
+    rows = lax.all_to_all(
+        jnp.broadcast_to(rows[None], (2 * n_ctx,) + rows.shape), ("ctx", "rank"), 0, 0, tiled=True
     )
-    bias_grad = jnp.sum(bias_all, axis=0, keepdims=True)
+    rows = jnp.sum(rows.reshape(n_ctx, 2, 40, WIDTH).astype(F32), axis=0)
+    weight_grad = rows[:, :32].reshape(64, WIDTH)
+    last = rows[0, 32] + rows[1, 32] + rows[0, 33] + rows[1, 33]
+    bias_grad = lax.dynamic_slice_in_dim(last.reshape(HEADS, DIM), ctx, 1)
     return (dq[None], dk[None], dv[None], gate_grad[None], weight_grad, bias_grad)
 
 

time: 160 us -> 178 us (1.11)
  waiting for transfers between devices: 16.3 us -> 63.1 us
  starting transfers between devices: 62.4 us -> 37.5 us
  Pallas kernels: 61.6 us -> 53.8 us
  other arithmetic: 6.45 us -> 9.43 us
    all_to_all x1, waiting for transfers between devices: 0.01 us -> 33.2 us  [on_device(): lax.all_to_all(jnp.broadcast_to(rows[None], (2 * n_ctx,) + rows.shape), (...]
    ppermute x7 -> x1, starting transfers between devices: 25.3 us -> 4.85 us  [on_device(): kv_came = lax.ppermute(jnp.concatenate([k, v, bkt_rows]), 'ctx', up)]
    all_to_all x1, waiting for transfers between devices: 0.01 us -> 9.21 us  [on_device(): rows = lax.all_to_all(pair, 'dp', 0, 0, tiled=True)]
    ppermute x1, waiting for transfers between devices: 0.01 us -> 6.56 us  [on_device(): bkt_after = lax.ppermute(bkt, 'ctx', down)]
    pallas_call x2 -> x1, Pallas kernels: 13.4 us -> 8.73 us  [sent_all(): call(functools.partial(sent_backward_body, 0), 'sent_backward', (HEADS //...]
    all_to_all x1, starting transfers between devices: 16.8 us -> 12.4 us  [on_device(): lax.all_to_all(jnp.broadcast_to(rows[None], (2 * n_ctx,) + rows.shape), (...]
    ppermute x7 -> x1, waiting for transfers between devices: 15.1 us -> 11 us  [on_device(): kv_came = lax.ppermute(jnp.concatenate([k, v, bkt_rows]), 'ctx', up)]
    concatenate x1 -> x4, other arithmetic: 0.72 us -> 4.48 us  [the longest x1 3.18 us: on_device(): kv_came = lax.ppermute(jnp.concatenate([k, v, bkt_rows]), 'ctx', up)]
  transfers between devices with their start and end apart: 14 -> 8, of which waited for: 4 -> 6; matrix products, arithmetic and copies ran while one was open for 7% -> 9% of each run, Pallas kernels for 28% -> 21%
where the time goes in v3:
time: 178 us; the launch traced here: 177 us
  waiting for transfers between devices  63.1 us (35%)
  Pallas kernels  53.8 us (30%)
  starting transfers between devices  37.5 us (21%)
  local copies, waits for them, and re-layouts  12.6 us (7%)
  other arithmetic  9.43 us (5%)
    all_to_all x1, waiting for transfers between devices, on_device(): lax.all_to_all(jnp.broadcast_to(rows[None], (2 * n_ctx,) + rows.shape), (...  33.2 us
    pallas_call x1, Pallas kernels, on_device(): call(own_backward_body, 'own_backward', (HEADS // STEP,), [SMEM] + [heads...  13.7 us
    all_to_all x1, starting transfers between devices, on_device(): lax.all_to_all(jnp.broadcast_to(rows[None], (2 * n_ctx,) + rows.shape), (...  12.4 us
    pallas_call x1, Pallas kernels, on_device(): call(rows_body, 'rows', (HEADS // STEP,), [SMEM, heads_of(TOK), heads_of(...  11.4 us
    ppermute x1, waiting for transfers between devices, on_device(): kv_came = lax.ppermute(jnp.concatenate([k, v, bkt_rows]), 'ctx', up)  11 us
    all_to_all x1, waiting for transfers between devices, on_device(): rows = lax.all_to_all(pair, 'dp', 0, 0, tiled=True)  9.21 us
    pallas_call x1, Pallas kernels, sent_all(): call(functools.partial(sent_backward_body, 0), 'sent_backward', (HEADS //...  8.73 us
    all_to_all x1, starting transfers between devices, on_device(): lax.all_to_all(jnp.broadcast_to(shared[None], (2 * n_dp, 32, WIDTH + DIM)...  8.59 us
  transfers between devices with their start and end apart: 8, of which 6 were waited for; matrix products, arithmetic and copies ran while one was open for 9% of the time, Pallas kernels for 21%

profile of v3, /device:TPU:1, one launch (start us, length us, event | category | flops | bytes accessed | tf_op | source)
XLA Modules:
  0.0 177.3 jit_solution(6985431040379337747)
XLA Ops:
  0.6 0.0 copy-start
  0.7 0.7 reshape.112
  1.4 0.2 copy-done
  1.6 1.6 broadcast_in_dim.42
  3.2 8.6 %all-to-all-start = ((bf16[32,32,1152]{2,1,0:T(8,128)(2,1)}), bf16[32,32,1152]{2,1,0:T(8,128)(2,1)S(1)}, u32[]{:S(2)}, u32[]{:S(2)}) async-start(bf16[32,32,1152]{2,1,0:T(8,128)(2,1)} %broadcast_in_dim.42), calls=%async_computation | async-start | bytes 4718592 | tf_op jit(solution)/shard_map/all_to_all | solution.py:367
  11.7 0.7 convert_reduce_fusion.2
  12.5 0.0 copy-start.3
  12.5 0.0 copy-start.5
  12.5 3.2 %pad_maximum_fusion = bf16[1040,1024]{1,0:T(8,128)(2,1)} fusion(bf16[16,1024]{1,0:T(8,128)(2,1)S(1)} %pad.15, bf16[512,1024]{1,0:T(8,128)(2,1)} %bitcast.38, bf16[512,1024]{1,0:T(8,128)(2,1)} %bitcast.33), kind=kLoop, calls=%fused_computation.2 | loop fusion | flops 6389760 | bytes 4259840 | tf_op jit(solution)/shard_map/concatenate | solution.py:341
  15.7 4.9 %collective-permute-start.2 = (bf16[1040,1024]{1,0:T(8,128)(2,1)}, bf16[1040,1024]{1,0:T(8,128)(2,1)}, u32[]{:S(2)}, u32[]{:S(2)}) collective-permute-start(bf16[1040,1024]{1,0:T(8,128)(2,1)} %pad_maximum_fusion), channel_id=1, source_target_pairs={{0,2},{2,4},{4,6},{6,8},{8,10},{10,12},{12,14},{1,3},{3,5},{5,7},{... | collective-permute-start | bytes 6389768 | tf_op jit(solution)/shard_map/ppermute | solution.py:341
  20.5 0.0 copy-done.3
  20.5 1.3 collective-permute-start
  21.8 1.3 collective-permute-start.1
  23.1 0.0 copy-done.5
  23.1 0.7 reduce-window.9
  23.8 0.7 reshape.114
  24.6 0.7 copy.21
  25.2 1.3 concatenate.18.meta
  26.5 1.3 convert_multiply_fusion.tab
  27.8 0.0 copy-start.4
  27.8 4.5 %own_forward_low.1.rest_0_ = f32[512,1024]{1,0:T(8,128)} custom-call(s32[9]{0:T(128)} %concatenate.18.meta, bf16[512,1024]{1,0:T(8,128)(2,1)} %bitcast.27, bf16[512,1024]{1,0:T(8,128)(2,1)} %bitcast.34, bf16[512,1024]{1,0:T(8,128)(2,1)} %bitcast.39, s32[1,512]{1,0:T(1,128)} %bkt.9, f32[8,128]{1,0:T(8,128)} %convert_multiply_fusion.tab), custom_call_target="tpu_custom_call" | custom-call | flops 2000000000 | bytes 3145728 | tf_op jit(solution)/shard_map/own_forward_low/pallas_call | solution.py:359
  32.3 0.0 copy-done.4
  32.3 0.6 broadcast_bitcast_fusion
  32.9 4.5 %own_forward_high.1.partial = f32[512,1024]{1,0:T(8,128)} custom-call(s32[9]{0:T(128)} %concatenate.18.meta, bf16[512,1024]{1,0:T(8,128)(2,1)} %bitcast.28, bf16[512,1024]{1,0:T(8,128)(2,1)} %bitcast.35, bf16[512,1024]{1,0:T(8,128)(2,1)} %bitcast.40, s32[1,512]{1,0:T(1,128)} %bkt.9, ...), custom_call_target="tpu_custom_call", output_to_operand_aliasing={{}: (6, {})} | custom-call | flops 2000000000 | bytes 3145728 | tf_op jit(solution)/shard_map/own_forward_high/pallas_call | solution.py:371
  37.4 0.8 copy.23
  38.2 0.6 pad.17.clone
  38.8 1.4 reshape.116.owner
  40.2 6.6 %collective-permute-done.1.q_bkt = s32[1,512]{1,0:T(1,128)} collective-permute-done((s32[1,512]{1,0:T(1,128)}, s32[1,512]{1,0:T(1,128)}, u32[]{:S(2)}, u32[]{:S(2)}) %collective-permute-start.1) | collective-permute-done | bytes 2080 | tf_op jit(solution)/shard_map/ppermute | solution.py:343
  46.8 0.0 collective-permute-done.qs
  46.8 0.0 all-to-all-done
  46.8 0.0 copy-start.1
  46.8 1.4 copy-done.1
  48.2 5.9 %lifted.1 = (f32[512,1024]{1,0:T(8,128)}, bf16[512,1024]{1,0:T(8,128)(2,1)}) custom-call(s32[9]{0:T(128)} %concatenate.18.meta, bf16[512,1024]{1,0:T(8,128)(2,1)} %bitcast.32, bf16[1024,1152]{1,0:T(8,128)(2,1)} %bitcast.23, s32[1,1024]{1,0:T(1,128)} %reshape.116.owner, bf16[1024,1152]{1,0:T(8,128)(2,1)} %bitcast.24), custom_call_target="tpu_custom_call" | custom-call | flops 1200000000 | bytes 6291456 | tf_op jit(solution)/shard_map/lifted/pallas_call | solution.py:378
  54.1 11.0 %collective-permute-done.2.k.v.k_bkt.kh.vh.kh_bkt = bf16[1040,1024]{1,0:T(8,128)(2,1)} collective-permute-done((bf16[1040,1024]{1,0:T(8,128)(2,1)}, bf16[1040,1024]{1,0:T(8,128)(2,1)}, u32[]{:S(2)}, u32[]{:S(2)}) %collective-permute-start.2) | collective-permute-done | bytes 2129952 | tf_op jit(solution)/shard_map/ppermute | solution.py:341
  65.0 11.4 %rows.1 = (bf16[512,1024]{1,0:T(8,128)(2,1)}, bf16[512,1024]{1,0:T(8,128)(2,1)}, bf16[512,1024]{1,0:T(8,128)(2,1)}) custom-call(s32[9]{0:T(128)} %concatenate.18.meta, bf16[512,1024]{1,0:T(8,128)(2,1)} %bitcast.29, bf16[1040,1024]{1,0:T(8,128)(2,1)} %collective-permute-done.2.k.v.k_bkt.kh.vh.kh_bkt, ...), custom_call_target="tpu_custom_call" | custom-call | flops 2000000000 | bytes 10485760 | tf_op jit(solution)/shard_map/rows/pallas_call | solution.py:388
  76.4 5.1 %weight_part.1 = (f32[16,32,1024]{2,1,0:T(8,128)}, bf16[16,32,1024]{2,1,0:T(8,128)(2,1)}) custom-call(s32[9]{0:T(128)} %concatenate.18.meta, bf16[512,1024]{1,0:T(8,128)(2,1)} %get-tuple-element.29.gated, bf16[512,1024]{1,0:T(8,128)(2,1)} %get-tuple-element.30.total), custom_call_target="tpu_custom_call" | custom-call | flops 1100000000 | bytes 6291456 | tf_op jit(solution)/shard_map/weight_part/pallas_call | solution.py:401
  81.5 1.0 collective-permute-start.3
  82.5 0.1 pad.26.clone
  82.6 0.0 copy-start.2
  82.6 1.4 collective-permute-start.4
  84.0 1.0 collective-permute-done.3
  85.0 13.7 %own_backward.1 = (bf16[512,1024]{1,0:T(8,128)(2,1)}, f32[512,1024]{1,0:T(8,128)}, f32[512,1024]{1,0:T(8,128)}, f32[8,128]{1,0:T(8,128)}) custom-call(s32[9]{0:T(128)} %concatenate.18.meta, bf16[512,1024]{1,0:T(8,128)(2,1)} %bitcast.30, bf16[512,1024]{1,0:T(8,128)(2,1)} %bitcast.36, bf16[512,1024]{1,0:T(8,128)(2,1)} %bitcast.41, ...), custom_call_target="tpu_custom_call" | custom-call | flops 10000000000 | bytes 12582912 | tf_op jit(solution)/shard_map/own_backward/pallas_call | solution.py:412
  98.7 0.8 subtract_convert_fusion.1
  99.5 0.7 convert_element_type.78
  100.2 0.0 copy-done.2
  100.2 0.3 add_convert_fusion
  100.5 0.1 maximum_maximum_fusion
  100.6 1.2 pad_maximum_fusion.1
  101.8 6.7 %all-to-all-start.1 = ((bf16[16,40,1024]{2,1,0:T(8,128)(2,1)}), bf16[16,40,1024]{2,1,0:T(8,128)(2,1)S(1)}, u32[]{:S(2)}, u32[]{:S(2)}) async-start(bf16[16,40,1024]{2,1,0:T(8,128)(2,1)} %pad_maximum_fusion.1), calls=%async_computation.1 | async-start | bytes 2621440 | tf_op jit(solution)/shard_map/all_to_all | solution.py:428
  108.5 2.2 %collective-permute-done.4.grad = bf16[512,1024]{1,0:T(8,128)(2,1)} collective-permute-done((bf16[512,1024]{1,0:T(8,128)(2,1)}, bf16[512,1024]{1,0:T(8,128)(2,1)}, u32[]{:S(2)}, u32[]{:S(2)}) %collective-permute-start.4) | collective-permute-done | bytes 1048608 | tf_op jit(solution)/shard_map/ppermute | solution.py:397
  110.7 8.7 %sent_backward.1 = (bf16[512,1024]{1,0:T(8,128)(2,1)}, bf16[512,1024]{1,0:T(8,128)(2,1)}) custom-call(s32[9]{0:T(128)} %concatenate.18.meta, bf16[512,1024]{1,0:T(8,128)(2,1)} %collective-permute-done.qs, s32[1,512]{1,0:T(1,128)} %collective-permute-done.1.q_bkt, bf16[512,1024]{1,0:T(8,128)(2,1)} %collective-permute-done.4.grad, bf16[512,1024]{1,0:T(8,128)(2,1)} %bitcast.37, ...), custom_call_target="tpu_custom_call" | custom-call | flops 4000000000 | bytes 10485760 | tf_op jit(solution)/shard_map/sent_backward/pallas_call | solution.py:431
  119.4 9.2 %all-to-all-done.1 = bf16[16,40,1024]{2,1,0:T(8,128)(2,1)S(1)} async-done(((bf16[16,40,1024]{2,1,0:T(8,128)(2,1)}), bf16[16,40,1024]{2,1,0:T(8,128)(2,1)S(1)}, u32[]{:S(2)}, u32[]{:S(2)}) %all-to-all-start.1) | async-done | bytes 1310752 | tf_op jit(solution)/shard_map/all_to_all | solution.py:428
  128.6 0.2 convert_reduce_fusion.1
  129.0 1.3 broadcast_in_dim.50
  130.2 12.4 %all-to-all-start.2 = ((bf16[16,40,1024]{2,1,0:T(8,128)(2,1)}), bf16[16,40,1024]{2,1,0:T(8,128)(2,1)S(1)}, u32[]{:S(2)}, u32[]{:S(2)}) async-start(bf16[16,40,1024]{2,1,0:T(8,128)(2,1)} %broadcast_in_dim.50), calls=%async_computation.2 | async-start | bytes 2621440 | tf_op jit(solution)/shard_map/all_to_all | solution.py:449
  142.6 33.2 %all-to-all-done.2 = bf16[16,40,1024]{2,1,0:T(8,128)(2,1)S(1)} async-done(((bf16[16,40,1024]{2,1,0:T(8,128)(2,1)}), bf16[16,40,1024]{2,1,0:T(8,128)(2,1)S(1)}, u32[]{:S(2)}, u32[]{:S(2)}) %all-to-all-start.2) | async-done | bytes 1310752 | tf_op jit(solution)/shard_map/all_to_all | solution.py:449
  175.8 0.2 convert_reduce_fusion
  176.1 0.7 slice.40
  176.8 0.5 constant_dynamic-slice_fusion
  (12 shorter events, 0.1 us)
Async XLA Ops:
  0.6 0.9 copy-start
  3.2 43.6 %all-to-all-start = ((bf16[32,32,1152]{2,1,0:T(8,128)(2,1)}), bf16[32,32,1152]{2,1,0:T(8,128)(2,1)S(1)}, u32[]{:S(2)}, u32[]{:S(2)}) async-start(bf16[32,32,1152]{2,1,0:T(8,128)(2,1)} %broadcast_in_dim.42), calls=%async_computation | async-start | bytes 4718592 | tf_op jit(solution)/shard_map/all_to_all | solution.py:367
  12.5 8.1 %copy-start.3 = (bf16[1,512,1024]{2,1,0:T(8,128)(2,1)S(1)}, bf16[1,512,1024]{2,1,0:T(8,128)(2,1)}, u32[]{:S(2)}) copy-start(bf16[1,512,1024]{2,1,0:T(8,128)(2,1)} %param.12) | copy-start | bytes 3145732
  12.5 10.7 %copy-start.5 = (s32[1,3]{1,0:T(1,128)S(1)}, s32[1,3]{1,0:T(1,128)}, u32[]{:S(2)}) copy-start(s32[1,3]{1,0:T(1,128)} %param.20) | copy-start | bytes 40
  15.7 49.3 %collective-permute-start.2 = (bf16[1040,1024]{1,0:T(8,128)(2,1)}, bf16[1040,1024]{1,0:T(8,128)(2,1)}, u32[]{:S(2)}, u32[]{:S(2)}) collective-permute-start(bf16[1040,1024]{1,0:T(8,128)(2,1)} %pad_maximum_fusion), channel_id=1, source_target_pairs={{0,2},{2,4},{4,6},{6,8},{8,10},{10,12},{12,14},{1,3},{3,5},{5,7},{... | collective-permute-start | bytes 6389768 | tf_op jit(solution)/shard_map/ppermute | solution.py:341
  20.5 26.2 %collective-permute-start = (bf16[512,1024]{1,0:T(8,128)(2,1)S(1)}, bf16[512,1024]{1,0:T(8,128)(2,1)}, u32[]{:S(2)}, u32[]{:S(2)}) collective-permute-start(bf16[512,1024]{1,0:T(8,128)(2,1)S(1)} %bitcast.31), channel_id=1, source_target_pairs={{2,0},{4,2},{6,4},{8,6},{10,8},{12,10},{14,12},{3,1},{5,3},{7,5},{... | collective-permute-start | bytes 3145736 | tf_op jit(solution)/shard_map/ppermute | solution.py:342
  21.8 25.0 %collective-permute-start.1 = (s32[1,512]{1,0:T(1,128)}, s32[1,512]{1,0:T(1,128)}, u32[]{:S(2)}, u32[]{:S(2)}) collective-permute-start(s32[1,512]{1,0:T(1,128)} %bkt.9), channel_id=1, source_target_pairs={{2,0},{4,2},{6,4},{8,6},{10,8},{12,10},{14,12},{3,1},{5,3},{7,5},{... | collective-permute-start | bytes 6152 | tf_op jit(solution)/shard_map/ppermute | solution.py:343
  27.8 4.5 %copy-start.4 = (s32[32,3]{0,1:T(4,128)S(1)}, s32[32,3]{0,1:T(4,128)}, u32[]{:S(2)}) copy-start(s32[32,3]{0,1:T(4,128)} %copy.21) | copy-start | bytes 1156
  46.8 1.4 copy-start.1
  81.5 3.5 %collective-permute-start.3 = (bf16[16,32,1024]{2,1,0:T(8,128)(2,1)}, bf16[16,32,1024]{2,1,0:T(8,128)(2,1)S(1)}, u32[]{:S(2)}, u32[]{:S(2)}) collective-permute-start(bf16[16,32,1024]{2,1,0:T(8,128)(2,1)} %get-tuple-element.31), channel_id=1, source_target_pairs={{0,1},{1,0},{2,3},{3,2},{4,5},{5,4},{6,7},{7,6},{8,9},{9,8},{10,11... | collective-permute-start | bytes 3145736 | tf_op jit(solution)/shard_map/ppermute | solution.py:408
  82.6 17.5 %copy-start.2 = (f32[16,32,1024]{2,1,0:T(8,128)S(1)}, f32[16,32,1024]{2,1,0:T(8,128)}, u32[]{:S(2)}) copy-start(f32[16,32,1024]{2,1,0:T(8,128)} %get-tuple-element.35) | copy-start | bytes 6291460
  82.6 28.1 %collective-permute-start.4 = (bf16[512,1024]{1,0:T(8,128)(2,1)}, bf16[512,1024]{1,0:T(8,128)(2,1)}, u32[]{:S(2)}, u32[]{:S(2)}) collective-permute-start(bf16[512,1024]{1,0:T(8,128)(2,1)} %get-tuple-element.33.grad), channel_id=1, source_target_pairs={{2,0},{4,2},{6,4},{8,6},{10,8},{12,10},{14,12},{3,1},{5,3},{7,5},{... | collective-permute-start | bytes 3145736 | tf_op jit(solution)/shard_map/ppermute | solution.py:397
  101.8 26.8 %all-to-all-start.1 = ((bf16[16,40,1024]{2,1,0:T(8,128)(2,1)}), bf16[16,40,1024]{2,1,0:T(8,128)(2,1)S(1)}, u32[]{:S(2)}, u32[]{:S(2)}) async-start(bf16[16,40,1024]{2,1,0:T(8,128)(2,1)} %pad_maximum_fusion.1), calls=%async_computation.1 | async-start | bytes 2621440 | tf_op jit(solution)/shard_map/all_to_all | solution.py:428
  130.2 45.6 %all-to-all-start.2 = ((bf16[16,40,1024]{2,1,0:T(8,128)(2,1)}), bf16[16,40,1024]{2,1,0:T(8,128)(2,1)S(1)}, u32[]{:S(2)}, u32[]{:S(2)}) async-start(bf16[16,40,1024]{2,1,0:T(8,128)(2,1)} %broadcast_in_dim.50), calls=%async_computation.2 | async-start | bytes 2621440 | tf_op jit(solution)/shard_map/all_to_all | solution.py:449

commit v4 on v2

--- a/solution.py
+++ b/solution.py
@@ -34,8 +34,9 @@
     return lax.dot_general(a, b, (((0,), (0,)), ((), ())), preferred_element_type=F32)
 
 
-def lowest_key(meta, first, rows):
-    pos = first + lax.broadcasted_iota(jnp.int32, (rows, 1), 0)
+def lowest_key(meta, first, rows, axis=0):
+    shape = (rows, 1) if axis == 0 else (1, rows)
+    pos = first + lax.broadcasted_iota(jnp.int32, shape, axis)
     e0, e1, e2 = meta[0], meta[1], meta[2]
     start = jnp.where(pos >= e0, e0, 0)
     band = jnp.where(pos >= e0, meta[4], meta[3])
@@ -46,9 +47,11 @@
     return pos, jnp.maximum(start, pos - band + 1)
 
 
-def mask_tile(meta, q_first, rows, k_first, cols, causal):
-    pos, low = lowest_key(meta, q_first, rows)
-    key = k_first + lax.broadcasted_iota(jnp.int32, (rows, cols), 1)
+def mask_tile(meta, q_first, rows, k_first, cols, causal, turned=False):
+    axis = 1 if turned else 0
+    pos, low = lowest_key(meta, q_first, rows, axis)
+    shape = (cols, rows) if turned else (rows, cols)
+    key = k_first + lax.broadcasted_iota(jnp.int32, shape, 1 - axis)
     ok = key >= low
     if causal:
         ok = ok & (key <= pos)
@@ -217,7 +220,7 @@
 ):
     @pl.when(pl.program_id(0) == 0)
     def _():
-        mask[...] = mask_tile(meta, meta[6], TOK, meta[6], TOK, True)
+        mask[...] = mask_tile(meta, meta[6], TOK, meta[6], TOK, True, True)
         mask_h[...] = mask_tile(meta, meta[6], TOK, meta[6] - TOK, TOK, False)
         hot[...] = one_hot(bkt[...])
         hot_h[...] = one_hot(kh_bkt[...])
@@ -237,20 +240,17 @@
     k_aug = cat(k, hot[...])
     kh_aug = cat(kh, hot_h[...])
     ge, gl = grad[:HALF], grad[HALF:]
-    attn, sg = back_of(q_aug[:HALF], k_aug[:HALF], mask[:HALF, :HALF], ge, v[:HALF])
-    early = dot_nn(sg, k_aug[:HALF])
-    dk[:HALF, at] = dot_tn(sg, q[:HALF])
-    dv[:HALF, at] = dot_tn(attn, ge)
+    attn, sg = back_of(k_aug[:HALF], q_aug, mask[:HALF, :], v[:HALF], grad)
+    dk[:HALF, at] = dot_nn(sg, q)
+    dv[:HALF, at] = dot_nn(attn, grad)
+    own = dot_tn(sg, k_aug[:HALF])
+    early, late = own[:HALF], own[HALF:]
+    attn, sg = back_of(k_aug[HALF:], q_aug[HALF:], mask[HALF:, HALF:], v[HALF:], gl)
+    dk[HALF:, at] = dot_nn(sg, q[HALF:])
+    dv[HALF:, at] = dot_nn(attn, gl)
+    late = late + dot_tn(sg, k_aug[HALF:])
     _, sg = back_of(q_aug[:HALF], kh_aug, mask_h[:HALF, :], ge, vh)
     early = early + dot_nn(sg, kh_aug)
-    attn, sg = back_of(q_aug[HALF:], k_aug, mask[HALF:, :], gl, v)
-    late = dot_nn(sg, k_aug)
-    more_k = dot_tn(sg, q[HALF:])
-    more_v = dot_tn(attn, gl)
-    dk[:HALF, at] += more_k[:HALF]
-    dv[:HALF, at] += more_v[:HALF]
-    dk[HALF:, at] = more_k[HALF:]
-    dv[HALF:, at] = more_v[HALF:]
     _, sg = back_of(q_aug[HALF:], kh_aug[HALF:], mask_h[HALF:, HALF:], gl, vh[HALF:])
     late = late + dot_nn(sg, kh_aug[HALF:])
     dq[:HALF, at] = (early[:, :DIM] * (0.5 * SCALE)).astype(BF16)
@@ -265,8 +265,8 @@
 
     @pl.when(pl.program_id(0) == 0)
     def _():
-        mask[...] = mask_tile(meta, meta[6] + TOK, HALF, meta[6], TOK, False)
-        mask_l[...] = mask_tile(meta, meta[6] + TOK + HALF, HALF, meta[6] + HALF, HALF, False)
+        mask[...] = mask_tile(meta, meta[6] + TOK, HALF, meta[6], TOK, False, True)
+        mask_l[...] = mask_tile(meta, meta[6] + TOK + HALF, HALF, meta[6] + HALF, HALF, False, True)
         hot[...] = one_hot(bkt[...])
         cols[...] = bucket_cols(q_bkt[...])
 
@@ -275,14 +275,14 @@
         k_aug = cat(k[:, at], hot[...])
         ge, gl = grad[:HALF, at], grad[HALF:, at]
         qe, ql = qs[:HALF, at], qs[HALF:, at]
-        attn, sg = back_of(cat(qe, added[:HALF]), k_aug, mask[...], ge, v[:, at])
-        sum_k = dk_own[:, at] + dot_tn(sg, qe)
-        sum_v = dv_own[:, at] + dot_tn(attn, ge)
-        attn, sg = back_of(cat(ql, added[HALF:]), k_aug[HALF:], mask_l[...], gl, v[HALF:, at])
+        attn, sg = back_of(k_aug, cat(qe, added[:HALF]), mask[...], v[:, at], ge)
+        sum_k = dk_own[:, at] + dot_nn(sg, qe)
+        sum_v = dv_own[:, at] + dot_nn(attn, ge)
+        attn, sg = back_of(k_aug[HALF:], cat(ql, added[HALF:]), mask_l[...], v[HALF:, at], gl)
         dk[:HALF, at] = (sum_k[:HALF] * (0.5 * SCALE)).astype(BF16)
         dv[:HALF, at] = sum_v[:HALF].astype(BF16)
-        dk[HALF:, at] = ((sum_k[HALF:] + dot_tn(sg, ql)) * (0.5 * SCALE)).astype(BF16)
-        dv[HALF:, at] = (sum_v[HALF:] + dot_tn(attn, gl)).astype(BF16)
+        dk[HALF:, at] = ((sum_k[HALF:] + dot_nn(sg, ql)) * (0.5 * SCALE)).astype(BF16)
+        dv[HALF:, at] = (sum_v[HALF:] + dot_nn(attn, gl)).astype(BF16)
 
 
 SMEM = pl.BlockSpec(memory_space=pltpu.SMEM)
@@ -432,7 +432,7 @@
             + [passed] * len(done),
             (out, out),
             (shape_of(TOK, BF16), shape_of(TOK, BF16)),
-            [pltpu.VMEM((HALF, TOK), F32), pltpu.VMEM((HALF, HALF), F32), hot, col],
+            [pltpu.VMEM((TOK, HALF), F32), pltpu.VMEM((HALF, HALF), F32), hot, col],
             aliases={10: 0, 11: 1} if done else None,
             flops=2_000_000_000, moved=5 << 20,
         )(meta, q_came, bkt_after, grad_came, k, v, bkt, tab, dk_own, dv_own, *done)
@@ -442,12 +442,12 @@
 
     rows, meta_back = lax.optimization_barrier((rows, meta))
     done = sent_half(0, meta_back)
-    rows = add_swap(rows, 1)
+    rows = add_swap(rows, 4)
     rows, meta_back, *done = lax.optimization_barrier((rows, meta, *done))
     dk, dv = sent_half(HEADS // STEP // 2, meta_back, *done)
     rows = add_swap(rows, 2)
     rows, dk, dv = lax.optimization_barrier((rows, dk, dv))
-    rows = add_swap(rows, 4)
+    rows = add_swap(rows, 1)
     rows, bias_all = lax.optimization_barrier((rows, bias_all))
     other_rows = lax.ppermute(rows, "rank", [(0, 1), (1, 0)])
     weight_grad = jnp.concatenate(

time: 160 us -> 155 us (0.969)
  Pallas kernels: 61.6 us -> 56.4 us
  waiting for transfers between devices: 16.3 us -> 19.5 us
  starting transfers between devices: 62.4 us -> 59.7 us
    pallas_call x1, Pallas kernels: 16.6 us -> 13.7 us  [on_device(): call(own_backward_body, 'own_backward', (HEADS // STEP,), [SMEM] + [heads...]
    pallas_call x2, Pallas kernels: 13.4 us -> 11.1 us  [sent_half(): call(functools.partial(sent_backward_body, at * STEP), 'sent_backward', (...]
    all_to_all x1, starting transfers between devices: 16.8 us -> 14.9 us  [on_device(): bias_all = lax.all_to_all(spread, ('dp', 'ctx', 'rank'), 0, 0, tiled=True)]
    ppermute x1, waiting for transfers between devices: 0.01 us -> 1.82 us  [on_device(): grad_came = lax.ppermute(grad, 'ctx', down)]
  transfers between devices with their start and end apart: 14 -> 14, of which waited for: 4 -> 6; matrix products, arithmetic and copies ran while one was open for 7% -> 8% of each run, Pallas kernels for 28% -> 26%
where the time goes in v4:
time: 155 us; the launch traced here: 154 us
  starting transfers between devices  59.7 us (39%)
  Pallas kernels  56.4 us (36%)
  waiting for transfers between devices  19.5 us (13%)
  local copies, waits for them, and re-layouts  11.4 us (7%)
  other arithmetic  6.45 us (4%)
    all_to_all x1, starting transfers between devices, on_device(): bias_all = lax.all_to_all(spread, ('dp', 'ctx', 'rank'), 0, 0, tiled=True)  14.9 us
    pallas_call x1, Pallas kernels, on_device(): call(own_backward_body, 'own_backward', (HEADS // STEP,), [SMEM] + [heads...  13.7 us
    pallas_call x1, Pallas kernels, on_device(): call(rows_body, 'rows', (HEADS // STEP,), [SMEM, heads_of(TOK), heads_of(...  11.5 us
    ppermute x1, waiting for transfers between devices, on_device(): bkt_before = lax.ppermute(bkt, 'ctx', up)  11.4 us
    pallas_call x2, Pallas kernels, sent_half(): call(functools.partial(sent_backward_body, at * STEP), 'sent_backward', (...  11.1 us
    ppermute x3, starting transfers between devices, add_swap(): lax.ppermute(rows, 'ctx', [(i, i ^ bit) for i in range(n_ctx)])  9.51 us
    all_to_all x1, starting transfers between devices, on_device(): lax.all_to_all(jnp.broadcast_to(shared[None], (2 * n_dp, 32, WIDTH + DIM)...  8.72 us
    all_to_all x1, starting transfers between devices, on_device(): rows = lax.all_to_all(pair, 'dp', 0, 0, tiled=True)  6.69 us
  transfers between devices with their start and end apart: 14, of which 6 were waited for; matrix products, arithmetic and copies ran while one was open for 8% of the time, Pallas kernels for 26%

profile of v4, /device:TPU:1, one launch (start us, length us, event | category | flops | bytes accessed | tf_op | source)
XLA Modules:
  0.0 154.2 jit_solution(1789684452494294507)
XLA Ops:
  0.6 0.0 copy-start
  0.7 0.7 reshape.63
  1.4 0.2 copy-done
  1.6 1.6 %broadcast_in_dim.30 = bf16[32,32,1152]{2,1,0:T(8,128)(2,1)} broadcast(bf16[32,1152]{1,0:T(8,128)(2,1)S(1)} %fusion.1), dimensions={1,2} | broadcast | bytes 2433024 | tf_op jit(solution)/shard_map/broadcast_in_dim | solution.py:367
  3.2 0.0 copy-start.2
  3.2 0.0 copy-start.6
  3.2 8.7 %all-to-all-start = ((bf16[32,32,1152]{2,1,0:T(8,128)(2,1)}), bf16[32,32,1152]{2,1,0:T(8,128)(2,1)S(1)}, u32[]{:S(2)}, u32[]{:S(2)}) async-start(bf16[32,32,1152]{2,1,0:T(8,128)(2,1)} %broadcast_in_dim.30), calls=%async_computation | async-start | bytes 4718592 | tf_op jit(solution)/shard_map/all_to_all | solution.py:366
  11.9 1.3 collective-permute-start
  13.2 0.0 copy-done.2
  13.2 5.1 %collective-permute-start.2 = (bf16[512,1024]{1,0:T(8,128)(2,1)S(1)}, bf16[512,1024]{1,0:T(8,128)(2,1)}, u32[]{:S(2)}, u32[]{:S(2)}) collective-permute-start(bf16[512,1024]{1,0:T(8,128)(2,1)S(1)} %bitcast.29), channel_id=1, source_target_pairs={{0,2},{2,4},{4,6},{6,8},{8,10},{10,12},{12,14},{1,3},{3,5},{5,7},{... | collective-permute-start | bytes 3145736 | tf_op jit(solution)/shard_map/ppermute | solution.py:339
  18.3 3.6 %collective-permute-start.3 = (bf16[512,1024]{1,0:T(8,128)(2,1)}, bf16[512,1024]{1,0:T(8,128)(2,1)}, u32[]{:S(2)}, u32[]{:S(2)}) collective-permute-start(bf16[512,1024]{1,0:T(8,128)(2,1)} %bitcast.30), channel_id=1, source_target_pairs={{0,2},{2,4},{4,6},{6,8},{8,10},{10,12},{12,14},{1,3},{3,5},{5,7},{... | collective-permute-start | bytes 3145736 | tf_op jit(solution)/shard_map/ppermute | solution.py:340
  21.9 3.2 %collective-permute-start.4 = (s32[1,512]{1,0:T(1,128)}, s32[1,512]{1,0:T(1,128)}, u32[]{:S(2)}, u32[]{:S(2)}) collective-permute-start(s32[1,512]{1,0:T(1,128)} %bkt.11), channel_id=1, source_target_pairs={{0,2},{2,4},{4,6},{6,8},{8,10},{10,12},{12,14},{1,3},{3,5},{5,7},{... | collective-permute-start | bytes 6152 | tf_op jit(solution)/shard_map/ppermute | solution.py:342
  25.1 1.3 collective-permute-start.1
  26.4 0.0 copy-done.6
  26.4 0.7 reduce-window.9
  27.1 0.7 reshape.65
  27.8 0.7 copy.23
  28.5 1.3 concatenate.9.meta
  29.8 1.3 convert_multiply_fusion.tab
  31.0 0.0 copy-start.4
  31.0 4.5 %own_forward_low.1.rest_0_ = f32[512,1024]{1,0:T(8,128)} custom-call(s32[9]{0:T(128)} %concatenate.9.meta, bf16[512,1024]{1,0:T(8,128)(2,1)} %bitcast.38, bf16[512,1024]{1,0:T(8,128)(2,1)} %bitcast.24, bf16[512,1024]{1,0:T(8,128)(2,1)} %bitcast.31, s32[1,512]{1,0:T(1,128)} %bkt.11, f32[8,128]{1,0:T(8,128)} %convert_multiply_fusion.tab), custom_call_target="tpu_custom_call" | custom-call | flops 2000000000 | bytes 3145728 | tf_op jit(solution)/shard_map/own_forward_low/pallas_call | solution.py:358
  35.6 0.0 copy-done.4
  35.6 0.6 broadcast_bitcast_fusion
  36.2 4.5 %own_forward_high.1.partial = f32[512,1024]{1,0:T(8,128)} custom-call(s32[9]{0:T(128)} %concatenate.9.meta, bf16[512,1024]{1,0:T(8,128)(2,1)} %bitcast.39, bf16[512,1024]{1,0:T(8,128)(2,1)} %bitcast.25, bf16[512,1024]{1,0:T(8,128)(2,1)} %bitcast.32, s32[1,512]{1,0:T(1,128)} %bkt.11, ...), custom_call_target="tpu_custom_call", output_to_operand_aliasing={{}: (6, {})} | custom-call | flops 2000000000 | bytes 3145728 | tf_op jit(solution)/shard_map/own_forward_high/pallas_call | solution.py:370
  40.7 0.8 copy.25
  41.5 0.6 pad.9.clone
  42.1 1.4 reshape.67.owner
  43.5 0.0 collective-permute-done.1.q_bkt
  43.5 0.0 collective-permute-done.qs
  43.5 0.0 all-to-all-done
  43.5 0.0 copy-start.1
  43.5 1.4 copy-done.1
  44.9 5.9 %lifted.1 = (f32[512,1024]{1,0:T(8,128)}, bf16[512,1024]{1,0:T(8,128)(2,1)}) custom-call(s32[9]{0:T(128)} %concatenate.9.meta, bf16[512,1024]{1,0:T(8,128)(2,1)} %bitcast.44, bf16[1024,1152]{1,0:T(8,128)(2,1)} %bitcast.22, s32[1,1024]{1,0:T(1,128)} %reshape.67.owner, bf16[1024,1152]{1,0:T(8,128)(2,1)} %bitcast.23), custom_call_target="tpu_custom_call" | custom-call | flops 1200000000 | bytes 6291456 | tf_op jit(solution)/shard_map/lifted/pallas_call | solution.py:377
  50.8 11.4 %collective-permute-done.4.k_bkt.kh_bkt = s32[1,512]{1,0:T(1,128)} collective-permute-done((s32[1,512]{1,0:T(1,128)}, s32[1,512]{1,0:T(1,128)}, u32[]{:S(2)}, u32[]{:S(2)}) %collective-permute-start.4) | collective-permute-done | bytes 2080 | tf_op jit(solution)/shard_map/ppermute | solution.py:342
  62.2 0.0 collective-permute-done.2.k.kh
  62.2 0.0 collective-permute-done.3.v.vh
  62.2 11.5 %rows.1 = (bf16[512,1024]{1,0:T(8,128)(2,1)}, bf16[512,1024]{1,0:T(8,128)(2,1)}, bf16[512,1024]{1,0:T(8,128)(2,1)}) custom-call(s32[9]{0:T(128)} %concatenate.9.meta, bf16[512,1024]{1,0:T(8,128)(2,1)} %bitcast.40, bf16[512,1024]{1,0:T(8,128)(2,1)} %collective-permute-done.2.k.kh, bf16[512,1024]{1,0:T(8,128)(2,1)} %collective-permute-done.3.v.vh, ...), custom_call_target="tpu_custom_call" | custom-call | flops 2000000000 | bytes 10485760 | tf_op jit(solution)/shard_map/rows/pallas_call | solution.py:387
  73.6 5.2 %weight_part.1 = (f32[16,32,1024]{2,1,0:T(8,128)}, bf16[16,32,1024]{2,1,0:T(8,128)(2,1)}) custom-call(s32[9]{0:T(128)} %concatenate.9.meta, bf16[512,1024]{1,0:T(8,128)(2,1)} %get-tuple-element.41.gated, bf16[512,1024]{1,0:T(8,128)(2,1)} %get-tuple-element.42.total), custom_call_target="tpu_custom_call" | custom-call | flops 1100000000 | bytes 6291456 | tf_op jit(solution)/shard_map/weight_part/pallas_call | solution.py:400
  78.8 1.1 collective-permute-start.5
  80.0 0.0 copy-done.5
  80.0 1.3 collective-permute-start.6
  81.2 1.2 collective-permute-done.5
  82.5 3.0 %add_convert_fusion = bf16[16,32,1024]{2,1,0:T(8,128)(2,1)} fusion(f32[16,32,1024]{2,1,0:T(8,128)} %get-tuple-element.43, bf16[16,32,1024]{2,1,0:T(8,128)(2,1)S(1)} %collective-permute-done.5), kind=kLoop, calls=%fused_computation.1 | loop fusion | flops 1572864 | bytes 4194304 | tf_op jit(solution)/shard_map/convert_element_type | solution.py:408
  85.4 6.7 %all-to-all-start.1 = ((bf16[16,32,1024]{2,1,0:T(8,128)(2,1)}), bf16[16,32,1024]{2,1,0:T(8,128)(2,1)S(1)}, u32[]{:S(2)}, u32[]{:S(2)}) async-start(bf16[16,32,1024]{2,1,0:T(8,128)(2,1)} %add_convert_fusion), calls=%async_computation.1 | async-start | bytes 2097152 | tf_op jit(solution)/shard_map/all_to_all | solution.py:409
  92.1 13.7 %own_backward.1 = (bf16[512,1024]{1,0:T(8,128)(2,1)}, f32[512,1024]{1,0:T(8,128)}, f32[512,1024]{1,0:T(8,128)}, f32[8,128]{1,0:T(8,128)}) custom-call(s32[9]{0:T(128)} %concatenate.9.meta, bf16[512,1024]{1,0:T(8,128)(2,1)} %bitcast.41, bf16[512,1024]{1,0:T(8,128)(2,1)} %bitcast.26, bf16[512,1024]{1,0:T(8,128)(2,1)} %bitcast.33, ...), custom_call_target="tpu_custom_call" | custom-call | flops 10000000000 | bytes 12582912 | tf_op jit(solution)/shard_map/own_backward/pallas_call | solution.py:413
  105.8 1.8 %collective-permute-done.6.grad = bf16[512,1024]{1,0:T(8,128)(2,1)S(1)} collective-permute-done((bf16[512,1024]{1,0:T(8,128)(2,1)S(1)}, bf16[512,1024]{1,0:T(8,128)(2,1)S(1)}, u32[]{:S(2)}, u32[]{:S(2)}) %collective-permute-start.6) | collective-permute-done | bytes 1048608 | tf_op jit(solution)/shard_map/ppermute | solution.py:396
  107.6 0.8 all-to-all-done.1
  108.4 1.4 broadcast_in_dim.33
  109.8 0.2 convert_reduce_fusion
  110.0 14.9 %all-to-all-start.2 = ((f32[256,1,128]{2,1,0:T(1,128)}), f32[256,1,128]{2,1,0:T(1,128)S(1)}, u32[]{:S(2)}, u32[]{:S(2)}) async-start(f32[256,1,128]{2,1,0:T(1,128)} %bitcast.18), calls=%async_computation.2 | async-start | bytes 262144 | tf_op jit(solution)/shard_map/all_to_all | solution.py:424
  124.9 6.3 %collective-permute-start.7 = (f32[32,1024]{1,0:T(8,128)S(1)}, f32[32,1024]{1,0:T(8,128)S(1)}, u32[]{:S(2)}, u32[]{:S(2)}) collective-permute-start(f32[32,1024]{1,0:T(8,128)S(1)} %convert_reduce_fusion), channel_id=1, source_target_pairs={{0,8},{2,10},{4,12},{6,14},{8,0},{10,2},{12,4},{14,6},{1,9},{3,11}... | collective-permute-start | bytes 393224 | tf_op jit(solution)/shard_map/ppermute | solution.py:441
  131.2 0.0 copy-done.3
  131.2 5.7 %sent_backward.2 = (bf16[512,1024]{1,0:T(8,128)(2,1)}, bf16[512,1024]{1,0:T(8,128)(2,1)}) custom-call(s32[9]{0:T(128)} %concatenate.9.meta, bf16[512,1024]{1,0:T(8,128)(2,1)} %collective-permute-done.qs, s32[1,512]{1,0:T(1,128)} %collective-permute-done.1.q_bkt, bf16[512,1024]{1,0:T(8,128)(2,1)} %copy-done.3, bf16[512,1024]{1,0:T(8,128)(2,1)} %bitcast.27, ...), custom_call_target="tpu_custom_call" | custom-call | flops 2000000000 | bytes 5242880 | tf_op jit(solution)/shard_map/sent_backward/pallas_call | solution.py:429
  136.9 0.0 collective-permute-done.7
  136.9 3.1 %collective-permute-start.8 = (f32[32,1024]{1,0:T(8,128)S(1)}, f32[32,1024]{1,0:T(8,128)S(1)}, u32[]{:S(2)}, u32[]{:S(2)}) collective-permute-start(f32[32,1024]{1,0:T(8,128)S(1)} %add.25), channel_id=1, source_target_pairs={{0,4},{2,6},{4,0},{6,2},{8,12},{10,14},{12,8},{14,10},{1,5},{3,7},... | collective-permute-start | bytes 393224 | tf_op jit(solution)/shard_map/ppermute | solution.py:441
  140.0 5.5 %sent_backward.3 = (bf16[512,1024]{1,0:T(8,128)(2,1)}, bf16[512,1024]{1,0:T(8,128)(2,1)}) custom-call(s32[9]{0:T(128)} %concatenate.9.meta, bf16[512,1024]{1,0:T(8,128)(2,1)} %collective-permute-done.qs, s32[1,512]{1,0:T(1,128)} %collective-permute-done.1.q_bkt, bf16[512,1024]{1,0:T(8,128)(2,1)} %copy-done.3, ...), custom_call_target="tpu_custom_call", output_to_operand_aliasing={{0}: (10, {}), {1}: (11, {})} | custom-call | flops 2000000000 | bytes 5242880 | tf_op jit(solution)/shard_map/sent_backward/pallas_call | solution.py:429
  145.5 0.0 collective-permute-done.8
  145.5 0.1 collective-permute-start.9
  145.7 3.8 %collective-permute-done.9 = f32[32,1024]{1,0:T(8,128)S(1)} collective-permute-done((f32[32,1024]{1,0:T(8,128)S(1)}, f32[32,1024]{1,0:T(8,128)S(1)}, u32[]{:S(2)}, u32[]{:S(2)}) %collective-permute-start.9) | collective-permute-done | bytes 131104 | tf_op jit(solution)/shard_map/ppermute | solution.py:441
  149.5 0.0 all-to-all-done.2
  149.5 3.0 %collective-permute-start.10 = (f32[32,1024]{1,0:T(8,128)S(1)}, f32[32,1024]{1,0:T(8,128)S(1)}, u32[]{:S(2)}, u32[]{:S(2)}) collective-permute-start(f32[32,1024]{1,0:T(8,128)S(1)} %add.27), channel_id=1, source_target_pairs={{0,1},{1,0},{2,3},{3,2},{4,5},{5,4},{6,7},{7,6},{8,9},{9,8},{10,11... | collective-permute-start | bytes 393224 | tf_op jit(solution)/shard_map/ppermute | solution.py:452
  152.5 0.6 reduce_sum.19
  153.0 0.4 collective-permute-done.10
  153.5 0.7 pad_maximum_fusion
  (8 shorter events, 0.1 us)
Async XLA Ops:
  0.6 0.9 copy-start
  3.2 10.0 %copy-start.2 = (bf16[1,512,1024]{2,1,0:T(8,128)(2,1)S(1)}, bf16[1,512,1024]{2,1,0:T(8,128)(2,1)}, u32[]{:S(2)}) copy-start(bf16[1,512,1024]{2,1,0:T(8,128)(2,1)} %param.13) | copy-start | bytes 3145732
  3.2 23.2 %copy-start.6 = (s32[1,3]{1,0:T(1,128)S(1)}, s32[1,3]{1,0:T(1,128)}, u32[]{:S(2)}) copy-start(s32[1,3]{1,0:T(1,128)} %param.20) | copy-start | bytes 40
  3.2 40.3 %all-to-all-start = ((bf16[32,32,1152]{2,1,0:T(8,128)(2,1)}), bf16[32,32,1152]{2,1,0:T(8,128)(2,1)S(1)}, u32[]{:S(2)}, u32[]{:S(2)}) async-start(bf16[32,32,1152]{2,1,0:T(8,128)(2,1)} %broadcast_in_dim.30), calls=%async_computation | async-start | bytes 4718592 | tf_op jit(solution)/shard_map/all_to_all | solution.py:366
  11.9 31.6 %collective-permute-start = (bf16[512,1024]{1,0:T(8,128)(2,1)}, bf16[512,1024]{1,0:T(8,128)(2,1)}, u32[]{:S(2)}, u32[]{:S(2)}) collective-permute-start(bf16[512,1024]{1,0:T(8,128)(2,1)} %bitcast.37), channel_id=1, source_target_pairs={{2,0},{4,2},{6,4},{8,6},{10,8},{12,10},{14,12},{3,1},{5,3},{7,5},{... | collective-permute-start | bytes 3145736 | tf_op jit(solution)/shard_map/ppermute | solution.py:341
  13.2 49.0 %collective-permute-start.2 = (bf16[512,1024]{1,0:T(8,128)(2,1)S(1)}, bf16[512,1024]{1,0:T(8,128)(2,1)}, u32[]{:S(2)}, u32[]{:S(2)}) collective-permute-start(bf16[512,1024]{1,0:T(8,128)(2,1)S(1)} %bitcast.29), channel_id=1, source_target_pairs={{0,2},{2,4},{4,6},{6,8},{8,10},{10,12},{12,14},{1,3},{3,5},{5,7},{... | collective-permute-start | bytes 3145736 | tf_op jit(solution)/shard_map/ppermute | solution.py:339
  18.3 43.8 %collective-permute-start.3 = (bf16[512,1024]{1,0:T(8,128)(2,1)}, bf16[512,1024]{1,0:T(8,128)(2,1)}, u32[]{:S(2)}, u32[]{:S(2)}) collective-permute-start(bf16[512,1024]{1,0:T(8,128)(2,1)} %bitcast.30), channel_id=1, source_target_pairs={{0,2},{2,4},{4,6},{6,8},{8,10},{10,12},{12,14},{1,3},{3,5},{5,7},{... | collective-permute-start | bytes 3145736 | tf_op jit(solution)/shard_map/ppermute | solution.py:340
  21.9 40.2 %collective-permute-start.4 = (s32[1,512]{1,0:T(1,128)}, s32[1,512]{1,0:T(1,128)}, u32[]{:S(2)}, u32[]{:S(2)}) collective-permute-start(s32[1,512]{1,0:T(1,128)} %bkt.11), channel_id=1, source_target_pairs={{0,2},{2,4},{4,6},{6,8},{8,10},{10,12},{12,14},{1,3},{3,5},{5,7},{... | collective-permute-start | bytes 6152 | tf_op jit(solution)/shard_map/ppermute | solution.py:342
  25.1 18.4 %collective-permute-start.1 = (s32[1,512]{1,0:T(1,128)}, s32[1,512]{1,0:T(1,128)}, u32[]{:S(2)}, u32[]{:S(2)}) collective-permute-start(s32[1,512]{1,0:T(1,128)} %bkt.11), channel_id=1, source_target_pairs={{2,0},{4,2},{6,4},{8,6},{10,8},{12,10},{14,12},{3,1},{5,3},{7,5},{... | collective-permute-start | bytes 6152 | tf_op jit(solution)/shard_map/ppermute | solution.py:343
  31.0 4.5 %copy-start.4 = (s32[32,3]{0,1:T(4,128)S(1)}, s32[32,3]{0,1:T(4,128)}, u32[]{:S(2)}) copy-start(s32[32,3]{0,1:T(4,128)} %copy.23) | copy-start | bytes 1156
  43.5 1.4 copy-start.1
  73.6 6.3 %copy-start.5 = (bf16[512,1024]{1,0:T(8,128)(2,1)S(1)}, bf16[512,1024]{1,0:T(8,128)(2,1)}, u32[]{:S(2)}) copy-start(bf16[512,1024]{1,0:T(8,128)(2,1)} %get-tuple-element.46.grad) | copy-start | bytes 3145732
  78.8 3.6 %collective-permute-start.5 = (bf16[16,32,1024]{2,1,0:T(8,128)(2,1)}, bf16[16,32,1024]{2,1,0:T(8,128)(2,1)S(1)}, u32[]{:S(2)}, u32[]{:S(2)}) collective-permute-start(bf16[16,32,1024]{2,1,0:T(8,128)(2,1)} %get-tuple-element.44), channel_id=1, source_target_pairs={{0,1},{1,0},{2,3},{3,2},{4,5},{5,4},{6,7},{7,6},{8,9},{9,8},{10,11... | collective-permute-start | bytes 3145736 | tf_op jit(solution)/shard_map/ppermute | solution.py:407
  80.0 27.6 %collective-permute-start.6 = (bf16[512,1024]{1,0:T(8,128)(2,1)S(1)}, bf16[512,1024]{1,0:T(8,128)(2,1)S(1)}, u32[]{:S(2)}, u32[]{:S(2)}) collective-permute-start(bf16[512,1024]{1,0:T(8,128)(2,1)S(1)} %copy-done.5), channel_id=1, source_target_pairs={{2,0},{4,2},{6,4},{8,6},{10,8},{12,10},{14,12},{3,1},{5,3},{7,5},{... | collective-permute-start | bytes 3145736 | tf_op jit(solution)/shard_map/ppermute | solution.py:396
  85.4 23.0 %all-to-all-start.1 = ((bf16[16,32,1024]{2,1,0:T(8,128)(2,1)}), bf16[16,32,1024]{2,1,0:T(8,128)(2,1)S(1)}, u32[]{:S(2)}, u32[]{:S(2)}) async-start(bf16[16,32,1024]{2,1,0:T(8,128)(2,1)} %add_convert_fusion), calls=%async_computation.1 | async-start | bytes 2097152 | tf_op jit(solution)/shard_map/all_to_all | solution.py:409
  107.6 23.6 %copy-start.3 = (bf16[512,1024]{1,0:T(8,128)(2,1)}, bf16[512,1024]{1,0:T(8,128)(2,1)S(1)}, u32[]{:S(2)}) copy-start(bf16[512,1024]{1,0:T(8,128)(2,1)S(1)} %collective-permute-done.6.grad) | copy-start | bytes 3145732
  110.0 39.5 %all-to-all-start.2 = ((f32[256,1,128]{2,1,0:T(1,128)}), f32[256,1,128]{2,1,0:T(1,128)S(1)}, u32[]{:S(2)}, u32[]{:S(2)}) async-start(f32[256,1,128]{2,1,0:T(1,128)} %bitcast.18), calls=%async_computation.2 | async-start | bytes 262144 | tf_op jit(solution)/shard_map/all_to_all | solution.py:424
  124.9 12.0 %collective-permute-start.7 = (f32[32,1024]{1,0:T(8,128)S(1)}, f32[32,1024]{1,0:T(8,128)S(1)}, u32[]{:S(2)}, u32[]{:S(2)}) collective-permute-start(f32[32,1024]{1,0:T(8,128)S(1)} %convert_reduce_fusion), channel_id=1, source_target_pairs={{0,8},{2,10},{4,12},{6,14},{8,0},{10,2},{12,4},{14,6},{1,9},{3,11}... | collective-permute-start | bytes 393224 | tf_op jit(solution)/shard_map/ppermute | solution.py:441
  136.9 8.6 %collective-permute-start.8 = (f32[32,1024]{1,0:T(8,128)S(1)}, f32[32,1024]{1,0:T(8,128)S(1)}, u32[]{:S(2)}, u32[]{:S(2)}) collective-permute-start(f32[32,1024]{1,0:T(8,128)S(1)} %add.25), channel_id=1, source_target_pairs={{0,4},{2,6},{4,0},{6,2},{8,12},{10,14},{12,8},{14,10},{1,5},{3,7},... | collective-permute-start | bytes 393224 | tf_op jit(solution)/shard_map/ppermute | solution.py:441
  145.5 3.9 %collective-permute-start.9 = (f32[32,1024]{1,0:T(8,128)S(1)}, f32[32,1024]{1,0:T(8,128)S(1)}, u32[]{:S(2)}, u32[]{:S(2)}) collective-permute-start(f32[32,1024]{1,0:T(8,128)S(1)} %add.26), channel_id=1, source_target_pairs={{0,2},{2,0},{4,6},{6,4},{8,10},{10,8},{12,14},{14,12},{1,3},{3,1},... | collective-permute-start | bytes 393224 | tf_op jit(solution)/shard_map/ppermute | solution.py:441
  149.5 4.0 %collective-permute-start.10 = (f32[32,1024]{1,0:T(8,128)S(1)}, f32[32,1024]{1,0:T(8,128)S(1)}, u32[]{:S(2)}, u32[]{:S(2)}) collective-permute-start(f32[32,1024]{1,0:T(8,128)S(1)} %add.27), channel_id=1, source_target_pairs={{0,1},{1,0},{2,3},{3,2},{4,5},{5,4},{6,7},{7,6},{8,9},{9,8},{10,11... | collective-permute-start | bytes 393224 | tf_op jit(solution)/shard_map/ppermute | solution.py:452

commit v5 on v4

--- a/solution.py
+++ b/solution.py
@@ -205,12 +205,12 @@
 
     @pl.when(meta[8] == 0)
     def _():
-        keep[...] = part[:, 0]
+        keep[...] = part[:, 0].astype(BF16)
         send[...] = part[:, 1].astype(BF16)
 
     @pl.when(meta[8] == 1)
     def _():
-        keep[...] = part[:, 1]
+        keep[...] = part[:, 1].astype(BF16)
         send[...] = part[:, 0].astype(BF16)
 
 
@@ -401,11 +401,11 @@
         weight_body, "weight_part", (4,),
         [SMEM, cut, whole(TOK, WIDTH)],
         (piece, piece),
-        (jax.ShapeDtypeStruct((16, 32, WIDTH), F32), jax.ShapeDtypeStruct((16, 32, WIDTH), BF16)),
+        (jax.ShapeDtypeStruct((16, 32, WIDTH), BF16),) * 2,
         flops=1_100_000_000, moved=6 << 20,
     )(meta, gated, total)
     other = lax.ppermute(send, "rank", [(0, 1), (1, 0)])
-    pair = (keep + other.astype(F32)).astype(BF16)
+    pair = (keep.astype(F32) + other.astype(F32)).astype(BF16)
     rows = lax.all_to_all(pair, "dp", 0, 0, tiled=True)
     meta_own, _ = lax.optimization_barrier((meta, pair))
     passed = pl.BlockSpec(memory_space=pl.ANY)
@@ -420,7 +420,7 @@
     )(meta_own, q, k, v, k_came, v_came, bkt_before, bkt, tab, grad)
 
     spread = jnp.broadcast_to(bias[None, :, None], (n_dp, n_ctx, 2, DIM)).reshape(-1, DIM)
-    rows, spread, grad_came = lax.optimization_barrier((rows, spread, grad_came))
+    rows, spread = lax.optimization_barrier((rows, spread))
     bias_all = lax.all_to_all(spread, ("dp", "ctx", "rank"), 0, 0, tiled=True)
     rows = jnp.sum(rows.astype(F32), axis=0)
     def sent_half(at, meta, *done):

time: 155 us -> 157 us (1.013)
    ppermute x1, waiting for transfers between devices: 1.82 us -> 0.01 us  [on_device(): grad_came = lax.ppermute(grad, 'ctx', down)]
    all_to_all x1, starting transfers between devices: 14.9 us -> 16.6 us  [on_device(): bias_all = lax.all_to_all(spread, ('dp', 'ctx', 'rank'), 0, 0, tiled=True)]
  transfers between devices with their start and end apart: 14 -> 14, of which waited for: 6 -> 6; matrix products, arithmetic and copies ran while one was open for 8% -> 7% of each run, Pallas kernels for 26% -> 26%
where the time goes in v5:
time: 157 us; the launch traced here: 156 us
  starting transfers between devices  60.3 us (38%)
  Pallas kernels  56.1 us (36%)
  waiting for transfers between devices  20 us (13%)
  local copies, waits for them, and re-layouts  12.3 us (8%)
  other arithmetic  6.18 us (4%)
    all_to_all x1, starting transfers between devices, on_device(): bias_all = lax.all_to_all(spread, ('dp', 'ctx', 'rank'), 0, 0, tiled=True)  16.6 us
    pallas_call x1, Pallas kernels, on_device(): call(own_backward_body, 'own_backward', (HEADS // STEP,), [SMEM] + [heads...  13.7 us
    pallas_call x1, Pallas kernels, on_device(): call(rows_body, 'rows', (HEADS // STEP,), [SMEM, heads_of(TOK), heads_of(...  11.5 us
    ppermute x1, waiting for transfers between devices, on_device(): bkt_before = lax.ppermute(bkt, 'ctx', up)  11.4 us
    pallas_call x2, Pallas kernels, sent_half(): call(functools.partial(sent_backward_body, at * STEP), 'sent_backward', (...  11.1 us
    all_to_all x1, starting transfers between devices, on_device(): lax.all_to_all(jnp.broadcast_to(shared[None], (2 * n_dp, 32, WIDTH + DIM)...  8.72 us
    ppermute x3, starting transfers between devices, add_swap(): lax.ppermute(rows, 'ctx', [(i, i ^ bit) for i in range(n_ctx)])  8.54 us
    all_to_all x1, starting transfers between devices, on_device(): rows = lax.all_to_all(pair, 'dp', 0, 0, tiled=True)  6.69 us
  transfers between devices with their start and end apart: 14, of which 6 were waited for; matrix products, arithmetic and copies ran while one was open for 7% of the time, Pallas kernels for 26%

profile of v5, /device:TPU:1, one launch (start us, length us, event | category | flops | bytes accessed | tf_op | source)
XLA Modules:
  0.0 155.8 jit_solution(6048545152010478324)
XLA Ops:
  0.6 0.0 copy-start
  0.7 0.7 reshape.63
  1.4 0.2 copy-done
  1.6 1.6 %broadcast_in_dim.30 = bf16[32,32,1152]{2,1,0:T(8,128)(2,1)} broadcast(bf16[32,1152]{1,0:T(8,128)(2,1)S(1)} %fusion.1), dimensions={1,2} | broadcast | bytes 2433024 | tf_op jit(solution)/shard_map/broadcast_in_dim | solution.py:367
  3.2 0.0 copy-start.2
  3.2 0.0 copy-start.6
  3.2 8.7 %all-to-all-start = ((bf16[32,32,1152]{2,1,0:T(8,128)(2,1)}), bf16[32,32,1152]{2,1,0:T(8,128)(2,1)S(1)}, u32[]{:S(2)}, u32[]{:S(2)}) async-start(bf16[32,32,1152]{2,1,0:T(8,128)(2,1)} %broadcast_in_dim.30), calls=%async_computation | async-start | bytes 4718592 | tf_op jit(solution)/shard_map/all_to_all | solution.py:366
  11.9 1.3 collective-permute-start
  13.2 0.0 copy-done.2
  13.2 5.1 %collective-permute-start.2 = (bf16[512,1024]{1,0:T(8,128)(2,1)S(1)}, bf16[512,1024]{1,0:T(8,128)(2,1)}, u32[]{:S(2)}, u32[]{:S(2)}) collective-permute-start(bf16[512,1024]{1,0:T(8,128)(2,1)S(1)} %bitcast.29), channel_id=1, source_target_pairs={{0,2},{2,4},{4,6},{6,8},{8,10},{10,12},{12,14},{1,3},{3,5},{5,7},{... | collective-permute-start | bytes 3145736 | tf_op jit(solution)/shard_map/ppermute | solution.py:339
  18.3 3.6 %collective-permute-start.3 = (bf16[512,1024]{1,0:T(8,128)(2,1)}, bf16[512,1024]{1,0:T(8,128)(2,1)}, u32[]{:S(2)}, u32[]{:S(2)}) collective-permute-start(bf16[512,1024]{1,0:T(8,128)(2,1)} %bitcast.30), channel_id=1, source_target_pairs={{0,2},{2,4},{4,6},{6,8},{8,10},{10,12},{12,14},{1,3},{3,5},{5,7},{... | collective-permute-start | bytes 3145736 | tf_op jit(solution)/shard_map/ppermute | solution.py:340
  21.9 3.2 %collective-permute-start.4 = (s32[1,512]{1,0:T(1,128)}, s32[1,512]{1,0:T(1,128)}, u32[]{:S(2)}, u32[]{:S(2)}) collective-permute-start(s32[1,512]{1,0:T(1,128)} %bkt.11), channel_id=1, source_target_pairs={{0,2},{2,4},{4,6},{6,8},{8,10},{10,12},{12,14},{1,3},{3,5},{5,7},{... | collective-permute-start | bytes 6152 | tf_op jit(solution)/shard_map/ppermute | solution.py:342
  25.1 1.3 collective-permute-start.1
  26.4 0.0 copy-done.6
  26.4 0.7 reduce-window.9
  27.1 0.7 reshape.65
  27.8 0.7 copy.23
  28.5 1.3 concatenate.9.meta
  29.8 1.3 convert_multiply_fusion.tab
  31.0 0.0 copy-start.4
  31.0 4.5 %own_forward_low.1.rest_0_ = f32[512,1024]{1,0:T(8,128)} custom-call(s32[9]{0:T(128)} %concatenate.9.meta, bf16[512,1024]{1,0:T(8,128)(2,1)} %bitcast.38, bf16[512,1024]{1,0:T(8,128)(2,1)} %bitcast.24, bf16[512,1024]{1,0:T(8,128)(2,1)} %bitcast.31, s32[1,512]{1,0:T(1,128)} %bkt.11, f32[8,128]{1,0:T(8,128)} %convert_multiply_fusion.tab), custom_call_target="tpu_custom_call" | custom-call | flops 2000000000 | bytes 3145728 | tf_op jit(solution)/shard_map/own_forward_low/pallas_call | solution.py:358
  35.6 0.0 copy-done.4
  35.6 0.6 broadcast_bitcast_fusion
  36.2 4.5 %own_forward_high.1.partial = f32[512,1024]{1,0:T(8,128)} custom-call(s32[9]{0:T(128)} %concatenate.9.meta, bf16[512,1024]{1,0:T(8,128)(2,1)} %bitcast.39, bf16[512,1024]{1,0:T(8,128)(2,1)} %bitcast.25, bf16[512,1024]{1,0:T(8,128)(2,1)} %bitcast.32, s32[1,512]{1,0:T(1,128)} %bkt.11, ...), custom_call_target="tpu_custom_call", output_to_operand_aliasing={{}: (6, {})} | custom-call | flops 2000000000 | bytes 3145728 | tf_op jit(solution)/shard_map/own_forward_high/pallas_call | solution.py:370
  40.7 0.8 copy.25
  41.5 0.6 pad.9.clone
  42.1 1.4 reshape.67.owner
  43.5 0.0 collective-permute-done.1.q_bkt
  43.5 0.0 collective-permute-done.qs
  43.5 0.0 all-to-all-done
  43.5 0.0 copy-start.1
  43.5 1.4 copy-done.1
  44.9 5.9 %lifted.1 = (f32[512,1024]{1,0:T(8,128)}, bf16[512,1024]{1,0:T(8,128)(2,1)}) custom-call(s32[9]{0:T(128)} %concatenate.9.meta, bf16[512,1024]{1,0:T(8,128)(2,1)} %bitcast.44, bf16[1024,1152]{1,0:T(8,128)(2,1)} %bitcast.22, s32[1,1024]{1,0:T(1,128)} %reshape.67.owner, bf16[1024,1152]{1,0:T(8,128)(2,1)} %bitcast.23), custom_call_target="tpu_custom_call" | custom-call | flops 1200000000 | bytes 6291456 | tf_op jit(solution)/shard_map/lifted/pallas_call | solution.py:377
  50.8 11.4 %collective-permute-done.4.k_bkt.kh_bkt = s32[1,512]{1,0:T(1,128)} collective-permute-done((s32[1,512]{1,0:T(1,128)}, s32[1,512]{1,0:T(1,128)}, u32[]{:S(2)}, u32[]{:S(2)}) %collective-permute-start.4) | collective-permute-done | bytes 2080 | tf_op jit(solution)/shard_map/ppermute | solution.py:342
  62.2 0.0 collective-permute-done.2.k.kh
  62.2 0.0 collective-permute-done.3.v.vh
  62.2 11.5 %rows.1 = (bf16[512,1024]{1,0:T(8,128)(2,1)}, bf16[512,1024]{1,0:T(8,128)(2,1)}, bf16[512,1024]{1,0:T(8,128)(2,1)}) custom-call(s32[9]{0:T(128)} %concatenate.9.meta, bf16[512,1024]{1,0:T(8,128)(2,1)} %bitcast.40, bf16[512,1024]{1,0:T(8,128)(2,1)} %collective-permute-done.2.k.kh, bf16[512,1024]{1,0:T(8,128)(2,1)} %collective-permute-done.3.v.vh, ...), custom_call_target="tpu_custom_call" | custom-call | flops 2000000000 | bytes 10485760 | tf_op jit(solution)/shard_map/rows/pallas_call | solution.py:387
  73.6 4.9 %weight_part.1 = (bf16[16,32,1024]{2,1,0:T(8,128)(2,1)}, bf16[16,32,1024]{2,1,0:T(8,128)(2,1)}) custom-call(s32[9]{0:T(128)} %concatenate.9.meta, bf16[512,1024]{1,0:T(8,128)(2,1)} %get-tuple-element.40.gated, bf16[512,1024]{1,0:T(8,128)(2,1)} %get-tuple-element.41.total), custom_call_target="tpu_custom_call" | custom-call | flops 1100000000 | bytes 6291456 | tf_op jit(solution)/shard_map/weight_part/pallas_call | solution.py:400
  78.6 1.2 collective-permute-start.5
  79.8 2.5 %collective-permute-done.5 = bf16[16,32,1024]{2,1,0:T(8,128)(2,1)S(1)} collective-permute-done((bf16[16,32,1024]{2,1,0:T(8,128)(2,1)}, bf16[16,32,1024]{2,1,0:T(8,128)(2,1)S(1)}, u32[]{:S(2)}, u32[]{:S(2)}) %collective-permute-start.5) | collective-permute-done | bytes 1048608 | tf_op jit(solution)/shard_map/ppermute | solution.py:407
  82.3 2.7 %add_convert_fusion = bf16[16,32,1024]{2,1,0:T(8,128)(2,1)} fusion(bf16[16,32,1024]{2,1,0:T(8,128)(2,1)S(1)} %collective-permute-done.5, bf16[16,32,1024]{2,1,0:T(8,128)(2,1)} %get-tuple-element.42), kind=kLoop, calls=%fused_computation.1 | loop fusion | flops 2097152 | bytes 3145728 | tf_op jit(solution)/shard_map/convert_element_type | solution.py:408
  84.9 6.7 %all-to-all-start.1 = ((bf16[16,32,1024]{2,1,0:T(8,128)(2,1)}), bf16[16,32,1024]{2,1,0:T(8,128)(2,1)S(1)}, u32[]{:S(2)}, u32[]{:S(2)}) async-start(bf16[16,32,1024]{2,1,0:T(8,128)(2,1)} %add_convert_fusion), calls=%async_computation.1 | async-start | bytes 2097152 | tf_op jit(solution)/shard_map/all_to_all | solution.py:409
  91.6 0.0 copy-done.5
  91.7 1.3 collective-permute-start.7
  93.0 13.7 %own_backward.1 = (bf16[512,1024]{1,0:T(8,128)(2,1)}, f32[512,1024]{1,0:T(8,128)}, f32[512,1024]{1,0:T(8,128)}, f32[8,128]{1,0:T(8,128)}) custom-call(s32[9]{0:T(128)} %concatenate.9.meta, bf16[512,1024]{1,0:T(8,128)(2,1)} %bitcast.41, bf16[512,1024]{1,0:T(8,128)(2,1)} %bitcast.26, bf16[512,1024]{1,0:T(8,128)(2,1)} %bitcast.33, ...), custom_call_target="tpu_custom_call" | custom-call | flops 10000000000 | bytes 12582912 | tf_op jit(solution)/shard_map/own_backward/pallas_call | solution.py:413
  106.6 1.4 all-to-all-done.1
  108.0 1.4 broadcast_in_dim.33
  109.4 0.2 convert_reduce_fusion
  109.5 16.6 %all-to-all-start.2 = ((f32[256,1,128]{2,1,0:T(1,128)}), f32[256,1,128]{2,1,0:T(1,128)S(1)}, u32[]{:S(2)}, u32[]{:S(2)}) async-start(f32[256,1,128]{2,1,0:T(1,128)} %bitcast.18), calls=%async_computation.2 | async-start | bytes 262144 | tf_op jit(solution)/shard_map/all_to_all | solution.py:424
  126.2 6.3 %collective-permute-start.6 = (f32[32,1024]{1,0:T(8,128)S(1)}, f32[32,1024]{1,0:T(8,128)S(1)}, u32[]{:S(2)}, u32[]{:S(2)}) collective-permute-start(f32[32,1024]{1,0:T(8,128)S(1)} %convert_reduce_fusion), channel_id=1, source_target_pairs={{0,8},{2,10},{4,12},{6,14},{8,0},{10,2},{12,4},{14,6},{1,9},{3,11}... | collective-permute-start | bytes 393224 | tf_op jit(solution)/shard_map/ppermute | solution.py:441
  132.5 0.0 collective-permute-done.7.grad
  132.5 1.0 copy-done.3
  133.5 5.7 %sent_backward.2 = (bf16[512,1024]{1,0:T(8,128)(2,1)}, bf16[512,1024]{1,0:T(8,128)(2,1)}) custom-call(s32[9]{0:T(128)} %concatenate.9.meta, bf16[512,1024]{1,0:T(8,128)(2,1)} %collective-permute-done.qs, s32[1,512]{1,0:T(1,128)} %collective-permute-done.1.q_bkt, bf16[512,1024]{1,0:T(8,128)(2,1)} %copy-done.3, bf16[512,1024]{1,0:T(8,128)(2,1)} %bitcast.27, ...), custom_call_target="tpu_custom_call" | custom-call | flops 2000000000 | bytes 5242880 | tf_op jit(solution)/shard_map/sent_backward/pallas_call | solution.py:429
  139.1 0.0 collective-permute-done.6
  139.1 2.1 %collective-permute-start.8 = (f32[32,1024]{1,0:T(8,128)S(1)}, f32[32,1024]{1,0:T(8,128)S(1)}, u32[]{:S(2)}, u32[]{:S(2)}) collective-permute-start(f32[32,1024]{1,0:T(8,128)S(1)} %add.25), channel_id=1, source_target_pairs={{0,4},{2,6},{4,0},{6,2},{8,12},{10,14},{12,8},{14,10},{1,5},{3,7},... | collective-permute-start | bytes 393224 | tf_op jit(solution)/shard_map/ppermute | solution.py:441
  141.3 5.5 %sent_backward.3 = (bf16[512,1024]{1,0:T(8,128)(2,1)}, bf16[512,1024]{1,0:T(8,128)(2,1)}) custom-call(s32[9]{0:T(128)} %concatenate.9.meta, bf16[512,1024]{1,0:T(8,128)(2,1)} %collective-permute-done.qs, s32[1,512]{1,0:T(1,128)} %collective-permute-done.1.q_bkt, bf16[512,1024]{1,0:T(8,128)(2,1)} %copy-done.3, ...), custom_call_target="tpu_custom_call", output_to_operand_aliasing={{0}: (10, {}), {1}: (11, {})} | custom-call | flops 2000000000 | bytes 5242880 | tf_op jit(solution)/shard_map/sent_backward/pallas_call | solution.py:429
  146.8 0.6 collective-permute-done.8
  147.4 0.1 collective-permute-start.9
  147.5 3.8 %collective-permute-done.9 = f32[32,1024]{1,0:T(8,128)S(1)} collective-permute-done((f32[32,1024]{1,0:T(8,128)S(1)}, f32[32,1024]{1,0:T(8,128)S(1)}, u32[]{:S(2)}, u32[]{:S(2)}) %collective-permute-start.9) | collective-permute-done | bytes 131104 | tf_op jit(solution)/shard_map/ppermute | solution.py:441
  151.3 0.0 all-to-all-done.2
  151.3 2.8 %collective-permute-start.10 = (f32[32,1024]{1,0:T(8,128)S(1)}, f32[32,1024]{1,0:T(8,128)S(1)}, u32[]{:S(2)}, u32[]{:S(2)}) collective-permute-start(f32[32,1024]{1,0:T(8,128)S(1)} %add.27), channel_id=1, source_target_pairs={{0,1},{1,0},{2,3},{3,2},{4,5},{5,4},{6,7},{7,6},{8,9},{9,8},{10,11... | collective-permute-start | bytes 393224 | tf_op jit(solution)/shard_map/ppermute | solution.py:452
  154.0 0.6 reduce_sum.19
  154.6 0.4 collective-permute-done.10
  155.1 0.7 pad_maximum_fusion
  (8 shorter events, 0.1 us)
Async XLA Ops:
  0.6 0.9 copy-start
  3.2 10.0 %copy-start.2 = (bf16[1,512,1024]{2,1,0:T(8,128)(2,1)S(1)}, bf16[1,512,1024]{2,1,0:T(8,128)(2,1)}, u32[]{:S(2)}) copy-start(bf16[1,512,1024]{2,1,0:T(8,128)(2,1)} %param.13) | copy-start | bytes 3145732
  3.2 23.2 %copy-start.6 = (s32[1,3]{1,0:T(1,128)S(1)}, s32[1,3]{1,0:T(1,128)}, u32[]{:S(2)}) copy-start(s32[1,3]{1,0:T(1,128)} %param.20) | copy-start | bytes 40
  3.2 40.3 %all-to-all-start = ((bf16[32,32,1152]{2,1,0:T(8,128)(2,1)}), bf16[32,32,1152]{2,1,0:T(8,128)(2,1)S(1)}, u32[]{:S(2)}, u32[]{:S(2)}) async-start(bf16[32,32,1152]{2,1,0:T(8,128)(2,1)} %broadcast_in_dim.30), calls=%async_computation | async-start | bytes 4718592 | tf_op jit(solution)/shard_map/all_to_all | solution.py:366
  11.9 31.6 %collective-permute-start = (bf16[512,1024]{1,0:T(8,128)(2,1)}, bf16[512,1024]{1,0:T(8,128)(2,1)}, u32[]{:S(2)}, u32[]{:S(2)}) collective-permute-start(bf16[512,1024]{1,0:T(8,128)(2,1)} %bitcast.37), channel_id=1, source_target_pairs={{2,0},{4,2},{6,4},{8,6},{10,8},{12,10},{14,12},{3,1},{5,3},{7,5},{... | collective-permute-start | bytes 3145736 | tf_op jit(solution)/shard_map/ppermute | solution.py:341
  13.2 49.0 %collective-permute-start.2 = (bf16[512,1024]{1,0:T(8,128)(2,1)S(1)}, bf16[512,1024]{1,0:T(8,128)(2,1)}, u32[]{:S(2)}, u32[]{:S(2)}) collective-permute-start(bf16[512,1024]{1,0:T(8,128)(2,1)S(1)} %bitcast.29), channel_id=1, source_target_pairs={{0,2},{2,4},{4,6},{6,8},{8,10},{10,12},{12,14},{1,3},{3,5},{5,7},{... | collective-permute-start | bytes 3145736 | tf_op jit(solution)/shard_map/ppermute | solution.py:339
  18.3 43.8 %collective-permute-start.3 = (bf16[512,1024]{1,0:T(8,128)(2,1)}, bf16[512,1024]{1,0:T(8,128)(2,1)}, u32[]{:S(2)}, u32[]{:S(2)}) collective-permute-start(bf16[512,1024]{1,0:T(8,128)(2,1)} %bitcast.30), channel_id=1, source_target_pairs={{0,2},{2,4},{4,6},{6,8},{8,10},{10,12},{12,14},{1,3},{3,5},{5,7},{... | collective-permute-start | bytes 3145736 | tf_op jit(solution)/shard_map/ppermute | solution.py:340
  21.9 40.2 %collective-permute-start.4 = (s32[1,512]{1,0:T(1,128)}, s32[1,512]{1,0:T(1,128)}, u32[]{:S(2)}, u32[]{:S(2)}) collective-permute-start(s32[1,512]{1,0:T(1,128)} %bkt.11), channel_id=1, source_target_pairs={{0,2},{2,4},{4,6},{6,8},{8,10},{10,12},{12,14},{1,3},{3,5},{5,7},{... | collective-permute-start | bytes 6152 | tf_op jit(solution)/shard_map/ppermute | solution.py:342
  25.1 18.4 %collective-permute-start.1 = (s32[1,512]{1,0:T(1,128)}, s32[1,512]{1,0:T(1,128)}, u32[]{:S(2)}, u32[]{:S(2)}) collective-permute-start(s32[1,512]{1,0:T(1,128)} %bkt.11), channel_id=1, source_target_pairs={{2,0},{4,2},{6,4},{8,6},{10,8},{12,10},{14,12},{3,1},{5,3},{7,5},{... | collective-permute-start | bytes 6152 | tf_op jit(solution)/shard_map/ppermute | solution.py:343
  31.0 4.5 %copy-start.4 = (s32[32,3]{0,1:T(4,128)S(1)}, s32[32,3]{0,1:T(4,128)}, u32[]{:S(2)}) copy-start(s32[32,3]{0,1:T(4,128)} %copy.23) | copy-start | bytes 1156
  43.5 1.4 copy-start.1
  78.6 3.7 %collective-permute-start.5 = (bf16[16,32,1024]{2,1,0:T(8,128)(2,1)}, bf16[16,32,1024]{2,1,0:T(8,128)(2,1)S(1)}, u32[]{:S(2)}, u32[]{:S(2)}) collective-permute-start(bf16[16,32,1024]{2,1,0:T(8,128)(2,1)} %get-tuple-element.43), channel_id=1, source_target_pairs={{0,1},{1,0},{2,3},{3,2},{4,5},{5,4},{6,7},{7,6},{8,9},{9,8},{10,11... | collective-permute-start | bytes 3145736 | tf_op jit(solution)/shard_map/ppermute | solution.py:407
  82.3 9.4 %copy-start.5 = (bf16[512,1024]{1,0:T(8,128)(2,1)S(1)}, bf16[512,1024]{1,0:T(8,128)(2,1)}, u32[]{:S(2)}) copy-start(bf16[512,1024]{1,0:T(8,128)(2,1)} %get-tuple-element.45.grad) | copy-start | bytes 3145732
  84.9 23.0 %all-to-all-start.1 = ((bf16[16,32,1024]{2,1,0:T(8,128)(2,1)}), bf16[16,32,1024]{2,1,0:T(8,128)(2,1)S(1)}, u32[]{:S(2)}, u32[]{:S(2)}) async-start(bf16[16,32,1024]{2,1,0:T(8,128)(2,1)} %add_convert_fusion), calls=%async_computation.1 | async-start | bytes 2097152 | tf_op jit(solution)/shard_map/all_to_all | solution.py:409
  91.7 40.8 %collective-permute-start.7 = (bf16[512,1024]{1,0:T(8,128)(2,1)S(1)}, bf16[512,1024]{1,0:T(8,128)(2,1)S(1)}, u32[]{:S(2)}, u32[]{:S(2)}) collective-permute-start(bf16[512,1024]{1,0:T(8,128)(2,1)S(1)} %copy-done.5), channel_id=1, source_target_pairs={{2,0},{4,2},{6,4},{8,6},{10,8},{12,10},{14,12},{3,1},{5,3},{7,5},{... | collective-permute-start | bytes 3145736 | tf_op jit(solution)/shard_map/ppermute | solution.py:396
  109.5 41.7 %all-to-all-start.2 = ((f32[256,1,128]{2,1,0:T(1,128)}), f32[256,1,128]{2,1,0:T(1,128)S(1)}, u32[]{:S(2)}, u32[]{:S(2)}) async-start(f32[256,1,128]{2,1,0:T(1,128)} %bitcast.18), calls=%async_computation.2 | async-start | bytes 262144 | tf_op jit(solution)/shard_map/all_to_all | solution.py:424
  126.2 12.9 %collective-permute-start.6 = (f32[32,1024]{1,0:T(8,128)S(1)}, f32[32,1024]{1,0:T(8,128)S(1)}, u32[]{:S(2)}, u32[]{:S(2)}) collective-permute-start(f32[32,1024]{1,0:T(8,128)S(1)} %convert_reduce_fusion), channel_id=1, source_target_pairs={{0,8},{2,10},{4,12},{6,14},{8,0},{10,2},{12,4},{14,6},{1,9},{3,11}... | collective-permute-start | bytes 393224 | tf_op jit(solution)/shard_map/ppermute | solution.py:441
  132.5 1.0 copy-start.3
  139.1 8.2 %collective-permute-start.8 = (f32[32,1024]{1,0:T(8,128)S(1)}, f32[32,1024]{1,0:T(8,128)S(1)}, u32[]{:S(2)}, u32[]{:S(2)}) collective-permute-start(f32[32,1024]{1,0:T(8,128)S(1)} %add.25), channel_id=1, source_target_pairs={{0,4},{2,6},{4,0},{6,2},{8,12},{10,14},{12,8},{14,10},{1,5},{3,7},... | collective-permute-start | bytes 393224 | tf_op jit(solution)/shard_map/ppermute | solution.py:441
  147.4 3.9 %collective-permute-start.9 = (f32[32,1024]{1,0:T(8,128)S(1)}, f32[32,1024]{1,0:T(8,128)S(1)}, u32[]{:S(2)}, u32[]{:S(2)}) collective-permute-start(f32[32,1024]{1,0:T(8,128)S(1)} %add.26), channel_id=1, source_target_pairs={{0,2},{2,0},{4,6},{6,4},{8,10},{10,8},{12,14},{14,12},{1,3},{3,1},... | collective-permute-start | bytes 393224 | tf_op jit(solution)/shard_map/ppermute | solution.py:441
  151.3 3.7 %collective-permute-start.10 = (f32[32,1024]{1,0:T(8,128)S(1)}, f32[32,1024]{1,0:T(8,128)S(1)}, u32[]{:S(2)}, u32[]{:S(2)}) collective-permute-start(f32[32,1024]{1,0:T(8,128)S(1)} %add.27), channel_id=1, source_target_pairs={{0,1},{1,0},{2,3},{3,2},{4,5},{5,4},{6,7},{7,6},{8,9},{9,8},{10,11... | collective-permute-start | bytes 393224 | tf_op jit(solution)/shard_map/ppermute | solution.py:452
